TPU v7x, 32 devices: a whole 2x2x4 slice. The times are simulated.
32 devices in a mesh: groups: 2 (over y), gx: 4 (over z), gy: 4 (over x, core).
Axes of the slice: x: 2, y: 2, z: 4, core: 2. Of those that a mesh axis runs over, the one named last changes fastest.
Arguments:
- activations: bfloat16 [128, 18432], P(('groups', 'gy'), 'gx'), parts along dimension 0, may hold values from -6 to 6
- ln_gain: bfloat16 [18432], P('gx'), may hold values from 0.099609375 to 1.8984375
- w_query: bfloat16 [18432, 12288], P('gx', 'gy'), may hold values from -0.046875 to 0.046875
- w_keyval: bfloat16 [18432, 512], P('gx'), may hold values from -0.046875 to 0.046875
- w_out: bfloat16 [12288, 18432], P('gy', 'gx'), may hold values from -0.0546875 to 0.0546875
- k_cache: bfloat16 [128, 1024, 256], P(('groups', 'gx', 'gy')), parts along dimension 0, may hold values from -4000 to 4000
- v_cache: bfloat16 [128, 1024, 256], P(('groups', 'gx', 'gy')), parts along dimension 0, may hold values from -24 to 24
- cache_lengths: int32 [128], P(('groups', 'gx', 'gy')), parts along dimension 0, may hold values from 1 to 1024, as said below
Outputs:
- attn_out: bfloat16 [128, 18432], P(('groups', 'gy'), 'gx'), parts along dimension 0
There are 2 independent parts, one for each index of `groups`. A program takes and returns all parts, laid end to end along the dimension named above; an argument that names none is the same for every part. Nothing has to cross between parts.
Inputs may be any that keep to these rules, and one draw needn't show every extreme that they name: `cache_lengths`: some sequence uses all 1024 positions.
All inputs are finite; a program needn't handle non-finite values.
Results may differ from a plain program's by a relative error of at most 0.012.
The roundings to bfloat16 on the way count: a program that leaves them out, or rounds other values in their place, can miss the bound.
Values may be sent and summed in bfloat16 or wider, within the bound.
No kernel may reach another device: no remote copies, remote signals or barrier semaphores. Data moves between devices by JAX's collectives and lax.ppermute only.
A program may use at most 192 MiB of HBM per device.

v0:
```python
import jax
import jax.numpy as jnp
from jax import lax
from jax.sharding import PartitionSpec as P

D = 18432


def attend_local(queries, k_cache, v_cache, cache_lengths, keyval):
    seq_count = queries.shape[0]
    head_dim = k_cache.shape[2]
    query_heads = queries.reshape(seq_count, -1, head_dim)
    new_key = keyval[:, :head_dim]
    new_value = keyval[:, head_dim:]
    scores = (
        jnp.einsum("shd,std->sht", query_heads, k_cache, preferred_element_type=jnp.float32)
        * 0.0625
    )
    new_score = (
        jnp.einsum("shd,sd->sh", query_heads, new_key, preferred_element_type=jnp.float32) * 0.0625
    )
    positions = lax.broadcasted_iota(jnp.int32, (1, 1, k_cache.shape[1]), 2)
    live = positions < cache_lengths[:, None, None]
    masked = jnp.where(live, scores, jnp.float32(-1e30))
    top = jnp.maximum(jnp.max(masked, axis=2), new_score)
    expo = jnp.where(live, jnp.exp(masked - top[:, :, None]), jnp.float32(0.0))
    new_expo = jnp.exp(new_score - top)
    denom = jnp.sum(expo, axis=2) + new_expo
    weights = (expo / denom[:, :, None]).astype(jnp.bfloat16)
    new_weight = (new_expo / denom).astype(jnp.bfloat16)
    mixed = jnp.einsum("sht,std->shd", weights, v_cache, preferred_element_type=jnp.float32)
    mixed = (
        mixed
        + new_weight.astype(jnp.float32)[:, :, None] * new_value.astype(jnp.float32)[:, None, :]
    )
    return mixed.astype(jnp.bfloat16).reshape(seq_count, -1)


def shards(activations, ln_gain, w_query, w_keyval, w_out, k_cache, v_cache, cache_lengths):
    as_float = activations.astype(jnp.float32)
    moments = lax.psum((jnp.sum(as_float, axis=1), jnp.sum(as_float * as_float, axis=1)), "gx")
    row_mean = moments[0] / D
    row_var = moments[1] / D - row_mean * row_mean
    normed = (
        (as_float - row_mean[:, None])
        * lax.rsqrt(row_var + 1e-06)[:, None]
        * ln_gain.astype(jnp.float32)
    ).astype(jnp.bfloat16)
    gathered = lax.all_gather(normed, "gy", axis=0, tiled=True)
    seq_count = k_cache.shape[0]
    head_cols = w_query.shape[1]
    summed = lax.psum_scatter(
        jnp.concatenate(
            [
                jnp.dot(gathered, w_query, preferred_element_type=jnp.float32),
                jnp.dot(gathered, w_keyval, preferred_element_type=jnp.float32),
            ],
            axis=1,
        ),
        "gx",
        scatter_dimension=0,
        tiled=True,
    )
    query_part = summed[:, :head_cols].astype(jnp.bfloat16)
    own_keyval = lax.dynamic_slice_in_dim(
        summed[:, head_cols:], lax.axis_index("gy") * seq_count, seq_count, 0
    )
    keyval = own_keyval.astype(jnp.bfloat16)
    queries = lax.all_to_all(query_part, "gy", split_axis=0, concat_axis=1, tiled=True)
    attended = attend_local(queries, k_cache, v_cache, cache_lengths, keyval)
    returned = lax.all_to_all(attended, "gy", split_axis=1, concat_axis=0, tiled=True)
    partial_terms = jnp.dot(
        lax.all_gather(returned, "gx", axis=0, tiled=True),
        w_out,
        preferred_element_type=jnp.float32,
    )
    return lax.psum_scatter(partial_terms, "gy", scatter_dimension=0, tiled=True).astype(
        jnp.bfloat16
    )


def solution(mesh):
    placed = (
        P(("groups", "gy"), "gx"),
        P("gx"),
        P("gx", "gy"),
        P("gx", None),
        P("gy", "gx"),
        P(("groups", "gx", "gy"), None, None),
        P(("groups", "gx", "gy"), None, None),
        P(("groups", "gx", "gy")),
    )
    return jax.shard_map(
        shards, mesh=mesh, in_specs=placed, out_specs=P(("groups", "gy"), "gx"), check_vma=False
    )
```

profile of v0, /device:TPU:0, one launch (start us, length us, event | category | flops | bytes accessed | tf_op | source)
XLA Modules:
  0.0 146.1 jit_solution(10651401032729517748)
XLA Ops:
  6.5 1.2 convert_reduce_fusion
  7.7 0.7 convert_element_type.32
  8.5 13.4 %all-reduce = (f32[16]{0:T(128)S(1)}, f32[16]{0:T(128)S(1)}) all-reduce(f32[16]{0:T(128)S(1)} %get-tuple-element.6, f32[16]{0:T(128)S(1)} %get-tuple-element.5), channel_id=1, replica_groups=mesh['groups'=2,'gx'=4,'gy'=4] {'gx'}, use_global_device_ids=true, to_apply=%region_3.0 | all-reduce | flops 32 | bytes 256 | tf_op jit(solution)/shard_map/psum | solution.py:41
  21.9 1.0 fusion.9
  22.9 7.7 %all_gather.6 = bf16[64,4608]{1,0:T(8,128)(2,1)S(1)} all-gather(bf16[16,4608]{1,0:T(8,128)(2,1)S(1)} %fusion.9), channel_id=1, replica_groups=mesh['groups'=2,'gx'=4,'gy'=4] {'gy'}, dimensions={0}, use_global_device_ids=true | all-gather | bytes 737280 | tf_op jit(solution)/shard_map/all_gather | solution.py:49
  30.6 11.7 %fusion.17 = f32[64,3072]{1,0:T(8,128)S(1)} fusion(bf16[64,4608]{1,0:T(8,128)(2,1)S(1)} %all_gather.6, bf16[4608,3072]{1,0:T(8,128)(2,1)} %param.10), kind=kOutput, calls=%fused_computation.35 | convolution fusion | flops 1811939328 | bytes 29687808 | tf_op jit(solution)/shard_map/dot_general | solution.py:55
  42.3 0.9 fusion.18
  43.2 1.0 pad_maximum_fusion
  44.3 0.1 iota_compare_fusion
  44.4 22.6 %reduce-scatter.3.cloned.1.call-done = f32[16,3584]{1,0:T(8,128)} async-done(((f32[64,3584]{1,0:T(8,128)}), f32[16,3584]{1,0:T(8,128)}) %reduce-scatter.3.cloned.1.call-update) | async-done | bytes 229392 | tf_op jit(solution)/shard_map/reduce_scatter | solution.py:52
  66.9 0.9 slice.24
  67.9 0.7 all_to_all.26
  68.5 3.3 %all-to-all-start = ((bf16[4,4,3072]{2,1,0:T(4,128)(2,1)}), bf16[4,4,3072]{2,1,0:T(4,128)(2,1)S(1)}, u32[]{:S(2)}, u32[]{:S(2)}) async-start(bf16[4,4,3072]{2,1,0:T(4,128)(2,1)} %all_to_all.26), calls=%async_computation.1 | async-start | bytes 196608 | tf_op jit(solution)/shard_map/all_to_all | solution.py:69
  71.9 0.8 slice.18
  72.7 3.4 %all-to-all-done = bf16[4,4,3072]{2,1,0:T(4,128)(2,1)S(1)} async-done(((bf16[4,4,3072]{2,1,0:T(4,128)(2,1)}), bf16[4,4,3072]{2,1,0:T(4,128)(2,1)S(1)}, u32[]{:S(2)}, u32[]{:S(2)}) %all-to-all-start) | async-done | bytes 98336 | tf_op jit(solution)/shard_map/all_to_all | solution.py:69
  76.2 0.1 fusion.11
  76.4 0.8 fusion.16
  77.2 0.3 fusion.2
  77.5 2.1 %fusion.1 = bf16[4,48,256]{2,1,0:T(8,128)(2,1)S(1)} fusion(bf16[4,1024,256]{2,1,0:T(8,128)(2,1)} %param.14, f32[4,48,1024]{2,1,0:T(8,128)S(1)} %get-tuple-element.16, f32[4,48]{1,0:T(4,128)S(1)} %get-tuple-element.10, f32[4,48]{1,0:T(4,128)S(1)} %multiply_maximum_fusion, pred[4,1024]{1,0:T(4,128)(4,1)S(1)} %iota_compare_fusion, ...), kind=kOutput, calls=%fused_computation.3 | convolution fusion | flops 101597184 | bytes 2992384 | tf_op jit(solution)/shard_map/sht,std->shd/dot_general | solution.py:31
  79.8 6.7 %all_to_all.35 = bf16[4,4,3072]{2,0,1:T(4,128)(2,1)S(1)} all-to-all(bf16[4,4,3072]{2,0,1:T(4,128)(2,1)S(1)} %copy.11), channel_id=1, replica_groups=mesh['groups'=2,'gx'=4,'gy'=4] {'gy'}, dimensions={1} | all-to-all | bytes 196608 | tf_op jit(solution)/shard_map/all_to_all | solution.py:71
  86.5 15.0 %all_gather.7 = bf16[64,3072]{1,0:T(8,128)(2,1)S(1)} all-gather(bf16[16,3072]{1,0:T(8,128)(2,1)S(1)} %all_to_all.32), channel_id=1, replica_groups=mesh['groups'=2,'gx'=4,'gy'=4] {'gx'}, dimensions={0}, use_global_device_ids=true | all-gather | bytes 491520 | tf_op jit(solution)/shard_map/all_gather | solution.py:73
  101.5 12.8 %fusion.19 = f32[64,4608]{1,0:T(8,128)} fusion(bf16[64,3072]{1,0:T(8,128)(2,1)S(1)} %all_gather.7, bf16[3072,4608]{1,0:T(8,128)(2,1)} %param.12), kind=kOutput, calls=%fused_computation.37 | convolution fusion | flops 1811939328 | bytes 29884416 | tf_op jit(solution)/shard_map/dot_general | solution.py:72
  114.3 23.3 %reduce-scatter.5.cloned.1.call-done = f32[16,4608]{1,0:T(8,128)} async-done(((f32[64,4608]{1,0:T(8,128)}), f32[16,4608]{1,0:T(8,128)}) %reduce-scatter.5.cloned.1.call-update) | async-done | bytes 294928 | tf_op jit(solution)/shard_map/reduce_scatter | solution.py:77
  137.6 1.6 %convert_element_type.40 = bf16[16,4608]{1,0:T(8,128)(2,1)} convert(f32[16,4608]{1,0:T(8,128)} %reduce-scatter.5.cloned.1.call-done) | non-fusion elementwise | flops 73728 | bytes 442368 | tf_op jit(solution)/shard_map/convert_element_type | solution.py:77
  (25 shorter events, 0.4 us)
Async XLA Ops:
  6.5 69.8 %copy-start = (bf16[4,1024,256]{2,1,0:T(8,128)(2,1)S(1)}, bf16[4,1024,256]{2,1,0:T(8,128)(2,1)}, u32[]{:S(2)}) copy-start(bf16[4,1024,256]{2,1,0:T(8,128)(2,1)} %param.13) | copy-start | bytes 6291460
  6.5 60.4 %reduce-scatter.3.cloned.1.call-start = ((), (), s32[]{:S(2)}) async-start(), calls=%async_computation.4 | async-start | bytes 1146880 | tf_op jit(solution)/shard_map/reduce_scatter | solution.py:52
  22.9 19.4 %slice-start = ((s8[4718592]{0:T(1024)(128)(4,1)}), s8[4194304]{0:T(1024)(128)(4,1)S(1)}, s32[]{:S(2)}) async-start(s8[4718592]{0:T(1024)(128)(4,1)} %bitcast.16), calls=%async_computation.6 | async-start | bytes 8388608
  30.6 11.7 %slice-start.1 = ((s8[4718592]{0:T(1024)(128)(4,1)}), s8[524288]{0:T(1024)(128)(4,1)S(1)}, s32[]{:S(2)}) async-start(s8[4718592]{0:T(1024)(128)(4,1)} %bitcast.16), calls=%async_computation.7 | async-start | bytes 1048576
  42.3 2.0 %copy-start.2 = (s32[4]{0:T(128)S(1)}, s32[4]{0:T(128)}, u32[]{:S(2)}) copy-start(s32[4]{0:T(128)} %param.15) | copy-start | bytes 52
  68.5 7.6 %all-to-all-start = ((bf16[4,4,3072]{2,1,0:T(4,128)(2,1)}), bf16[4,4,3072]{2,1,0:T(4,128)(2,1)S(1)}, u32[]{:S(2)}, u32[]{:S(2)}) async-start(bf16[4,4,3072]{2,1,0:T(4,128)(2,1)} %all_to_all.26), calls=%async_computation.1 | async-start | bytes 196608 | tf_op jit(solution)/shard_map/all_to_all | solution.py:69
  71.9 65.8 %reduce-scatter.5.cloned.1.call-start = ((), (), s32[]{:S(2)}) async-start(), calls=%async_computation.5 | async-start | bytes 1474560 | tf_op jit(solution)/shard_map/reduce_scatter | solution.py:77
  101.5 37.7 %copy-start.1 = (bf16[4,1024,256]{2,1,0:T(8,128)(2,1)S(1)}, bf16[4,1024,256]{2,1,0:T(8,128)(2,1)}, u32[]{:S(2)}) copy-start(bf16[4,1024,256]{2,1,0:T(8,128)(2,1)} %param.13) | copy-start | bytes 6291460
Sparse Core Ops, SparseCore 0:
  44.4 22.4 reduce-scatter.2
  114.4 23.1 reduce-scatter.4
where the time goes:
time: 147 us; the launch traced here: 146 us
  waiting for transfers between devices  49.3 us (34%)
  blocking collectives  42.8 us (29%)
  matrix products  28.4 us (19%)
  between operations  13.5 us (9%)
  other arithmetic  5.99 us (4%)
  starting transfers between devices  3.35 us (2%)
  local copies, waits for them, and re-layouts  2.66 us (2%)
    reduce_scatter x1, waiting for transfers between devices, shards(): lax.psum_scatter(partial_terms, 'gy', scatter_dimension=0, tiled=True)  23.3 us
    reduce_scatter x1, waiting for transfers between devices, shards(): lax.psum_scatter(jnp.concatenate([jnp.dot(gathered, w_query, preferred_el...  22.6 us
    all_gather x1, blocking collectives, shards(): lax.all_gather(returned, 'gx', axis=0, tiled=True)  15 us
    psum x1, blocking collectives, shards(): lax.psum((jnp.sum(as_float, axis=1), jnp.sum(as_float * as_float, axis=1)...  13.4 us
    dot_general x1, matrix products, shards(): jnp.dot(lax.all_gather(returned, 'gx', axis=0, tiled=True), w_out, prefer...  12.8 us
    dot_general x1, matrix products, shards(): jnp.dot(gathered, w_query, preferred_element_type=jnp.float32)  11.7 us
    all_gather x1, blocking collectives, shards(): gathered = lax.all_gather(normed, 'gy', axis=0, tiled=True)  7.66 us
    all_to_all x1, blocking collectives, shards(): lax.all_to_all(attended, 'gy', split_axis=1, concat_axis=0, tiled=True)  6.67 us
  transfers between devices with their start and end apart: 3, of which 3 were waited for; matrix products, arithmetic and copies ran while one was open for 1% of the time, Pallas kernels for 0%

commit v1 on v0

v1 whole, which is shorter than its diff:
```python
import jax
import jax.numpy as jnp
from jax import lax
from jax.sharding import PartitionSpec as P

D = 18432
WIRE_SCALE = 16.0


def swap(x, axis, n, m):
    return lax.ppermute(x, axis, [(k, k ^ m) for k in range(n)])


def rows_of(x, block, n):
    size = x.shape[0] // n
    return lax.dynamic_slice_in_dim(x, block * size, size, 0)


def reduce_rows(partial, axis, n, encode, decode):
    me = lax.axis_index(axis)
    got = [swap(encode(rows_of(partial, me ^ m, n)), axis, n, m) for m in range(1, n)]
    total = rows_of(partial, me, n)
    for part in got:
        total = total + decode(part)
    return total


def gather_rows(x, axis, n):
    me = lax.axis_index(axis)
    got = [x] + [swap(x, axis, n, m) for m in range(1, n)]
    out = jnp.zeros((n * x.shape[0],) + x.shape[1:], x.dtype)
    for m in range(n):
        out = lax.dynamic_update_slice_in_dim(out, got[m], (me ^ m) * x.shape[0], 0)
    return out


def attend_local(query_heads, new_key, new_value, k_cache, v_cache, cache_lengths):
    scores = (
        jnp.einsum("shd,std->sht", query_heads, k_cache, preferred_element_type=jnp.float32)
        * 0.0625
    )
    new_score = (
        jnp.einsum("shd,sd->sh", query_heads, new_key, preferred_element_type=jnp.float32) * 0.0625
    )
    positions = lax.broadcasted_iota(jnp.int32, (1, 1, k_cache.shape[1]), 2)
    live = positions < cache_lengths[:, None, None]
    masked = jnp.where(live, scores, jnp.float32(-1e30))
    top = jnp.maximum(jnp.max(masked, axis=2), new_score)
    expo = jnp.where(live, jnp.exp(masked - top[:, :, None]), jnp.float32(0.0))
    new_expo = jnp.exp(new_score - top)
    denom = jnp.sum(expo, axis=2) + new_expo
    weights = (expo / denom[:, :, None]).astype(jnp.bfloat16)
    new_weight = (new_expo / denom).astype(jnp.bfloat16)
    mixed = jnp.einsum("sht,std->shd", weights, v_cache, preferred_element_type=jnp.float32)
    mixed = (
        mixed
        + new_weight.astype(jnp.float32)[:, :, None] * new_value.astype(jnp.float32)[:, None, :]
    )
    return mixed.astype(jnp.bfloat16)


def make(nx, ny):
    def to_wire(x):
        return (x * WIRE_SCALE).astype(jnp.float16)

    def from_wire(x):
        return x.astype(jnp.float32) * (1.0 / WIRE_SCALE)

    def shards(activations, ln_gain, w_query, w_keyval, w_out, k_cache, v_cache, cache_lengths):
        gy = lax.axis_index("gy")
        head_dim = k_cache.shape[2]
        seqs = k_cache.shape[0]
        as_float = activations.astype(jnp.float32)
        sums = jnp.stack([jnp.sum(as_float, axis=1), jnp.sum(as_float * as_float, axis=1)])
        moments = sums
        for part in [swap(sums, "gx", nx, m) for m in range(1, nx)]:
            moments = moments + part
        row_mean = moments[0] / D
        row_var = moments[1] / D - row_mean * row_mean
        normed = (
            (as_float - row_mean[:, None])
            * lax.rsqrt(row_var + 1e-06)[:, None]
            * ln_gain.astype(jnp.float32)
        ).astype(jnp.bfloat16)
        gathered = lax.all_gather(normed, "gy", axis=0, tiled=True)
        kv_cols = w_keyval.shape[1] // ny
        w_own = lax.dynamic_slice_in_dim(w_keyval, gy * kv_cols, kv_cols, 1)
        q_cols = w_query.shape[1]
        kv_sum = jnp.dot(gathered, w_own, preferred_element_type=jnp.float32)
        q_sum = jnp.dot(gathered, w_query, preferred_element_type=jnp.float32)
        part = reduce_rows(
            jnp.concatenate([q_sum, kv_sum], axis=1), "gx", nx, to_wire, from_wire
        ).astype(jnp.bfloat16)
        mixed = lax.all_to_all(
            part.reshape(ny, seqs, q_cols + kv_cols), "gy", split_axis=0, concat_axis=0, tiled=True
        )
        queries = mixed[:, :, :q_cols].reshape(ny, seqs, -1, head_dim)
        queries = queries.transpose(1, 0, 2, 3).reshape(seqs, -1, head_dim)
        keyval = mixed[:, :, q_cols:].transpose(1, 0, 2).reshape(seqs, -1)
        attended = attend_local(
            queries, keyval[:, :head_dim], keyval[:, head_dim:], k_cache, v_cache, cache_lengths
        ).reshape(seqs, -1)
        returned = lax.all_to_all(attended, "gy", split_axis=1, concat_axis=0, tiled=True)
        everyone = gather_rows(returned, "gx", nx)
        partial_terms = jnp.dot(everyone, w_out, preferred_element_type=jnp.float32)
        return reduce_rows(
            partial_terms,
            "gy",
            ny,
            lambda x: x.astype(jnp.bfloat16),
            lambda x: x.astype(jnp.float32),
        ).astype(jnp.bfloat16)

    return shards


def solution(mesh):
    placed = (
        P(("groups", "gy"), "gx"),
        P("gx"),
        P("gx", "gy"),
        P("gx", None),
        P("gy", "gx"),
        P(("groups", "gx", "gy"), None, None),
        P(("groups", "gx", "gy"), None, None),
        P(("groups", "gx", "gy")),
    )
    return jax.shard_map(
        make(mesh.shape["gx"], mesh.shape["gy"]),
        mesh=mesh,
        in_specs=placed,
        out_specs=P(("groups", "gy"), "gx"),
        check_vma=False,
    )
```

time: 147 us -> 99.1 us (0.67)
  blocking collectives: 42.8 us -> 7.53 us
  starting transfers between devices: 3.35 us -> 23.6 us
  waiting for transfers between devices: 49.3 us -> 32 us
  between operations: 13.5 us -> 0.23 us
  matrix products: 28.4 us -> 26.5 us
    reduce_scatter x2 -> x0, waiting for transfers between devices: 45.9 us -> none  [the longest x1 23.3 us: shards(): lax.psum_scatter(partial_terms, 'gy', scatter_dimension=0, tiled=True)]
    ppermute x0 -> x12, waiting for transfers between devices: none -> 23.6 us  [swap(): return lax.ppermute(x, axis, [(k, k ^ m) for k in range(n)])]
    ppermute x0 -> x12, starting transfers between devices: none -> 17 us  [swap(): return lax.ppermute(x, axis, [(k, k ^ m) for k in range(n)])]
    all_gather x1 -> x0, blocking collectives: 15 us -> none  [shards(): lax.all_gather(returned, 'gx', axis=0, tiled=True)]
    psum x1 -> x0, blocking collectives: 13.4 us -> none  [shards(): lax.psum((jnp.sum(as_float, axis=1), jnp.sum(as_float * as_float, axis=1)...]
    all_to_all x1 -> x0, blocking collectives: 6.67 us -> none  [shards(): lax.all_to_all(attended, 'gy', split_axis=1, concat_axis=0, tiled=True)]
    all_to_all x1 -> x2, waiting for transfers between devices: 3.43 us -> 8.45 us  [the longest x1 4.24 us: shards(): lax.all_to_all(attended, 'gy', split_axis=1, concat_axis=0, tiled=True)]
    all_to_all x1 -> x2, starting transfers between devices: 3.3 us -> 6.61 us  [the longest x1 3.31 us: shards(): lax.all_to_all(part.reshape(ny, seqs, q_cols + kv_cols), 'gy', split_axis...]
  transfers between devices with their start and end apart: 3 -> 14, of which waited for: 3 -> 10; matrix products, arithmetic and copies ran while one was open for 1% -> 1% of each run, Pallas kernels for 0% -> 0%
where the time goes in v1:
time: 99.1 us; the launch traced here: 97.7 us
  waiting for transfers between devices  32 us (32%)
  matrix products  26.5 us (27%)
  starting transfers between devices  23.6 us (24%)
  blocking collectives  7.53 us (8%)
  other arithmetic  5.23 us (5%)
  local copies, waits for them, and re-layouts  2.66 us (3%)
    ppermute x12, waiting for transfers between devices, swap(): return lax.ppermute(x, axis, [(k, k ^ m) for k in range(n)])  23.6 us
    ppermute x12, starting transfers between devices, swap(): return lax.ppermute(x, axis, [(k, k ^ m) for k in range(n)])  17 us
    dot_general x1, matrix products, shards(): partial_terms = jnp.dot(everyone, w_out, preferred_element_type=jnp.float32)  11.8 us
    dot_general x1, matrix products, shards(): q_sum = jnp.dot(gathered, w_query, preferred_element_type=jnp.float32)  11.6 us
    all_gather x1, blocking collectives, shards(): gathered = lax.all_gather(normed, 'gy', axis=0, tiled=True)  7.53 us
    all_to_all x1, waiting for transfers between devices, shards(): lax.all_to_all(attended, 'gy', split_axis=1, concat_axis=0, tiled=True)  4.24 us
    all_to_all x1, waiting for transfers between devices, shards(): lax.all_to_all(part.reshape(ny, seqs, q_cols + kv_cols), 'gy', split_axis...  4.2 us
    all_to_all x1, starting transfers between devices, shards(): lax.all_to_all(part.reshape(ny, seqs, q_cols + kv_cols), 'gy', split_axis...  3.31 us
  transfers between devices with their start and end apart: 14, of which 10 were waited for; matrix products, arithmetic and copies ran while one was open for 1% of the time, Pallas kernels for 0%

profile of v1, /device:TPU:0, one launch (start us, length us, event | category | flops | bytes accessed | tf_op | source)
XLA Modules:
  0.0 97.7 jit_solution(12229376086368987174)
XLA Ops:
  0.0 1.2 %convert_reduce_fusion = (f32[16]{0:T(128)S(1)}, f32[16]{0:T(128)S(1)}) fusion(bf16[16,4608]{1,0:T(8,128)(2,1)} %param.8), kind=kLoop, calls=%fused_computation.19 | loop fusion | flops 294880 | bytes 147584 | tf_op jit(solution)/shard_map/reduce_sum | solution.py:74
  1.2 3.1 %collective-permute-start = (f32[2,16]{1,0:T(2,128)S(1)}, f32[2,16]{1,0:T(2,128)S(1)}, u32[]{:S(2)}, u32[]{:S(2)}) collective-permute-start(f32[2,16]{1,0:T(2,128)S(1)} %pad_maximum_fusion), channel_id=1, source_target_pairs={{0,4},{4,0},{8,12},{12,8},{1,5},{5,1},{9,13},{13,9},{2,6},{6,2},{1... | collective-permute-start | bytes 392 | tf_op jit(solution)/shard_map/ppermute | solution.py:11
  4.3 2.6 %collective-permute-start.1 = (f32[2,16]{1,0:T(2,128)S(1)}, f32[2,16]{1,0:T(2,128)S(1)}, u32[]{:S(2)}, u32[]{:S(2)}) collective-permute-start(f32[2,16]{1,0:T(2,128)S(1)} %pad_maximum_fusion), channel_id=1, source_target_pairs={{0,8},{4,12},{8,0},{12,4},{1,9},{5,13},{9,1},{13,5},{2,10},{6,14},... | collective-permute-start | bytes 392 | tf_op jit(solution)/shard_map/ppermute | solution.py:11
  7.6 1.2 %collective-permute-done.1 = f32[2,16]{1,0:T(2,128)S(1)} collective-permute-done((f32[2,16]{1,0:T(2,128)S(1)}, f32[2,16]{1,0:T(2,128)S(1)}, u32[]{:S(2)}, u32[]{:S(2)}) %collective-permute-start.1) | collective-permute-done | bytes 160 | tf_op jit(solution)/shard_map/ppermute | solution.py:11
  8.8 3.5 %collective-permute-done.2 = f32[2,16]{1,0:T(2,128)S(1)} collective-permute-done((f32[2,16]{1,0:T(2,128)S(1)}, f32[2,16]{1,0:T(2,128)S(1)}, u32[]{:S(2)}, u32[]{:S(2)}) %collective-permute-start.2) | collective-permute-done | bytes 160 | tf_op jit(solution)/shard_map/ppermute | solution.py:11
  12.3 1.0 %fusion.12 = bf16[16,4608]{1,0:T(8,128)(2,1)S(1)} fusion(bf16[16,4608]{1,0:T(8,128)(2,1)} %param.8, f32[4608]{0:T(1024)S(1)} %convert_element_type.67, f32[16]{0:T(128)S(1)} %fusion.34, f32[16]{0:T(128)S(1)} %multiply_bitcast_fusion), kind=kLoop, calls=%fused_computation.27 | loop fusion | flops 368640 | bytes 313472 | tf_op jit(solution)/shard_map/convert_element_type | solution.py:84
  13.3 7.5 %all_gather.3 = bf16[64,4608]{1,0:T(8,128)(2,1)S(1)} all-gather(bf16[16,4608]{1,0:T(8,128)(2,1)S(1)} %fusion.12), channel_id=1, replica_groups=mesh['groups'=2,'gx'=4,'gy'=4] {'gy'}, dimensions={0}, use_global_device_ids=true | all-gather | bytes 737280 | tf_op jit(solution)/shard_map/all_gather | solution.py:85
  20.9 11.6 %fusion.38 = f32[64,3072]{1,0:T(8,128)S(1)} fusion(bf16[64,4608]{1,0:T(8,128)(2,1)S(1)} %all_gather.3, bf16[4608,3072]{1,0:T(8,128)(2,1)} %param.10), kind=kOutput, calls=%fused_computation.72 | convolution fusion | flops 1811939328 | bytes 29687808 | tf_op jit(solution)/shard_map/dot_general | solution.py:90
  32.5 1.6 %fusion.1 = f32[64,128]{1,0:T(8,128)S(1)} fusion(bf16[64,4608]{1,0:T(8,128)(2,1)S(1)} %all_gather.3, bf16[4608,512]{1,0:T(8,128)(2,1)} %param.11, s32[]{:T(128)S(6)} %select_n.38), kind=kOutput, calls=%fused_computation.6 | convolution fusion | flops 75497472 | bytes 1802244 | tf_op jit(solution)/shard_map/dot_general | solution.py:89
  35.1 3.6 %collective-permute-start.5 = (f16[16,3200]{1,0:T(8,128)(2,1)S(1)}, f16[16,3200]{1,0:T(8,128)(2,1)S(1)}, u32[]{:S(2)}, u32[]{:S(2)}) collective-permute-start(f16[16,3200]{1,0:T(8,128)(2,1)S(1)} %get-tuple-element.12), channel_id=1, source_target_pairs={{0,12},{4,8},{8,4},{12,0},{1,13},{5,9},{9,5},{13,1},{2,14},{6,10},... | collective-permute-start | bytes 307208 | tf_op jit(solution)/shard_map/ppermute | solution.py:11
  38.7 1.9 %collective-permute-done.3 = f16[16,3200]{1,0:T(8,128)(2,1)S(1)} collective-permute-done((f16[16,3200]{1,0:T(8,128)(2,1)S(1)}, f16[16,3200]{1,0:T(8,128)(2,1)S(1)}, u32[]{:S(2)}, u32[]{:S(2)}) %collective-permute-start.3) | collective-permute-done | bytes 102432 | tf_op jit(solution)/shard_map/ppermute | solution.py:11
  40.6 4.8 %collective-permute-done.4 = f16[16,3200]{1,0:T(8,128)(2,1)S(1)} collective-permute-done((f16[16,3200]{1,0:T(8,128)(2,1)S(1)}, f16[16,3200]{1,0:T(8,128)(2,1)S(1)}, u32[]{:S(2)}, u32[]{:S(2)}) %collective-permute-start.4) | collective-permute-done | bytes 102432 | tf_op jit(solution)/shard_map/ppermute | solution.py:11
  46.1 3.3 %all-to-all-start = ((bf16[4,4,3200]{2,1,0:T(4,128)(2,1)}), bf16[4,4,3200]{2,1,0:T(4,128)(2,1)S(1)}, u32[]{:S(2)}, u32[]{:S(2)}) async-start(bf16[4,4,3200]{2,1,0:T(4,128)(2,1)} %reshape.64), calls=%async_computation | async-start | bytes 204800 | tf_op jit(solution)/shard_map/all_to_all | solution.py:94
  49.5 4.2 %all-to-all-done = bf16[4,4,3200]{2,1,0:T(4,128)(2,1)S(1)} async-done(((bf16[4,4,3200]{2,1,0:T(4,128)(2,1)}), bf16[4,4,3200]{2,1,0:T(4,128)(2,1)S(1)}, u32[]{:S(2)}, u32[]{:S(2)}) %all-to-all-start) | async-done | bytes 102432 | tf_op jit(solution)/shard_map/all_to_all | solution.py:94
  54.1 0.8 fusion.37
  56.7 3.3 %all-to-all-start.1 = ((bf16[4,4,3072]{2,0,1:T(4,128)(2,1)}), bf16[4,4,3072]{2,0,1:T(4,128)(2,1)S(1)}, u32[]{:S(2)}, u32[]{:S(2)}) async-start(bf16[4,4,3072]{2,0,1:T(4,128)(2,1)} %copy.12), calls=%async_computation.1 | async-start | bytes 196608 | tf_op jit(solution)/shard_map/all_to_all | solution.py:103
  60.0 4.2 %all-to-all-done.1 = bf16[4,4,3072]{2,0,1:T(4,128)(2,1)S(1)} async-done(((bf16[4,4,3072]{2,0,1:T(4,128)(2,1)}), bf16[4,4,3072]{2,0,1:T(4,128)(2,1)S(1)}, u32[]{:S(2)}, u32[]{:S(2)}) %all-to-all-start.1) | async-done | bytes 98336 | tf_op jit(solution)/shard_map/all_to_all | solution.py:103
  64.3 2.3 %collective-permute-start.6 = (bf16[16,3072]{1,0:T(8,128)(2,1)S(1)}, bf16[16,3072]{1,0:T(8,128)(2,1)S(1)}, u32[]{:S(2)}, u32[]{:S(2)}) collective-permute-start(bf16[16,3072]{1,0:T(8,128)(2,1)S(1)} %all_to_all.21), channel_id=1, source_target_pairs={{0,4},{4,0},{8,12},{12,8},{1,5},{5,1},{9,13},{13,9},{2,6},{6,2},{1... | collective-permute-start | bytes 294920 | tf_op jit(solution)/shard_map/ppermute | solution.py:11
  66.6 2.4 %collective-permute-start.8 = (bf16[16,3072]{1,0:T(8,128)(2,1)S(1)}, bf16[16,3072]{1,0:T(8,128)(2,1)S(1)}, u32[]{:S(2)}, u32[]{:S(2)}) collective-permute-start(bf16[16,3072]{1,0:T(8,128)(2,1)S(1)} %all_to_all.21), channel_id=1, source_target_pairs={{0,12},{4,8},{8,4},{12,0},{1,13},{5,9},{9,5},{13,1},{2,14},{6,10},... | collective-permute-start | bytes 294920 | tf_op jit(solution)/shard_map/ppermute | solution.py:11
  69.8 6.5 %collective-permute-done.7 = bf16[16,3072]{1,0:T(8,128)(2,1)S(1)} collective-permute-done((bf16[16,3072]{1,0:T(8,128)(2,1)S(1)}, bf16[16,3072]{1,0:T(8,128)(2,1)S(1)}, u32[]{:S(2)}, u32[]{:S(2)}) %collective-permute-start.7) | collective-permute-done | bytes 98336 | tf_op jit(solution)/shard_map/ppermute | solution.py:11
  76.4 11.8 %fusion.39 = f32[64,4608]{1,0:T(8,128)S(1)} fusion(bf16[64,3072]{1,0:T(8,128)(2,1)S(1)} %constant_dynamic-update-slice_fusion, bf16[3072,4608]{1,0:T(8,128)(2,1)} %param.12), kind=kOutput, calls=%fused_computation.73 | convolution fusion | flops 1811939328 | bytes 29884416 | tf_op jit(solution)/shard_map/dot_general | solution.py:105
  89.6 1.5 %collective-permute-start.9 = (bf16[16,4608]{1,0:T(8,128)(2,1)}, bf16[16,4608]{1,0:T(8,128)(2,1)}, u32[]{:S(2)}, u32[]{:S(2)}) collective-permute-start(bf16[16,4608]{1,0:T(8,128)(2,1)} %get-tuple-element.7), channel_id=1, source_target_pairs={{0,1},{1,0},{2,3},{3,2},{4,5},{5,4},{6,7},{7,6},{8,9},{9,8},{10,11... | collective-permute-start | bytes 442376 | tf_op jit(solution)/shard_map/ppermute | solution.py:11
  91.1 4.7 %collective-permute-done.10 = bf16[16,4608]{1,0:T(8,128)(2,1)S(1)} collective-permute-done((bf16[16,4608]{1,0:T(8,128)(2,1)}, bf16[16,4608]{1,0:T(8,128)(2,1)S(1)}, u32[]{:S(2)}, u32[]{:S(2)}) %collective-permute-start.10) | collective-permute-done | bytes 147488 | tf_op jit(solution)/shard_map/ppermute | solution.py:11
  96.0 1.7 %add_convert_fusion = bf16[16,4608]{1,0:T(8,128)(2,1)} fusion(bf16[16,4608]{1,0:T(8,128)(2,1)} %collective-permute-done.11, bf16[16,4608]{1,0:T(8,128)(2,1)S(1)} %collective-permute-done.10, bf16[16,4608]{1,0:T(8,128)(2,1)} %collective-permute-done.9, f32[64,4608]{1,0:T(8,128)S(1)} %fusion.39, s32[]{:T(128)S(6)} %select_n.45), kind=kLoop, calls=%fused_computation.28 | loop fusion | flops 516096 | bytes 884740 | tf_op jit(solution)/shard_map/convert_element_type | solution.py:112
  (48 shorter events, 7.1 us)
Async XLA Ops:
  0.0 54.1 %copy-start = (bf16[4,1024,256]{2,1,0:T(8,128)(2,1)S(1)}, bf16[4,1024,256]{2,1,0:T(8,128)(2,1)}, u32[]{:S(2)}) copy-start(bf16[4,1024,256]{2,1,0:T(8,128)(2,1)} %param.13) | copy-start | bytes 6291460
  1.2 6.4 %collective-permute-start = (f32[2,16]{1,0:T(2,128)S(1)}, f32[2,16]{1,0:T(2,128)S(1)}, u32[]{:S(2)}, u32[]{:S(2)}) collective-permute-start(f32[2,16]{1,0:T(2,128)S(1)} %pad_maximum_fusion), channel_id=1, source_target_pairs={{0,4},{4,0},{8,12},{12,8},{1,5},{5,1},{9,13},{13,9},{2,6},{6,2},{1... | collective-permute-start | bytes 392 | tf_op jit(solution)/shard_map/ppermute | solution.py:11
  4.3 4.5 %collective-permute-start.1 = (f32[2,16]{1,0:T(2,128)S(1)}, f32[2,16]{1,0:T(2,128)S(1)}, u32[]{:S(2)}, u32[]{:S(2)}) collective-permute-start(f32[2,16]{1,0:T(2,128)S(1)} %pad_maximum_fusion), channel_id=1, source_target_pairs={{0,8},{4,12},{8,0},{12,4},{1,9},{5,13},{9,1},{13,5},{2,10},{6,14},... | collective-permute-start | bytes 392 | tf_op jit(solution)/shard_map/ppermute | solution.py:11
  6.9 5.4 %collective-permute-start.2 = (f32[2,16]{1,0:T(2,128)S(1)}, f32[2,16]{1,0:T(2,128)S(1)}, u32[]{:S(2)}, u32[]{:S(2)}) collective-permute-start(f32[2,16]{1,0:T(2,128)S(1)} %pad_maximum_fusion), channel_id=1, source_target_pairs={{0,12},{4,8},{8,4},{12,0},{1,13},{5,9},{9,5},{13,1},{2,14},{6,10},... | collective-permute-start | bytes 392 | tf_op jit(solution)/shard_map/ppermute | solution.py:11
  32.5 17.0 %copy-start.2 = (s32[4]{0:T(128)S(1)}, s32[4]{0:T(128)}, u32[]{:S(2)}) copy-start(s32[4]{0:T(128)} %param.15) | copy-start | bytes 52
  34.2 6.4 %collective-permute-start.3 = (f16[16,3200]{1,0:T(8,128)(2,1)S(1)}, f16[16,3200]{1,0:T(8,128)(2,1)S(1)}, u32[]{:S(2)}, u32[]{:S(2)}) collective-permute-start(f16[16,3200]{1,0:T(8,128)(2,1)S(1)} %get-tuple-element.10), channel_id=1, source_target_pairs={{0,4},{4,0},{8,12},{12,8},{1,5},{5,1},{9,13},{13,9},{2,6},{6,2},{1... | collective-permute-start | bytes 307208 | tf_op jit(solution)/shard_map/ppermute | solution.py:11
  34.3 11.1 %collective-permute-start.4 = (f16[16,3200]{1,0:T(8,128)(2,1)S(1)}, f16[16,3200]{1,0:T(8,128)(2,1)S(1)}, u32[]{:S(2)}, u32[]{:S(2)}) collective-permute-start(f16[16,3200]{1,0:T(8,128)(2,1)S(1)} %get-tuple-element.11), channel_id=1, source_target_pairs={{0,8},{4,12},{8,0},{12,4},{1,9},{5,13},{9,1},{13,5},{2,10},{6,14},... | collective-permute-start | bytes 307208 | tf_op jit(solution)/shard_map/ppermute | solution.py:11
  35.1 10.3 %collective-permute-start.5 = (f16[16,3200]{1,0:T(8,128)(2,1)S(1)}, f16[16,3200]{1,0:T(8,128)(2,1)S(1)}, u32[]{:S(2)}, u32[]{:S(2)}) collective-permute-start(f16[16,3200]{1,0:T(8,128)(2,1)S(1)} %get-tuple-element.12), channel_id=1, source_target_pairs={{0,12},{4,8},{8,4},{12,0},{1,13},{5,9},{9,5},{13,1},{2,14},{6,10},... | collective-permute-start | bytes 307208 | tf_op jit(solution)/shard_map/ppermute | solution.py:11
  46.1 7.6 %all-to-all-start = ((bf16[4,4,3200]{2,1,0:T(4,128)(2,1)}), bf16[4,4,3200]{2,1,0:T(4,128)(2,1)S(1)}, u32[]{:S(2)}, u32[]{:S(2)}) async-start(bf16[4,4,3200]{2,1,0:T(4,128)(2,1)} %reshape.64), calls=%async_computation | async-start | bytes 204800 | tf_op jit(solution)/shard_map/all_to_all | solution.py:94
  53.8 1.6 %copy-start.3 = (bf16[4,1024,256]{2,1,0:T(8,128)(2,1)S(1)}, bf16[4,1024,256]{2,1,0:T(8,128)(2,1)}, u32[]{:S(2)}) copy-start(bf16[4,1024,256]{2,1,0:T(8,128)(2,1)} %param.14) | copy-start | bytes 6291460
  56.7 7.6 %all-to-all-start.1 = ((bf16[4,4,3072]{2,0,1:T(4,128)(2,1)}), bf16[4,4,3072]{2,0,1:T(4,128)(2,1)S(1)}, u32[]{:S(2)}, u32[]{:S(2)}) async-start(bf16[4,4,3072]{2,0,1:T(4,128)(2,1)} %copy.12), calls=%async_computation.1 | async-start | bytes 196608 | tf_op jit(solution)/shard_map/all_to_all | solution.py:103
  64.3 5.5 %collective-permute-start.6 = (bf16[16,3072]{1,0:T(8,128)(2,1)S(1)}, bf16[16,3072]{1,0:T(8,128)(2,1)S(1)}, u32[]{:S(2)}, u32[]{:S(2)}) collective-permute-start(bf16[16,3072]{1,0:T(8,128)(2,1)S(1)} %all_to_all.21), channel_id=1, source_target_pairs={{0,4},{4,0},{8,12},{12,8},{1,5},{5,1},{9,13},{13,9},{2,6},{6,2},{1... | collective-permute-start | bytes 294920 | tf_op jit(solution)/shard_map/ppermute | solution.py:11
  66.6 9.7 %collective-permute-start.7 = (bf16[16,3072]{1,0:T(8,128)(2,1)S(1)}, bf16[16,3072]{1,0:T(8,128)(2,1)S(1)}, u32[]{:S(2)}, u32[]{:S(2)}) collective-permute-start(bf16[16,3072]{1,0:T(8,128)(2,1)S(1)} %all_to_all.21), channel_id=1, source_target_pairs={{0,8},{4,12},{8,0},{12,4},{1,9},{5,13},{9,1},{13,5},{2,10},{6,14},... | collective-permute-start | bytes 294920 | tf_op jit(solution)/shard_map/ppermute | solution.py:11
  66.6 9.8 %collective-permute-start.8 = (bf16[16,3072]{1,0:T(8,128)(2,1)S(1)}, bf16[16,3072]{1,0:T(8,128)(2,1)S(1)}, u32[]{:S(2)}, u32[]{:S(2)}) collective-permute-start(bf16[16,3072]{1,0:T(8,128)(2,1)S(1)} %all_to_all.21), channel_id=1, source_target_pairs={{0,12},{4,8},{8,4},{12,0},{1,13},{5,9},{9,5},{13,1},{2,14},{6,10},... | collective-permute-start | bytes 294920 | tf_op jit(solution)/shard_map/ppermute | solution.py:11
  76.4 21.4 %copy-start.1 = (bf16[4,1024,256]{2,1,0:T(8,128)(2,1)S(1)}, bf16[4,1024,256]{2,1,0:T(8,128)(2,1)}, u32[]{:S(2)}) copy-start(bf16[4,1024,256]{2,1,0:T(8,128)(2,1)} %param.13) | copy-start | bytes 6291460
  88.9 6.9 %collective-permute-start.10 = (bf16[16,4608]{1,0:T(8,128)(2,1)}, bf16[16,4608]{1,0:T(8,128)(2,1)S(1)}, u32[]{:S(2)}, u32[]{:S(2)}) collective-permute-start(bf16[16,4608]{1,0:T(8,128)(2,1)} %get-tuple-element.9), channel_id=1, source_target_pairs={{0,2},{1,3},{2,0},{3,1},{4,6},{5,7},{6,4},{7,5},{8,10},{9,11},{10,... | collective-permute-start | bytes 442376 | tf_op jit(solution)/shard_map/ppermute | solution.py:11
  89.6 6.5 %collective-permute-start.11 = (bf16[16,4608]{1,0:T(8,128)(2,1)}, bf16[16,4608]{1,0:T(8,128)(2,1)}, u32[]{:S(2)}, u32[]{:S(2)}) collective-permute-start(bf16[16,4608]{1,0:T(8,128)(2,1)} %get-tuple-element.8), channel_id=1, source_target_pairs={{0,3},{1,2},{2,1},{3,0},{4,7},{5,6},{6,5},{7,4},{8,11},{9,10},{10,... | collective-permute-start | bytes 442376 | tf_op jit(solution)/shard_map/ppermute | solution.py:11
  89.6 6.5 %collective-permute-start.9 = (bf16[16,4608]{1,0:T(8,128)(2,1)}, bf16[16,4608]{1,0:T(8,128)(2,1)}, u32[]{:S(2)}, u32[]{:S(2)}) collective-permute-start(bf16[16,4608]{1,0:T(8,128)(2,1)} %get-tuple-element.7), channel_id=1, source_target_pairs={{0,1},{1,0},{2,3},{3,2},{4,5},{5,4},{6,7},{7,6},{8,9},{9,8},{10,11... | collective-permute-start | bytes 442376 | tf_op jit(solution)/shard_map/ppermute | solution.py:11

commit v2 on v1

v2 whole, which is shorter than its diff:
```python
import jax
import jax.numpy as jnp
from jax import lax
from jax.sharding import PartitionSpec as P
import jax.experimental.pallas as pl
import jax.experimental.pallas.tpu as pltpu

D = 18432
WIRE_SCALE = 16.0


def swap(x, axis, n, m):
    return lax.ppermute(x, axis, [(k, k ^ m) for k in range(n)])


def rows_of(x, block, n):
    size = x.shape[0] // n
    return lax.dynamic_slice_in_dim(x, block * size, size, 0)


def far_first(n):
    return list(range(n // 2, n)) + list(range(1, n // 2))


def exchange(parts, axis, n):
    back = {m: swap(parts[m], axis, n, m) for m in far_first(n)}
    return [parts[0]] + [back[m] for m in range(1, n)]


def reduce_rows(partial, axis, n, encode, decode):
    me = lax.axis_index(axis)
    got = [swap(encode(rows_of(partial, me ^ m, n)), axis, n, m) for m in far_first(n)]
    total = rows_of(partial, me, n)
    for part in got:
        total = total + decode(part)
    return total


def in_order(parts, axis):
    me = lax.axis_index(axis)
    size = parts[0].shape[0]
    out = jnp.zeros((len(parts) * size,) + parts[0].shape[1:], parts[0].dtype)
    for m in [0] + far_first(len(parts)):
        out = lax.dynamic_update_slice_in_dim(out, parts[m], (me ^ m) * size, 0)
    return out


def gather_rows(x, axis, n):
    return in_order(exchange([x] * n, axis, n), axis)


def double_rows(x, axis, n):
    me = lax.axis_index(axis)
    size = x.shape[0]
    held = x[None]
    bit = n // 2
    while bit:
        other = swap(held, axis, n, bit)
        low = (me & bit) == 0
        held = jnp.stack([jnp.where(low, held, other), jnp.where(low, other, held)])
        held = held.reshape((-1,) + x.shape)
        bit //= 2
    bits = n.bit_length() - 1
    held = held.reshape((2,) * bits + x.shape)
    held = held.transpose(tuple(reversed(range(bits))) + (bits, bits + 1))
    return held.reshape(n * size, x.shape[1])


def in_vmem():
    return pl.BlockSpec(memory_space=pltpu.VMEM)


def dot_f32(x, w):
    return jnp.dot(x, w, preferred_element_type=jnp.float32)


def fetch(w, start, cols, after):
    def body(w_ref, after_ref, out_ref, sem):
        copy = pltpu.make_async_copy(w_ref.at[:, pl.ds(start, cols)], out_ref, sem)
        copy.start()
        copy.wait()

    rows = w.shape[0]
    return pl.pallas_call(
        body,
        out_shape=pltpu.VMEM((rows, cols), w.dtype),
        in_specs=[pl.BlockSpec(memory_space=pltpu.HBM), pl.BlockSpec(memory_space=pl.ANY)],
        out_specs=in_vmem(),
        scratch_shapes=[pltpu.SemaphoreType.DMA],
        compiler_params=pltpu.CompilerParams(vmem_limit_bytes=1 << 20),
        cost_estimate=pl.CostEstimate(
            flops=0, bytes_accessed=2 * rows * cols, transcendentals=0
        ),
        name="fetch",
    )(pltpu.with_memory_space_constraint(w, pltpu.HBM), after)


def tiles(cols, size=512):
    return [(c, min(size, cols - c)) for c in range(0, cols, size)]


def project(x, w_head, w_all, w_last, last_cols, axis):
    depth, cols = w_all.shape
    held = w_head.shape[1]
    rest = tiles(cols - held)
    whole_tiles = last_cols % 128 == 0
    if not whole_tiles:
        start = lax.axis_index(axis) * last_cols
        w_last = lax.dynamic_slice_in_dim(w_last, start, last_cols, 1)

    def body(x_ref, head_ref, all_ref, last_ref, out_ref, scratch, last_scratch, sems):
        start = 0
        if whole_tiles:
            start = pl.multiple_of(lax.axis_index(axis) * last_cols, 128)
        first = pltpu.make_async_copy(
            last_ref.at[:, pl.ds(start, last_cols)], last_scratch, sems.at[len(rest)]
        )
        copies = [
            pltpu.make_async_copy(
                all_ref.at[:, pl.ds(held + c, size)], scratch.at[:, pl.ds(c, size)], sems.at[i]
            )
            for i, (c, size) in enumerate(rest)
        ]
        for copy in [first] + copies:
            copy.start()
        for c, size in tiles(held):
            out_ref[:, c : c + size] = dot_f32(x_ref[...], head_ref[:, c : c + size])
        first.wait()
        out_ref[:, cols : cols + last_cols] = dot_f32(x_ref[...], last_scratch[...])
        for copy, (c, size) in zip(copies, rest):
            copy.wait()
            out_ref[:, held + c : held + c + size] = dot_f32(x_ref[...], scratch[:, c : c + size])

    rows = x.shape[0]
    in_hbm = pl.BlockSpec(memory_space=pltpu.HBM)
    return pl.pallas_call(
        body,
        out_shape=jax.ShapeDtypeStruct((rows, cols + last_cols), jnp.float32),
        in_specs=[in_vmem(), in_vmem(), in_hbm, in_hbm],
        out_specs=in_vmem(),
        scratch_shapes=[
            pltpu.VMEM((depth, cols - held), w_all.dtype),
            pltpu.VMEM((depth, last_cols), w_last.dtype),
            pltpu.SemaphoreType.DMA((len(rest) + 1,)),
        ],
        compiler_params=pltpu.CompilerParams(vmem_limit_bytes=28 << 20),
        cost_estimate=pl.CostEstimate(
            flops=2 * rows * depth * cols, bytes_accessed=2 * depth * cols, transcendentals=0
        ),
        name="project",
    )(
        x,
        pltpu.with_memory_space_constraint(w_head, pltpu.VMEM),
        pltpu.with_memory_space_constraint(w_all, pltpu.HBM),
        pltpu.with_memory_space_constraint(w_last, pltpu.HBM),
    )


def multiply_left(x, w_held, w_all, cut):
    depth, cols = w_all.shape
    held = w_held.shape[1]

    def body(x_ref, held_ref, all_ref, out_ref, rest_ref, sem):
        copy = pltpu.make_async_copy(all_ref.at[:, pl.ds(held, cols - held)], rest_ref, sem)
        copy.start()
        for c, size in tiles(cut):
            out_ref[:, c : c + size] = dot_f32(x_ref[...], held_ref[:, c : c + size])
        copy.wait()

    rows = x.shape[0]
    return pl.pallas_call(
        body,
        out_shape=[
            jax.ShapeDtypeStruct((rows, cut), jnp.float32),
            pltpu.VMEM((depth, cols - held), w_all.dtype),
        ],
        in_specs=[in_vmem(), in_vmem(), pl.BlockSpec(memory_space=pltpu.HBM)],
        out_specs=[in_vmem(), in_vmem()],
        scratch_shapes=[pltpu.SemaphoreType.DMA],
        compiler_params=pltpu.CompilerParams(vmem_limit_bytes=4 << 20),
        cost_estimate=pl.CostEstimate(
            flops=2 * rows * depth * cut, bytes_accessed=2 * depth * cut, transcendentals=0
        ),
        name="multiply_left",
    )(
        x,
        pltpu.with_memory_space_constraint(w_held, pltpu.VMEM),
        pltpu.with_memory_space_constraint(w_all, pltpu.HBM),
    )


def multiply_right(x, w_held, w_rest, cut):
    held, extra = w_held.shape[1] - cut, w_rest.shape[1]

    def body(x_ref, held_ref, rest_ref, out_ref):
        for c, size in tiles(held):
            out_ref[:, c : c + size] = dot_f32(x_ref[...], held_ref[:, cut + c : cut + c + size])
        for c, size in tiles(extra):
            out_ref[:, held + c : held + c + size] = dot_f32(x_ref[...], rest_ref[:, c : c + size])

    rows, depth = x.shape
    return pl.pallas_call(
        body,
        out_shape=jax.ShapeDtypeStruct((rows, held + extra), jnp.float32),
        in_specs=[in_vmem()] * 3,
        out_specs=in_vmem(),
        compiler_params=pltpu.CompilerParams(vmem_limit_bytes=4 << 20),
        cost_estimate=pl.CostEstimate(
            flops=2 * rows * depth * (held + extra),
            bytes_accessed=2 * depth * (held + extra),
            transcendentals=0,
        ),
        name="multiply_right",
    )(
        x,
        pltpu.with_memory_space_constraint(w_held, pltpu.VMEM),
        pltpu.with_memory_space_constraint(w_rest, pltpu.VMEM),
    )


def attend_local(query_heads, new_key, new_value, k_cache, v_cache, cache_lengths):
    scores = (
        jnp.einsum("shd,std->sht", query_heads, k_cache, preferred_element_type=jnp.float32)
        * 0.0625
    )
    new_score = (
        jnp.einsum("shd,sd->sh", query_heads, new_key, preferred_element_type=jnp.float32) * 0.0625
    )
    positions = lax.broadcasted_iota(jnp.int32, (1, 1, k_cache.shape[1]), 2)
    live = positions < cache_lengths[:, None, None]
    masked = jnp.where(live, scores, jnp.float32(-1e30))
    top = jnp.maximum(jnp.max(masked, axis=2), new_score)
    expo = jnp.where(live, jnp.exp(masked - top[:, :, None]), jnp.float32(0.0))
    new_expo = jnp.exp(new_score - top)
    denom = jnp.sum(expo, axis=2) + new_expo
    weights = (expo / denom[:, :, None]).astype(jnp.bfloat16)
    new_weight = (new_expo / denom).astype(jnp.bfloat16)
    mixed = jnp.einsum("sht,std->shd", weights, v_cache, preferred_element_type=jnp.float32)
    mixed = (
        mixed
        + new_weight.astype(jnp.float32)[:, :, None] * new_value.astype(jnp.float32)[:, None, :]
    )
    return mixed.astype(jnp.bfloat16)


def whole_tiles(cols):
    return cols // 128 * 128


def make(nx, ny):
    def to_wire(x):
        return (x * WIRE_SCALE).astype(jnp.float16)

    def from_wire(x):
        return x.astype(jnp.float32) * (1.0 / WIRE_SCALE)

    def shards(activations, ln_gain, w_query, w_keyval, w_out, k_cache, v_cache, cache_lengths):
        gy = lax.axis_index("gy")
        head_dim = k_cache.shape[2]
        seqs = k_cache.shape[0]
        own = activations.astype(jnp.float32)
        sums = jnp.stack([jnp.sum(own, axis=1), jnp.sum(own * own, axis=1)], axis=1)
        partial_moments = double_rows(sums, "gy", ny)
        moments = partial_moments
        as_float = double_rows(activations, "gy", ny).astype(jnp.float32)
        for part in exchange([moments] * nx, "gx", nx)[1:]:
            moments = moments + part
        row_mean = moments[:, 0] / D
        row_var = moments[:, 1] / D - row_mean * row_mean
        normed = (
            (as_float - row_mean[:, None])
            * lax.rsqrt(row_var + 1e-06)[:, None]
            * ln_gain.astype(jnp.float32)
        ).astype(jnp.bfloat16)
        kv_cols = w_keyval.shape[1] // ny
        q_cols = w_query.shape[1]
        w_head = fetch(w_query, 0, whole_tiles(q_cols * 3 // 8), partial_moments)
        projected = project(normed, w_head, w_query, w_keyval, kv_cols, "gy")
        part = reduce_rows(projected, "gx", nx, to_wire, from_wire).astype(jnp.bfloat16)
        mixed = exchange([rows_of(part, gy ^ m, ny) for m in range(ny)], "gy", ny)
        queries = jnp.concatenate(
            [x[:, :q_cols].reshape(seqs, -1, head_dim) for x in mixed], axis=1
        )
        keyval = in_order([x[:, q_cols:][None] for x in mixed], "gy")
        keyval = keyval.transpose(1, 0, 2).reshape(seqs, -1)
        attended = attend_local(
            queries, keyval[:, :head_dim], keyval[:, head_dim:], k_cache, v_cache, cache_lengths
        )
        heads = attended.shape[1] // ny
        returned = in_order(
            exchange(
                [attended[:, m * heads : (m + 1) * heads].reshape(seqs, -1) for m in range(ny)],
                "gy",
                ny,
            ),
            "gy",
        )
        width = w_out.shape[1]
        cut = whole_tiles(width * 5 // 8)
        w_held = fetch(w_out, 0, whole_tiles(width * 2 // 3), returned)
        everyone = gather_rows(returned, "gx", nx)
        left, w_rest = multiply_left(everyone, w_held, w_out, cut)
        right = multiply_right(everyone, w_held, w_rest, cut)
        outs = [
            reduce_rows(
                x,
                "gy",
                ny,
                lambda x: x.astype(jnp.bfloat16),
                lambda x: x.astype(jnp.float32),
            ).astype(jnp.bfloat16)
            for x in (left, right)
        ]
        return jnp.concatenate(outs, axis=1)

    return shards


def solution(mesh):
    placed = (
        P(("groups", "gy"), "gx"),
        P("gx"),
        P("gx", "gy"),
        P("gx", None),
        P("gy", "gx"),
        P(("groups", "gx", "gy"), None, None),
        P(("groups", "gx", "gy"), None, None),
        P(("groups", "gx", "gy")),
    )
    return jax.shard_map(
        make(mesh.shape["gx"], mesh.shape["gy"]),
        mesh=mesh,
        in_specs=placed,
        out_specs=P(("groups", "gy"), "gx"),
        check_vma=False,
    )
```

time: 99.1 us -> 79.2 us (0.80); the launches traced: 97.7 us -> 78.9 us
  Pallas kernels: 0 us -> 26.6 us
  matrix products: 26.5 us -> 1.49 us
  waiting for transfers between devices: 32 us -> 21.3 us
  blocking collectives: 7.53 us -> 0 us
  other arithmetic: 5.23 us -> 3.67 us
  local copies, waits for them, and re-layouts: 2.66 us -> 1.17 us
    pallas_call x0 -> x5, Pallas kernels: none -> 26.6 us  [the longest x2 10.5 us: fetch(): pl.pallas_call(body, out_shape=pltpu.VMEM((rows, cols), w.dtype), in_spec...]
    dot_general x3 -> x0, matrix products: 25 us -> none  [the longest x1 11.8 us: shards(): partial_terms = jnp.dot(everyone, w_out, preferred_element_type=jnp.float32)]
    all_to_all x2 -> x0, waiting for transfers between devices: 8.45 us -> none  [the longest x1 4.24 us: shards(): lax.all_to_all(attended, 'gy', split_axis=1, concat_axis=0, tiled=True)]
    all_gather x1 -> x0, blocking collectives: 7.53 us -> none  [shards(): gathered = lax.all_gather(normed, 'gy', axis=0, tiled=True)]
    ppermute x12 -> x25, starting transfers between devices: 17 us -> 24.3 us  [swap(): return lax.ppermute(x, axis, [(k, k ^ m) for k in range(n)])]
    all_to_all x2 -> x0, starting transfers between devices: 6.61 us -> none  [the longest x1 3.31 us: shards(): lax.all_to_all(part.reshape(ny, seqs, q_cols + kv_cols), 'gy', split_axis...]
    ppermute x12 -> x25, waiting for transfers between devices: 23.6 us -> 21.3 us  [swap(): return lax.ppermute(x, axis, [(k, k ^ m) for k in range(n)])]
    convert_element_type x2 -> x4, other arithmetic: 1.78 us -> 0.23 us  [the longest x1 0.08 us: shards(): as_float = double_rows(activations, 'gy', ny).astype(jnp.float32)]
  transfers between devices with their start and end apart: 14 -> 25, of which waited for: 10 -> 16; matrix products, arithmetic and copies ran while one was open for 1% -> 2% of each run, Pallas kernels for 0% -> 13%
where the time goes in v2:
time: 79.2 us; the launch traced here: 78.9 us
  Pallas kernels  26.6 us (34%)
  starting transfers between devices  24.3 us (31%)
  waiting for transfers between devices  21.3 us (27%)
  other arithmetic  3.67 us (5%)
  matrix products  1.49 us (2%)
  local copies, waits for them, and re-layouts  1.17 us (1%)
    ppermute x25, starting transfers between devices, swap(): return lax.ppermute(x, axis, [(k, k ^ m) for k in range(n)])  24.3 us
    ppermute x25, waiting for transfers between devices, swap(): return lax.ppermute(x, axis, [(k, k ^ m) for k in range(n)])  21.3 us
    pallas_call x2, Pallas kernels, fetch(): pl.pallas_call(body, out_shape=pltpu.VMEM((rows, cols), w.dtype), in_spec...  10.5 us
    pallas_call x1, Pallas kernels, project(): pl.pallas_call(body, out_shape=jax.ShapeDtypeStruct((rows, cols + last_co...  7.38 us
    pallas_call x1, Pallas kernels, multiply_left(): pl.pallas_call(body, out_shape=[jax.ShapeDtypeStruct((rows, cut), jnp.flo...  6.67 us
    pallas_call x1, Pallas kernels, multiply_right(): pl.pallas_call(body, out_shape=jax.ShapeDtypeStruct((rows, held + extra),...  2.02 us
  transfers between devices with their start and end apart: 25, of which 16 were waited for; matrix products, arithmetic and copies ran while one was open for 2% of the time, Pallas kernels for 13%

profile of v2, /device:TPU:0, one launch (start us, length us, event | category | flops | bytes accessed | tf_op | source)
XLA Modules:
  0.0 78.9 jit_solution(2055566407924224544)
XLA Ops:
  0.0 1.2 %convert_reduce_fusion = (f32[16]{0:T(128)S(1)}, f32[16]{0:T(128)S(1)}) fusion(bf16[16,4608]{1,0:T(8,128)(2,1)} %param.8), kind=kLoop, calls=%fused_computation.17 | loop fusion | flops 294880 | bytes 147584 | tf_op jit(solution)/shard_map/reduce_sum | solution.py:262
  1.2 3.0 %collective-permute-start.2 = (f32[1,16,2]{1,2,0:T(2,128)S(1)}, f32[1,16,2]{1,2,0:T(2,128)S(1)}, u32[]{:S(2)}, u32[]{:S(2)}) collective-permute-start(f32[1,16,2]{1,2,0:T(2,128)S(1)} %maximum_bitcast_fusion.3), channel_id=1, source_target_pairs={{0,2},{1,3},{2,0},{3,1},{4,6},{5,7},{6,4},{7,5},{8,10},{9,11},{10,... | collective-permute-start | bytes 392 | tf_op jit(solution)/shard_map/ppermute | solution.py:13
  4.3 1.5 %collective-permute-done.2 = f32[1,16,2]{1,2,0:T(2,128)S(1)} collective-permute-done((f32[1,16,2]{1,2,0:T(2,128)S(1)}, f32[1,16,2]{1,2,0:T(2,128)S(1)}, u32[]{:S(2)}, u32[]{:S(2)}) %collective-permute-start.2) | collective-permute-done | bytes 160 | tf_op jit(solution)/shard_map/ppermute | solution.py:13
  7.1 2.1 %collective-permute-start.4 = (f32[64,2]{0,1:T(2,128)S(1)}, f32[64,2]{0,1:T(2,128)S(1)}, u32[]{:S(2)}, u32[]{:S(2)}) collective-permute-start(f32[64,2]{0,1:T(2,128)S(1)} %reshape.67), channel_id=1, source_target_pairs={{0,4},{4,0},{8,12},{12,8},{1,5},{5,1},{9,13},{13,9},{2,6},{6,2},{1... | collective-permute-start | bytes 1544 | tf_op jit(solution)/shard_map/ppermute | solution.py:13
  9.2 2.6 %collective-permute-start.5 = (f32[64,2]{0,1:T(2,128)S(1)}, f32[64,2]{0,1:T(2,128)S(1)}, u32[]{:S(2)}, u32[]{:S(2)}) collective-permute-start(f32[64,2]{0,1:T(2,128)S(1)} %reshape.67), channel_id=1, source_target_pairs={{0,8},{4,12},{8,0},{12,4},{1,9},{5,13},{9,1},{13,5},{2,10},{6,14},... | collective-permute-start | bytes 1544 | tf_op jit(solution)/shard_map/ppermute | solution.py:13
  11.9 4.1 %fetch.2.head_ref = bf16[4608,1152]{1,0:T(8,128)(2,1)S(1)} custom-call(bf16[4608,3072]{1,0:T(8,128)(2,1)} %all_ref.2, f32[64,2]{1,0:T(8,128)S(1)} %copy.14.after_ref), custom_call_target="tpu_custom_call" | custom-call | bytes 10616832 | tf_op jit(solution)/shard_map/fetch/pallas_call | solution.py:84
  16.2 1.0 %collective-permute-done.6 = f32[64,2]{0,1:T(2,128)S(1)} collective-permute-done((f32[64,2]{0,1:T(2,128)S(1)}, f32[64,2]{0,1:T(2,128)S(1)}, u32[]{:S(2)}, u32[]{:S(2)}) %collective-permute-start.6) | collective-permute-done | bytes 544 | tf_op jit(solution)/shard_map/ppermute | solution.py:13
  18.2 7.4 %project.1 = f32[64,3200]{1,0:T(8,128)S(1)} custom-call(bf16[64,4608]{1,0:T(8,128)(2,1)S(1)} %fusion.3.x_ref, bf16[4608,1152]{1,0:T(8,128)(2,1)S(1)} %fetch.2.head_ref, bf16[4608,3072]{1,0:T(8,128)(2,1)} %all_ref.2, bf16[4608,512]{1,0:T(8,128)(2,1)} %last_ref.1), custom_call_target="tpu_custom_call" | custom-call | flops 1811939328 | bytes 28311552 | tf_op jit(solution)/shard_map/project/pallas_call | solution.py:136
  25.6 2.0 %collective-permute-start.7 = (f16[16,3200]{1,0:T(8,128)(2,1)S(1)}, f16[16,3200]{1,0:T(8,128)(2,1)S(1)}, u32[]{:S(2)}, u32[]{:S(2)}) collective-permute-start(f16[16,3200]{1,0:T(8,128)(2,1)S(1)} %get-tuple-element.11), channel_id=1, source_target_pairs={{0,8},{4,12},{8,0},{12,4},{1,9},{5,13},{9,1},{13,5},{2,10},{6,14},... | collective-permute-start | bytes 307208 | tf_op jit(solution)/shard_map/ppermute | solution.py:13
  27.6 2.0 %collective-permute-start.8 = (f16[16,3200]{1,0:T(8,128)(2,1)S(1)}, f16[16,3200]{1,0:T(8,128)(2,1)S(1)}, u32[]{:S(2)}, u32[]{:S(2)}) collective-permute-start(f16[16,3200]{1,0:T(8,128)(2,1)S(1)} %get-tuple-element.13), channel_id=1, source_target_pairs={{0,12},{4,8},{8,4},{12,0},{1,13},{5,9},{9,5},{13,1},{2,14},{6,10},... | collective-permute-start | bytes 307208 | tf_op jit(solution)/shard_map/ppermute | solution.py:13
  30.2 6.6 %collective-permute-done.7 = f16[16,3200]{1,0:T(8,128)(2,1)S(1)} collective-permute-done((f16[16,3200]{1,0:T(8,128)(2,1)S(1)}, f16[16,3200]{1,0:T(8,128)(2,1)S(1)}, u32[]{:S(2)}, u32[]{:S(2)}) %collective-permute-start.7) | collective-permute-done | bytes 102432 | tf_op jit(solution)/shard_map/ppermute | solution.py:13
  37.5 1.8 %collective-permute-start.11 = (bf16[4,3200]{1,0:T(4,128)(2,1)S(1)}, bf16[4,3200]{1,0:T(4,128)(2,1)S(1)}, u32[]{:S(2)}, u32[]{:S(2)}) collective-permute-start(bf16[4,3200]{1,0:T(4,128)(2,1)S(1)} %get-tuple-element.26), channel_id=1, source_target_pairs={{0,2},{1,3},{2,0},{3,1},{4,6},{5,7},{6,4},{7,5},{8,10},{9,11},{10,... | collective-permute-start | bytes 76808 | tf_op jit(solution)/shard_map/ppermute | solution.py:13
  39.8 1.6 %collective-permute-done.11 = bf16[4,3200]{1,0:T(4,128)(2,1)S(1)} collective-permute-done((bf16[4,3200]{1,0:T(4,128)(2,1)S(1)}, bf16[4,3200]{1,0:T(4,128)(2,1)S(1)}, u32[]{:S(2)}, u32[]{:S(2)}) %collective-permute-start.11) | collective-permute-done | bytes 25632 | tf_op jit(solution)/shard_map/ppermute | solution.py:13
  41.4 1.1 %collective-permute-done.12 = bf16[4,3200]{1,0:T(4,128)(2,1)S(1)} collective-permute-done((bf16[4,3200]{1,0:T(4,128)(2,1)S(1)}, bf16[4,3200]{1,0:T(4,128)(2,1)S(1)}, u32[]{:S(2)}, u32[]{:S(2)}) %collective-permute-start.12) | collective-permute-done | bytes 25632 | tf_op jit(solution)/shard_map/ppermute | solution.py:13
  45.7 1.6 %collective-permute-start.15 = (bf16[4,3072]{1,0:T(4,128)(2,1)S(1)}, bf16[4,3072]{1,0:T(4,128)(2,1)S(1)}, u32[]{:S(2)}, u32[]{:S(2)}) collective-permute-start(bf16[4,3072]{1,0:T(4,128)(2,1)S(1)} %bitcast.96), channel_id=1, source_target_pairs={{0,1},{1,0},{2,3},{3,2},{4,5},{5,4},{6,7},{7,6},{8,9},{9,8},{10,11... | collective-permute-start | bytes 73736 | tf_op jit(solution)/shard_map/ppermute | solution.py:13
  47.3 1.6 %collective-permute-done.13 = bf16[4,3072]{1,0:T(4,128)(2,1)S(1)} collective-permute-done((bf16[4,3072]{1,0:T(4,128)(2,1)S(1)}, bf16[4,3072]{1,0:T(4,128)(2,1)S(1)}, u32[]{:S(2)}, u32[]{:S(2)}) %collective-permute-start.13) | collective-permute-done | bytes 24608 | tf_op jit(solution)/shard_map/ppermute | solution.py:13
  49.2 2.8 %collective-permute-start.16 = (bf16[16,3072]{1,0:T(8,128)(2,1)S(1)}, bf16[16,3072]{1,0:T(8,128)(2,1)S(1)}, u32[]{:S(2)}, u32[]{:S(2)}) collective-permute-start(bf16[16,3072]{1,0:T(8,128)(2,1)S(1)} %constant_dynamic-update-slice_fusion.4.after_ref), channel_id=1, source_target_pairs={{0,8},{4,12},{8,0},{12,4},{1,9},{5,13},{9,1},{13,5},{2,10},{6,14},... | collective-permute-start | bytes 294920 | tf_op jit(solution)/shard_map/ppermute | solution.py:13
  52.0 1.0 %collective-permute-start.17 = (bf16[16,3072]{1,0:T(8,128)(2,1)S(1)}, bf16[16,3072]{1,0:T(8,128)(2,1)S(1)}, u32[]{:S(2)}, u32[]{:S(2)}) collective-permute-start(bf16[16,3072]{1,0:T(8,128)(2,1)S(1)} %constant_dynamic-update-slice_fusion.4.after_ref), channel_id=1, source_target_pairs={{0,12},{4,8},{8,4},{12,0},{1,13},{5,9},{9,5},{13,1},{2,14},{6,10},... | collective-permute-start | bytes 294920 | tf_op jit(solution)/shard_map/ppermute | solution.py:13
  53.1 6.4 %fetch.3.held_ref = bf16[3072,3072]{1,0:T(8,128)(2,1)S(1)} custom-call(bf16[3072,4608]{1,0:T(8,128)(2,1)} %all_ref.3, bf16[16,3072]{1,0:T(8,128)(2,1)S(1)} %constant_dynamic-update-slice_fusion.4.after_ref), custom_call_target="tpu_custom_call" | custom-call | bytes 18874368 | tf_op jit(solution)/shard_map/fetch/pallas_call | solution.py:84
  60.7 6.7 %multiply_left.1 = (f32[64,2816]{1,0:T(8,128)S(1)}, bf16[3072,1536]{1,0:T(8,128)(2,1)S(1)}) custom-call(bf16[64,3072]{1,0:T(8,128)(2,1)S(1)} %constant_dynamic-update-slice_fusion.x_ref, bf16[3072,3072]{1,0:T(8,128)(2,1)S(1)} %fetch.3.held_ref, bf16[3072,4608]{1,0:T(8,128)(2,1)} %all_ref.3), custom_call_target="tpu_custom_call" | custom-call | flops 1107296256 | bytes 17301504 | tf_op jit(solution)/shard_map/multiply_left/pallas_call | solution.py:171
  67.4 2.0 %multiply_right.1 = f32[64,1792]{1,0:T(8,128)S(1)} custom-call(bf16[64,3072]{1,0:T(8,128)(2,1)S(1)} %constant_dynamic-update-slice_fusion.x_ref, bf16[3072,3072]{1,0:T(8,128)(2,1)S(1)} %fetch.3.held_ref, bf16[3072,1536]{1,0:T(8,128)(2,1)S(1)} %get-tuple-element.8.rest_ref), custom_call_target="tpu_custom_call" | custom-call | flops 704643072 | bytes 11010048 | tf_op jit(solution)/shard_map/multiply_right/pallas_call | solution.py:202
  70.1 1.5 %collective-permute-start.24 = (bf16[16,1792]{1,0:T(8,128)(2,1)S(1)}, bf16[16,1792]{1,0:T(8,128)(2,1)S(1)}, u32[]{:S(2)}, u32[]{:S(2)}) collective-permute-start(bf16[16,1792]{1,0:T(8,128)(2,1)S(1)} %get-tuple-element.20), channel_id=1, source_target_pairs={{0,1},{1,0},{2,3},{3,2},{4,5},{5,4},{6,7},{7,6},{8,9},{9,8},{10,11... | collective-permute-start | bytes 172040 | tf_op jit(solution)/shard_map/ppermute | solution.py:13
  73.1 1.1 %collective-permute-done.22 = bf16[16,1792]{1,0:T(8,128)(2,1)S(1)} collective-permute-done((bf16[16,1792]{1,0:T(8,128)(2,1)S(1)}, bf16[16,1792]{1,0:T(8,128)(2,1)S(1)}, u32[]{:S(2)}, u32[]{:S(2)}) %collective-permute-start.22) | collective-permute-done | bytes 57376 | tf_op jit(solution)/shard_map/ppermute | solution.py:13
  74.4 3.0 %collective-permute-done.19 = bf16[16,2816]{1,0:T(8,128)(2,1)S(1)} collective-permute-done((bf16[16,2816]{1,0:T(8,128)(2,1)S(1)}, bf16[16,2816]{1,0:T(8,128)(2,1)S(1)}, u32[]{:S(2)}, u32[]{:S(2)}) %collective-permute-start.19) | collective-permute-done | bytes 90144 | tf_op jit(solution)/shard_map/ppermute | solution.py:13
  (103 shorter events, 13.0 us)
Async XLA Ops:
  1.2 4.5 %collective-permute-start.2 = (f32[1,16,2]{1,2,0:T(2,128)S(1)}, f32[1,16,2]{1,2,0:T(2,128)S(1)}, u32[]{:S(2)}, u32[]{:S(2)}) collective-permute-start(f32[1,16,2]{1,2,0:T(2,128)S(1)} %maximum_bitcast_fusion.3), channel_id=1, source_target_pairs={{0,2},{1,3},{2,0},{3,1},{4,6},{5,7},{6,4},{7,5},{8,10},{9,11},{10,... | collective-permute-start | bytes 392 | tf_op jit(solution)/shard_map/ppermute | solution.py:13
  4.2 11.8 %collective-permute-start = (bf16[1,16,4608]{2,1,0:T(8,128)(2,1)}, bf16[1,16,4608]{2,1,0:T(8,128)(2,1)S(1)}, u32[]{:S(2)}, u32[]{:S(2)}) collective-permute-start(bf16[1,16,4608]{2,1,0:T(8,128)(2,1)} %bitcast.94), channel_id=1, source_target_pairs={{0,2},{1,3},{2,0},{3,1},{4,6},{5,7},{6,4},{7,5},{8,10},{9,11},{10,... | collective-permute-start | bytes 442376 | tf_op jit(solution)/shard_map/ppermute | solution.py:13
  7.1 9.0 %collective-permute-start.4 = (f32[64,2]{0,1:T(2,128)S(1)}, f32[64,2]{0,1:T(2,128)S(1)}, u32[]{:S(2)}, u32[]{:S(2)}) collective-permute-start(f32[64,2]{0,1:T(2,128)S(1)} %reshape.67), channel_id=1, source_target_pairs={{0,4},{4,0},{8,12},{12,8},{1,5},{5,1},{9,13},{13,9},{2,6},{6,2},{1... | collective-permute-start | bytes 1544 | tf_op jit(solution)/shard_map/ppermute | solution.py:13
  9.2 6.9 %collective-permute-start.5 = (f32[64,2]{0,1:T(2,128)S(1)}, f32[64,2]{0,1:T(2,128)S(1)}, u32[]{:S(2)}, u32[]{:S(2)}) collective-permute-start(f32[64,2]{0,1:T(2,128)S(1)} %reshape.67), channel_id=1, source_target_pairs={{0,8},{4,12},{8,0},{12,4},{1,9},{5,13},{9,1},{13,5},{2,10},{6,14},... | collective-permute-start | bytes 1544 | tf_op jit(solution)/shard_map/ppermute | solution.py:13
  11.8 5.4 %collective-permute-start.6 = (f32[64,2]{0,1:T(2,128)S(1)}, f32[64,2]{0,1:T(2,128)S(1)}, u32[]{:S(2)}, u32[]{:S(2)}) collective-permute-start(f32[64,2]{0,1:T(2,128)S(1)} %reshape.67), channel_id=1, source_target_pairs={{0,12},{4,8},{8,4},{12,0},{1,13},{5,9},{9,5},{13,1},{2,14},{6,10},... | collective-permute-start | bytes 1544 | tf_op jit(solution)/shard_map/ppermute | solution.py:13
  16.1 1.6 %collective-permute-start.1 = (bf16[2,16,4608]{2,1,0:T(8,128)(2,1)S(1)}, bf16[2,16,4608]{2,1,0:T(8,128)(2,1)S(1)}, u32[]{:S(2)}, u32[]{:S(2)}) collective-permute-start(bf16[2,16,4608]{2,1,0:T(8,128)(2,1)S(1)} %maximum_bitcast_fusion), channel_id=1, source_target_pairs={{0,1},{1,0},{2,3},{3,2},{4,5},{5,4},{6,7},{7,6},{8,9},{9,8},{10,11... | collective-permute-start | bytes 884744 | tf_op jit(solution)/shard_map/ppermute | solution.py:13
  25.6 11.1 %collective-permute-start.7 = (f16[16,3200]{1,0:T(8,128)(2,1)S(1)}, f16[16,3200]{1,0:T(8,128)(2,1)S(1)}, u32[]{:S(2)}, u32[]{:S(2)}) collective-permute-start(f16[16,3200]{1,0:T(8,128)(2,1)S(1)} %get-tuple-element.11), channel_id=1, source_target_pairs={{0,8},{4,12},{8,0},{12,4},{1,9},{5,13},{9,1},{13,5},{2,10},{6,14},... | collective-permute-start | bytes 307208 | tf_op jit(solution)/shard_map/ppermute | solution.py:13
  27.6 9.2 %collective-permute-start.8 = (f16[16,3200]{1,0:T(8,128)(2,1)S(1)}, f16[16,3200]{1,0:T(8,128)(2,1)S(1)}, u32[]{:S(2)}, u32[]{:S(2)}) collective-permute-start(f16[16,3200]{1,0:T(8,128)(2,1)S(1)} %get-tuple-element.13), channel_id=1, source_target_pairs={{0,12},{4,8},{8,4},{12,0},{1,13},{5,9},{9,5},{13,1},{2,14},{6,10},... | collective-permute-start | bytes 307208 | tf_op jit(solution)/shard_map/ppermute | solution.py:13
  29.6 7.8 %collective-permute-start.9 = (f16[16,3200]{1,0:T(8,128)(2,1)S(1)}, f16[16,3200]{1,0:T(8,128)(2,1)S(1)}, u32[]{:S(2)}, u32[]{:S(2)}) collective-permute-start(f16[16,3200]{1,0:T(8,128)(2,1)S(1)} %get-tuple-element.12), channel_id=1, source_target_pairs={{0,4},{4,0},{8,12},{12,8},{1,5},{5,1},{9,13},{13,9},{2,6},{6,2},{1... | collective-permute-start | bytes 307208 | tf_op jit(solution)/shard_map/ppermute | solution.py:13
  37.5 3.9 %collective-permute-start.11 = (bf16[4,3200]{1,0:T(4,128)(2,1)S(1)}, bf16[4,3200]{1,0:T(4,128)(2,1)S(1)}, u32[]{:S(2)}, u32[]{:S(2)}) collective-permute-start(bf16[4,3200]{1,0:T(4,128)(2,1)S(1)} %get-tuple-element.26), channel_id=1, source_target_pairs={{0,2},{1,3},{2,0},{3,1},{4,6},{5,7},{6,4},{7,5},{8,10},{9,11},{10,... | collective-permute-start | bytes 76808 | tf_op jit(solution)/shard_map/ppermute | solution.py:13
  39.3 3.3 %collective-permute-start.12 = (bf16[4,3200]{1,0:T(4,128)(2,1)S(1)}, bf16[4,3200]{1,0:T(4,128)(2,1)S(1)}, u32[]{:S(2)}, u32[]{:S(2)}) collective-permute-start(bf16[4,3200]{1,0:T(4,128)(2,1)S(1)} %get-tuple-element.25), channel_id=1, source_target_pairs={{0,3},{1,2},{2,1},{3,0},{4,7},{5,6},{6,5},{7,4},{8,11},{9,10},{10,... | collective-permute-start | bytes 76808 | tf_op jit(solution)/shard_map/ppermute | solution.py:13
  39.3 3.3 %collective-permute-start.10 = (bf16[4,3200]{1,0:T(4,128)(2,1)S(1)}, bf16[4,3200]{1,0:T(4,128)(2,1)S(1)}, u32[]{:S(2)}, u32[]{:S(2)}) collective-permute-start(bf16[4,3200]{1,0:T(4,128)(2,1)S(1)} %get-tuple-element.24), channel_id=1, source_target_pairs={{0,1},{1,0},{2,3},{3,2},{4,5},{5,4},{6,7},{7,6},{8,9},{9,8},{10,11... | collective-permute-start | bytes 76808 | tf_op jit(solution)/shard_map/ppermute | solution.py:13
  44.9 4.0 %collective-permute-start.13 = (bf16[4,3072]{1,0:T(4,128)(2,1)S(1)}, bf16[4,3072]{1,0:T(4,128)(2,1)S(1)}, u32[]{:S(2)}, u32[]{:S(2)}) collective-permute-start(bf16[4,3072]{1,0:T(4,128)(2,1)S(1)} %bitcast.98), channel_id=1, source_target_pairs={{0,2},{1,3},{2,0},{3,1},{4,6},{5,7},{6,4},{7,5},{8,10},{9,11},{10,... | collective-permute-start | bytes 73736 | tf_op jit(solution)/shard_map/ppermute | solution.py:13
  45.6 3.6 %collective-permute-start.14 = (bf16[4,3072]{1,0:T(4,128)(2,1)S(1)}, bf16[4,3072]{1,0:T(4,128)(2,1)S(1)}, u32[]{:S(2)}, u32[]{:S(2)}) collective-permute-start(bf16[4,3072]{1,0:T(4,128)(2,1)S(1)} %bitcast.97), channel_id=1, source_target_pairs={{0,3},{1,2},{2,1},{3,0},{4,7},{5,6},{6,5},{7,4},{8,11},{9,10},{10,... | collective-permute-start | bytes 73736 | tf_op jit(solution)/shard_map/ppermute | solution.py:13
  45.7 3.5 %collective-permute-start.15 = (bf16[4,3072]{1,0:T(4,128)(2,1)S(1)}, bf16[4,3072]{1,0:T(4,128)(2,1)S(1)}, u32[]{:S(2)}, u32[]{:S(2)}) collective-permute-start(bf16[4,3072]{1,0:T(4,128)(2,1)S(1)} %bitcast.96), channel_id=1, source_target_pairs={{0,1},{1,0},{2,3},{3,2},{4,5},{5,4},{6,7},{7,6},{8,9},{9,8},{10,11... | collective-permute-start | bytes 73736 | tf_op jit(solution)/shard_map/ppermute | solution.py:13
  49.2 10.8 %collective-permute-start.16 = (bf16[16,3072]{1,0:T(8,128)(2,1)S(1)}, bf16[16,3072]{1,0:T(8,128)(2,1)S(1)}, u32[]{:S(2)}, u32[]{:S(2)}) collective-permute-start(bf16[16,3072]{1,0:T(8,128)(2,1)S(1)} %constant_dynamic-update-slice_fusion.4.after_ref), channel_id=1, source_target_pairs={{0,8},{4,12},{8,0},{12,4},{1,9},{5,13},{9,1},{13,5},{2,10},{6,14},... | collective-permute-start | bytes 294920 | tf_op jit(solution)/shard_map/ppermute | solution.py:13
  52.0 8.1 %collective-permute-start.17 = (bf16[16,3072]{1,0:T(8,128)(2,1)S(1)}, bf16[16,3072]{1,0:T(8,128)(2,1)S(1)}, u32[]{:S(2)}, u32[]{:S(2)}) collective-permute-start(bf16[16,3072]{1,0:T(8,128)(2,1)S(1)} %constant_dynamic-update-slice_fusion.4.after_ref), channel_id=1, source_target_pairs={{0,12},{4,8},{8,4},{12,0},{1,13},{5,9},{9,5},{13,1},{2,14},{6,10},... | collective-permute-start | bytes 294920 | tf_op jit(solution)/shard_map/ppermute | solution.py:13
  53.0 7.6 %collective-permute-start.18 = (bf16[16,3072]{1,0:T(8,128)(2,1)S(1)}, bf16[16,3072]{1,0:T(8,128)(2,1)S(1)}, u32[]{:S(2)}, u32[]{:S(2)}) collective-permute-start(bf16[16,3072]{1,0:T(8,128)(2,1)S(1)} %constant_dynamic-update-slice_fusion.4.after_ref), channel_id=1, source_target_pairs={{0,4},{4,0},{8,12},{12,8},{1,5},{5,1},{9,13},{13,9},{2,6},{6,2},{1... | collective-permute-start | bytes 294920 | tf_op jit(solution)/shard_map/ppermute | solution.py:13
  69.4 4.8 %collective-permute-start.22 = (bf16[16,1792]{1,0:T(8,128)(2,1)S(1)}, bf16[16,1792]{1,0:T(8,128)(2,1)S(1)}, u32[]{:S(2)}, u32[]{:S(2)}) collective-permute-start(bf16[16,1792]{1,0:T(8,128)(2,1)S(1)} %get-tuple-element.19), channel_id=1, source_target_pairs={{0,2},{1,3},{2,0},{3,1},{4,6},{5,7},{6,4},{7,5},{8,10},{9,11},{10,... | collective-permute-start | bytes 172040 | tf_op jit(solution)/shard_map/ppermute | solution.py:13
  70.1 4.2 %collective-permute-start.23 = (bf16[16,1792]{1,0:T(8,128)(2,1)S(1)}, bf16[16,1792]{1,0:T(8,128)(2,1)S(1)}, u32[]{:S(2)}, u32[]{:S(2)}) collective-permute-start(bf16[16,1792]{1,0:T(8,128)(2,1)S(1)} %get-tuple-element.21), channel_id=1, source_target_pairs={{0,3},{1,2},{2,1},{3,0},{4,7},{5,6},{6,5},{7,4},{8,11},{9,10},{10,... | collective-permute-start | bytes 172040 | tf_op jit(solution)/shard_map/ppermute | solution.py:13
  70.1 4.2 %collective-permute-start.24 = (bf16[16,1792]{1,0:T(8,128)(2,1)S(1)}, bf16[16,1792]{1,0:T(8,128)(2,1)S(1)}, u32[]{:S(2)}, u32[]{:S(2)}) collective-permute-start(bf16[16,1792]{1,0:T(8,128)(2,1)S(1)} %get-tuple-element.20), channel_id=1, source_target_pairs={{0,1},{1,0},{2,3},{3,2},{4,5},{5,4},{6,7},{7,6},{8,9},{9,8},{10,11... | collective-permute-start | bytes 172040 | tf_op jit(solution)/shard_map/ppermute | solution.py:13
  71.7 5.7 %collective-permute-start.19 = (bf16[16,2816]{1,0:T(8,128)(2,1)S(1)}, bf16[16,2816]{1,0:T(8,128)(2,1)S(1)}, u32[]{:S(2)}, u32[]{:S(2)}) collective-permute-start(bf16[16,2816]{1,0:T(8,128)(2,1)S(1)} %get-tuple-element.14), channel_id=1, source_target_pairs={{0,2},{1,3},{2,0},{3,1},{4,6},{5,7},{6,4},{7,5},{8,10},{9,11},{10,... | collective-permute-start | bytes 270344 | tf_op jit(solution)/shard_map/ppermute | solution.py:13
  72.4 5.8 %collective-permute-start.20 = (bf16[16,2816]{1,0:T(8,128)(2,1)S(1)}, bf16[16,2816]{1,0:T(8,128)(2,1)S(1)}, u32[]{:S(2)}, u32[]{:S(2)}) collective-permute-start(bf16[16,2816]{1,0:T(8,128)(2,1)S(1)} %get-tuple-element.16), channel_id=1, source_target_pairs={{0,3},{1,2},{2,1},{3,0},{4,7},{5,6},{6,5},{7,4},{8,11},{9,10},{10,... | collective-permute-start | bytes 270344 | tf_op jit(solution)/shard_map/ppermute | solution.py:13
  74.2 4.0 %collective-permute-start.21 = (bf16[16,2816]{1,0:T(8,128)(2,1)S(1)}, bf16[16,2816]{1,0:T(8,128)(2,1)S(1)}, u32[]{:S(2)}, u32[]{:S(2)}) collective-permute-start(bf16[16,2816]{1,0:T(8,128)(2,1)S(1)} %get-tuple-element.15), channel_id=1, source_target_pairs={{0,1},{1,0},{2,3},{3,2},{4,5},{5,4},{6,7},{7,6},{8,9},{9,8},{10,11... | collective-permute-start | bytes 270344 | tf_op jit(solution)/shard_map/ppermute | solution.py:13
  (6 other events, 73.3 us)

commit v3 on v2

--- a/solution.py
+++ b/solution.py
@@ -36,6 +36,14 @@
     return total
 
 
+def to_bfloat16(x):
+    return x.astype(jnp.bfloat16)
+
+
+def to_float32(x):
+    return x.astype(jnp.float32)
+
+
 def in_order(parts, axis):
     me = lax.axis_index(axis)
     size = parts[0].shape[0]
@@ -49,7 +57,7 @@
     return in_order(exchange([x] * n, axis, n), axis)
 
 
-def double_rows(x, axis, n):
+def double_rows(x, axis, n, steps):
     me = lax.axis_index(axis)
     size = x.shape[0]
     held = x[None]
@@ -59,6 +67,7 @@
         low = (me & bit) == 0
         held = jnp.stack([jnp.where(low, held, other), jnp.where(low, other, held)])
         held = held.reshape((-1,) + x.shape)
+        steps.append(held)
         bit //= 2
     bits = n.bit_length() - 1
     held = held.reshape((2,) * bits + x.shape)
@@ -74,25 +83,52 @@
     return jnp.dot(x, w, preferred_element_type=jnp.float32)
 
 
-def fetch(w, start, cols, after):
-    def body(w_ref, after_ref, out_ref, sem):
+def row_sums(x):
+    def body(x_ref, sums_ref, out_ref):
+        value = x_ref[...]
+        out_ref[...] = value
+        value = value.astype(jnp.float32)
+        sums_ref[:, 0:1] = jnp.sum(value, axis=1, keepdims=True)
+        sums_ref[:, 1:2] = jnp.sum(value * value, axis=1, keepdims=True)
+
+    return pl.pallas_call(
+        body,
+        out_shape=[
+            jax.ShapeDtypeStruct((x.shape[0], 2), jnp.float32),
+            jax.ShapeDtypeStruct(x.shape, x.dtype),
+        ],
+        in_specs=[in_vmem()],
+        out_specs=[in_vmem()] * 2,
+        compiler_params=pltpu.CompilerParams(vmem_limit_bytes=8 << 20),
+        name="row_sums",
+    )(x)
+
+
+def fetch(w, start, cols, passed, *after):
+    def body(w_ref, passed_ref, *refs):
+        out_ref, passed_out, sem = refs[len(after) :]
         copy = pltpu.make_async_copy(w_ref.at[:, pl.ds(start, cols)], out_ref, sem)
         copy.start()
+        passed_out[...] = passed_ref[...]
         copy.wait()
 
     rows = w.shape[0]
     return pl.pallas_call(
         body,
-        out_shape=pltpu.VMEM((rows, cols), w.dtype),
-        in_specs=[pl.BlockSpec(memory_space=pltpu.HBM), pl.BlockSpec(memory_space=pl.ANY)],
-        out_specs=in_vmem(),
+        out_shape=[
+            pltpu.VMEM((rows, cols), w.dtype),
+            pltpu.VMEM(passed.shape, passed.dtype),
+        ],
+        in_specs=[pl.BlockSpec(memory_space=pltpu.HBM), in_vmem()]
+        + [pl.BlockSpec(memory_space=pl.ANY)] * len(after),
+        out_specs=[in_vmem(), in_vmem()],
         scratch_shapes=[pltpu.SemaphoreType.DMA],
         compiler_params=pltpu.CompilerParams(vmem_limit_bytes=1 << 20),
         cost_estimate=pl.CostEstimate(
             flops=0, bytes_accessed=2 * rows * cols, transcendentals=0
         ),
         name="fetch",
-    )(pltpu.with_memory_space_constraint(w, pltpu.HBM), after)
+    )(pltpu.with_memory_space_constraint(w, pltpu.HBM), passed, *after)
 
 
 def tiles(cols, size=512):
@@ -156,66 +192,78 @@
     )
 
 
-def multiply_left(x, w_held, w_all, cut):
-    depth, cols = w_all.shape
-    held = w_held.shape[1]
-
-    def body(x_ref, held_ref, all_ref, out_ref, rest_ref, sem):
-        copy = pltpu.make_async_copy(all_ref.at[:, pl.ds(held, cols - held)], rest_ref, sem)
-        copy.start()
-        for c, size in tiles(cut):
-            out_ref[:, c : c + size] = dot_f32(x_ref[...], held_ref[:, c : c + size])
-        copy.wait()
-
-    rows = x.shape[0]
-    return pl.pallas_call(
-        body,
-        out_shape=[
-            jax.ShapeDtypeStruct((rows, cut), jnp.float32),
-            pltpu.VMEM((depth, cols - held), w_all.dtype),
+def shares(total_ref, out_refs, axis, n):
+    me = lax.axis_index(axis)
+    rows = total_ref.shape[0] // n
+    for m, out_ref in enumerate(out_refs):
+        block = total_ref[pl.ds(pl.multiple_of((me ^ m) * rows, rows), rows), :]
+        out_ref[...] = block.astype(out_ref.dtype)
+
+
+def share_shapes(rows, cols, n):
+    kept = jax.ShapeDtypeStruct((rows // n, cols), jnp.float32)
+    return [kept] + [pltpu.VMEM((rows // n, cols), jnp.bfloat16)] * (n - 1)
+
+
+def multiply_held(x, w, axis, n):
+    rows, depth, cols = x.shape[0], x.shape[1], w.shape[1]
+
+    def body(x_ref, w_ref, *refs):
+        total = refs[-1]
+        for c, size in tiles(cols):
+            total[:, c : c + size] = dot_f32(x_ref[...], w_ref[:, c : c + size])
+        shares(total, refs[:-1], axis, n)
+
+    return pl.pallas_call(
+        body,
+        out_shape=share_shapes(rows, cols, n),
+        in_specs=[in_vmem(), in_vmem()],
+        out_specs=[in_vmem()] * n,
+        scratch_shapes=[pltpu.VMEM((rows, cols), jnp.float32)],
+        compiler_params=pltpu.CompilerParams(vmem_limit_bytes=8 << 20),
+        cost_estimate=pl.CostEstimate(
+            flops=2 * rows * depth * cols, bytes_accessed=2 * depth * cols, transcendentals=0
+        ),
+        name="multiply_held",
+    )(x, pltpu.with_memory_space_constraint(w, pltpu.VMEM))
+
+
+def multiply_streamed(x, w, start, axis, n):
+    rows, depth = x.shape
+    cols = w.shape[1] - start
+    parts = tiles(cols, 384)
+
+    def body(x_ref, w_ref, *refs):
+        total, scratch, sems = refs[-3:]
+        copies = [
+            pltpu.make_async_copy(
+                w_ref.at[:, pl.ds(start + c, size)], scratch.at[:, pl.ds(c, size)], sems.at[i]
+            )
+            for i, (c, size) in enumerate(parts)
+        ]
+        for copy in copies:
+            copy.start()
+        for copy, (c, size) in zip(copies, parts):
+            copy.wait()
+            total[:, c : c + size] = dot_f32(x_ref[...], scratch[:, c : c + size])
+        shares(total, refs[:-3], axis, n)
+
+    return pl.pallas_call(
+        body,
+        out_shape=share_shapes(rows, cols, n),
+        in_specs=[in_vmem(), pl.BlockSpec(memory_space=pltpu.HBM)],
+        out_specs=[in_vmem()] * n,
+        scratch_shapes=[
+            pltpu.VMEM((rows, cols), jnp.float32),
+            pltpu.VMEM((depth, cols), w.dtype),
+            pltpu.SemaphoreType.DMA((len(parts),)),
         ],
-        in_specs=[in_vmem(), in_vmem(), pl.BlockSpec(memory_space=pltpu.HBM)],
-        out_specs=[in_vmem(), in_vmem()],
-        scratch_shapes=[pltpu.SemaphoreType.DMA],
-        compiler_params=pltpu.CompilerParams(vmem_limit_bytes=4 << 20),
+        compiler_params=pltpu.CompilerParams(vmem_limit_bytes=16 << 20),
         cost_estimate=pl.CostEstimate(
-            flops=2 * rows * depth * cut, bytes_accessed=2 * depth * cut, transcendentals=0
+            flops=2 * rows * depth * cols, bytes_accessed=2 * depth * cols, transcendentals=0
         ),
-        name="multiply_left",
-    )(
-        x,
-        pltpu.with_memory_space_constraint(w_held, pltpu.VMEM),
-        pltpu.with_memory_space_constraint(w_all, pltpu.HBM),
-    )
-
-
-def multiply_right(x, w_held, w_rest, cut):
-    held, extra = w_held.shape[1] - cut, w_rest.shape[1]
-
-    def body(x_ref, held_ref, rest_ref, out_ref):
-        for c, size in tiles(held):
-            out_ref[:, c : c + size] = dot_f32(x_ref[...], held_ref[:, cut + c : cut + c + size])
-        for c, size in tiles(extra):
-            out_ref[:, held + c : held + c + size] = dot_f32(x_ref[...], rest_ref[:, c : c + size])
-
-    rows, depth = x.shape
-    return pl.pallas_call(
-        body,
-        out_shape=jax.ShapeDtypeStruct((rows, held + extra), jnp.float32),
-        in_specs=[in_vmem()] * 3,
-        out_specs=in_vmem(),
-        compiler_params=pltpu.CompilerParams(vmem_limit_bytes=4 << 20),
-        cost_estimate=pl.CostEstimate(
-            flops=2 * rows * depth * (held + extra),
-            bytes_accessed=2 * depth * (held + extra),
-            transcendentals=0,
-        ),
-        name="multiply_right",
-    )(
-        x,
-        pltpu.with_memory_space_constraint(w_held, pltpu.VMEM),
-        pltpu.with_memory_space_constraint(w_rest, pltpu.VMEM),
-    )
+        name="multiply_streamed",
+    )(x, pltpu.with_memory_space_constraint(w, pltpu.HBM))
 
 
 def attend_local(query_heads, new_key, new_value, k_cache, v_cache, cache_lengths):
@@ -258,13 +306,18 @@
         gy = lax.axis_index("gy")
         head_dim = k_cache.shape[2]
         seqs = k_cache.shape[0]
-        own = activations.astype(jnp.float32)
-        sums = jnp.stack([jnp.sum(own, axis=1), jnp.sum(own * own, axis=1)], axis=1)
-        partial_moments = double_rows(sums, "gy", ny)
-        moments = partial_moments
-        as_float = double_rows(activations, "gy", ny).astype(jnp.float32)
-        for part in exchange([moments] * nx, "gx", nx)[1:]:
-            moments = moments + part
+        sums, own = row_sums(activations)
+        partial_moments = double_rows(sums, "gy", ny, [])
+        steps = []
+        as_float = double_rows(own, "gy", ny, steps).astype(jnp.float32)
+        q_cols = w_query.shape[1]
+        w_head, moments = fetch(
+            w_query, 0, whole_tiles(q_cols * 3 // 8), partial_moments, steps[0]
+        )
+        others, moments = lax.optimization_barrier(
+            (exchange([partial_moments] * nx, "gx", nx)[1:], moments)
+        )
+        moments = sum(others, moments)
         row_mean = moments[:, 0] / D
         row_var = moments[:, 1] / D - row_mean * row_mean
         normed = (
@@ -273,8 +326,6 @@
             * ln_gain.astype(jnp.float32)
         ).astype(jnp.bfloat16)
         kv_cols = w_keyval.shape[1] // ny
-        q_cols = w_query.shape[1]
-        w_head = fetch(w_query, 0, whole_tiles(q_cols * 3 // 8), partial_moments)
         projected = project(normed, w_head, w_query, w_keyval, kv_cols, "gy")
         part = reduce_rows(projected, "gx", nx, to_wire, from_wire).astype(jnp.bfloat16)
         mixed = exchange([rows_of(part, gy ^ m, ny) for m in range(ny)], "gy", ny)
@@ -295,23 +346,15 @@
             ),
             "gy",
         )
-        width = w_out.shape[1]
-        cut = whole_tiles(width * 5 // 8)
-        w_held = fetch(w_out, 0, whole_tiles(width * 2 // 3), returned)
-        everyone = gather_rows(returned, "gx", nx)
-        left, w_rest = multiply_left(everyone, w_held, w_out, cut)
-        right = multiply_right(everyone, w_held, w_rest, cut)
-        outs = [
-            reduce_rows(
-                x,
-                "gy",
-                ny,
-                lambda x: x.astype(jnp.bfloat16),
-                lambda x: x.astype(jnp.float32),
-            ).astype(jnp.bfloat16)
-            for x in (left, right)
-        ]
-        return jnp.concatenate(outs, axis=1)
+        cut = whole_tiles(w_out.shape[1] * 3 // 4)
+        w_left, own = fetch(w_out, 0, cut, returned)
+        everyone = in_order([own] + exchange([returned] * nx, "gx", nx)[1:], "gx")
+        left = exchange(multiply_held(everyone, w_left, "gy", ny), "gy", ny)
+        right = multiply_streamed(everyone, w_out, cut, "gy", ny)
+        right, left[ny // 2] = lax.optimization_barrier((right, left[ny // 2]))
+        right = exchange(right, "gy", ny)
+        outs = [sum((to_float32(x) for x in parts[1:]), parts[0]) for parts in (left, right)]
+        return jnp.concatenate([to_bfloat16(x) for x in outs], axis=1)
 
     return shards
 

time: 79.2 us -> 75.2 us (0.949)
  waiting for transfers between devices: 21.3 us -> 18 us
  other arithmetic: 3.67 us -> 2.63 us
  local copies, waits for them, and re-layouts: 1.17 us -> 2.17 us
    ppermute x25, waiting for transfers between devices: 21.3 us -> 18 us  [swap(): return lax.ppermute(x, axis, [(k, k ^ m) for k in range(n)])]
    reduce_sum x1 -> x0, other arithmetic: 1.21 us -> none  [shards(): sums = jnp.stack([jnp.sum(own, axis=1), jnp.sum(own * own, axis=1)], axis=1)]
    unnamed x15, local copies, waits for them, and re-layouts: 0.38 us -> 1.43 us
    pallas_call x4 -> x5, Pallas kernels: 19.2 us -> 19 us  [the longest x2 11.2 us: fetch(): pl.pallas_call(body, out_shape=[pltpu.VMEM((rows, cols), w.dtype), pltpu....]
  transfers between devices with their start and end apart: 25 -> 25, of which waited for: 16 -> 12; matrix products, arithmetic and copies ran while one was open for 2% -> 2% of each run, Pallas kernels for 13% -> 20%
where the time goes in v3:
time: 75.2 us; the launch traced here: 75 us
  Pallas kernels  26.4 us (35%)
  starting transfers between devices  23.8 us (32%)
  waiting for transfers between devices  18 us (24%)
  other arithmetic  2.63 us (3%)
  local copies, waits for them, and re-layouts  2.17 us (3%)
  matrix products  1.49 us (2%)
    ppermute x25, starting transfers between devices, swap(): return lax.ppermute(x, axis, [(k, k ^ m) for k in range(n)])  23.8 us
    ppermute x25, waiting for transfers between devices, swap(): return lax.ppermute(x, axis, [(k, k ^ m) for k in range(n)])  18 us
    pallas_call x2, Pallas kernels, fetch(): pl.pallas_call(body, out_shape=[pltpu.VMEM((rows, cols), w.dtype), pltpu....  11.2 us
    pallas_call x1, Pallas kernels, project(): pl.pallas_call(body, out_shape=jax.ShapeDtypeStruct((rows, cols + last_co...  7.37 us
    pallas_call x1, Pallas kernels, multiply_streamed(): pl.pallas_call(body, out_shape=share_shapes(rows, cols, n), in_specs=[in_...  3.91 us
    pallas_call x1, Pallas kernels, multiply_held(): pl.pallas_call(body, out_shape=share_shapes(rows, cols, n), in_specs=[in_...  3.79 us
  transfers between devices with their start and end apart: 25, of which 12 were waited for; matrix products, arithmetic and copies ran while one was open for 2% of the time, Pallas kernels for 20%

profile of v3, /device:TPU:0, one launch (start us, length us, event | category | flops | bytes accessed | tf_op | source)
XLA Modules:
  0.0 75.0 jit_solution(8795023403136408523)
XLA Ops:
  0.0 1.1 %copy-done.2 = bf16[16,4608]{1,0:T(8,128)(2,1)S(1)} copy-done((bf16[16,4608]{1,0:T(8,128)(2,1)S(1)}, bf16[16,4608]{1,0:T(8,128)(2,1)}, u32[]{:S(2)}) %copy-start.2) | copy-done | bytes 147480
  1.3 2.9 %collective-permute-start.2 = (f32[1,16,2]{1,2,0:T(2,128)S(1)}, f32[1,16,2]{1,2,0:T(2,128)S(1)}, u32[]{:S(2)}, u32[]{:S(2)}) collective-permute-start(f32[1,16,2]{1,2,0:T(2,128)S(1)} %bitcast.98), channel_id=1, source_target_pairs={{0,2},{1,3},{2,0},{3,1},{4,6},{5,7},{6,4},{7,5},{8,10},{9,11},{10,... | collective-permute-start | bytes 392 | tf_op jit(solution)/shard_map/ppermute | solution.py:13
  4.3 1.5 %collective-permute-done.2 = f32[1,16,2]{1,2,0:T(2,128)S(1)} collective-permute-done((f32[1,16,2]{1,2,0:T(2,128)S(1)}, f32[1,16,2]{1,2,0:T(2,128)S(1)}, u32[]{:S(2)}, u32[]{:S(2)}) %collective-permute-start.2) | collective-permute-done | bytes 160 | tf_op jit(solution)/shard_map/ppermute | solution.py:13
  7.1 2.1 %collective-permute-start.4 = (f32[64,2]{1,0:T(8,128)S(1)}, f32[64,2]{1,0:T(8,128)S(1)}, u32[]{:S(2)}, u32[]{:S(2)}) collective-permute-start(f32[64,2]{1,0:T(8,128)S(1)} %bitcast.87), channel_id=1, source_target_pairs={{0,4},{4,0},{8,12},{12,8},{1,5},{5,1},{9,13},{13,9},{2,6},{6,2},{1... | collective-permute-start | bytes 1544 | tf_op jit(solution)/shard_map/ppermute | solution.py:13
  9.2 2.6 %collective-permute-start.5 = (f32[64,2]{1,0:T(8,128)S(1)}, f32[64,2]{1,0:T(8,128)S(1)}, u32[]{:S(2)}, u32[]{:S(2)}) collective-permute-start(f32[64,2]{1,0:T(8,128)S(1)} %bitcast.88), channel_id=1, source_target_pairs={{0,8},{4,12},{8,0},{12,4},{1,9},{5,13},{9,1},{13,5},{2,10},{6,14},... | collective-permute-start | bytes 1544 | tf_op jit(solution)/shard_map/ppermute | solution.py:13
  12.0 4.0 %fetch.2 = (bf16[4608,1152]{1,0:T(8,128)(2,1)S(1)}, f32[64,2]{1,0:T(8,128)S(1)}) custom-call(bf16[4608,3072]{1,0:T(8,128)(2,1)} %all_ref.1, f32[64,2]{1,0:T(8,128)S(1)} %bitcast.90, bf16[2,16,4608]{2,1,0:T(8,128)(2,1)S(1)} %maximum_bitcast_fusion.refs_0_), custom_call_target="tpu_custom_call" | custom-call | bytes 10616832 | tf_op jit(solution)/shard_map/fetch/pallas_call | solution.py:116
  16.0 1.5 %collective-permute-done.6 = f32[64,2]{1,0:T(8,128)S(1)} collective-permute-done((f32[64,2]{1,0:T(8,128)S(1)}, f32[64,2]{1,0:T(8,128)S(1)}, u32[]{:S(2)}, u32[]{:S(2)}) %collective-permute-start.6) | collective-permute-done | bytes 544 | tf_op jit(solution)/shard_map/ppermute | solution.py:13
  18.2 7.4 %project.1 = f32[64,3200]{1,0:T(8,128)S(1)} custom-call(bf16[64,4608]{1,0:T(8,128)(2,1)S(1)} %fusion.3.x_ref, bf16[4608,1152]{1,0:T(8,128)(2,1)S(1)} %get-tuple-element.35.head_ref, bf16[4608,3072]{1,0:T(8,128)(2,1)} %all_ref.1, bf16[4608,512]{1,0:T(8,128)(2,1)} %last_ref.1), custom_call_target="tpu_custom_call" | custom-call | flops 1811939328 | bytes 28311552 | tf_op jit(solution)/shard_map/project/pallas_call | solution.py:172
  26.2 2.0 %collective-permute-start.8 = (f16[16,3200]{1,0:T(8,128)(2,1)S(1)}, f16[16,3200]{1,0:T(8,128)(2,1)S(1)}, u32[]{:S(2)}, u32[]{:S(2)}) collective-permute-start(f16[16,3200]{1,0:T(8,128)(2,1)S(1)} %get-tuple-element.55), channel_id=1, source_target_pairs={{0,12},{4,8},{8,4},{12,0},{1,13},{5,9},{9,5},{13,1},{2,14},{6,10},... | collective-permute-start | bytes 307208 | tf_op jit(solution)/shard_map/ppermute | solution.py:13
  28.1 1.1 %collective-permute-start.9 = (f16[16,3200]{1,0:T(8,128)(2,1)S(1)}, f16[16,3200]{1,0:T(8,128)(2,1)S(1)}, u32[]{:S(2)}, u32[]{:S(2)}) collective-permute-start(f16[16,3200]{1,0:T(8,128)(2,1)S(1)} %get-tuple-element.54), channel_id=1, source_target_pairs={{0,4},{4,0},{8,12},{12,8},{1,5},{5,1},{9,13},{13,9},{2,6},{6,2},{1... | collective-permute-start | bytes 307208 | tf_op jit(solution)/shard_map/ppermute | solution.py:13
  29.3 6.7 %collective-permute-done.7 = f16[16,3200]{1,0:T(8,128)(2,1)S(1)} collective-permute-done((f16[16,3200]{1,0:T(8,128)(2,1)S(1)}, f16[16,3200]{1,0:T(8,128)(2,1)S(1)}, u32[]{:S(2)}, u32[]{:S(2)}) %collective-permute-start.7) | collective-permute-done | bytes 102432 | tf_op jit(solution)/shard_map/ppermute | solution.py:13
  36.5 1.7 %collective-permute-start.11 = (bf16[4,3200]{1,0:T(4,128)(2,1)S(1)}, bf16[4,3200]{1,0:T(4,128)(2,1)S(1)}, u32[]{:S(2)}, u32[]{:S(2)}) collective-permute-start(bf16[4,3200]{1,0:T(4,128)(2,1)S(1)} %get-tuple-element.62), channel_id=1, source_target_pairs={{0,2},{1,3},{2,0},{3,1},{4,6},{5,7},{6,4},{7,5},{8,10},{9,11},{10,... | collective-permute-start | bytes 76808 | tf_op jit(solution)/shard_map/ppermute | solution.py:13
  38.9 1.6 %collective-permute-done.11 = bf16[4,3200]{1,0:T(4,128)(2,1)S(1)} collective-permute-done((bf16[4,3200]{1,0:T(4,128)(2,1)S(1)}, bf16[4,3200]{1,0:T(4,128)(2,1)S(1)}, u32[]{:S(2)}, u32[]{:S(2)}) %collective-permute-start.11) | collective-permute-done | bytes 25632 | tf_op jit(solution)/shard_map/ppermute | solution.py:13
  40.4 1.0 %collective-permute-done.12 = bf16[4,3200]{1,0:T(4,128)(2,1)S(1)} collective-permute-done((bf16[4,3200]{1,0:T(4,128)(2,1)S(1)}, bf16[4,3200]{1,0:T(4,128)(2,1)S(1)}, u32[]{:S(2)}, u32[]{:S(2)}) %collective-permute-start.12) | collective-permute-done | bytes 25632 | tf_op jit(solution)/shard_map/ppermute | solution.py:13
  44.7 1.5 %collective-permute-start.15 = (bf16[4,3072]{1,0:T(4,128)(2,1)S(1)}, bf16[4,3072]{1,0:T(4,128)(2,1)S(1)}, u32[]{:S(2)}, u32[]{:S(2)}) collective-permute-start(bf16[4,3072]{1,0:T(4,128)(2,1)S(1)} %bitcast.92), channel_id=1, source_target_pairs={{0,1},{1,0},{2,3},{3,2},{4,5},{5,4},{6,7},{7,6},{8,9},{9,8},{10,11... | collective-permute-start | bytes 73736 | tf_op jit(solution)/shard_map/ppermute | solution.py:13
  46.2 1.5 %collective-permute-done.13 = bf16[4,3072]{1,0:T(4,128)(2,1)S(1)} collective-permute-done((bf16[4,3072]{1,0:T(4,128)(2,1)S(1)}, bf16[4,3072]{1,0:T(4,128)(2,1)S(1)}, u32[]{:S(2)}, u32[]{:S(2)}) %collective-permute-start.13) | collective-permute-done | bytes 24608 | tf_op jit(solution)/shard_map/ppermute | solution.py:13
  48.2 2.7 %collective-permute-start.16 = (bf16[16,3072]{1,0:T(8,128)(2,1)S(1)}, bf16[16,3072]{1,0:T(8,128)(2,1)S(1)}, u32[]{:S(2)}, u32[]{:S(2)}) collective-permute-start(bf16[16,3072]{1,0:T(8,128)(2,1)S(1)} %constant_dynamic-update-slice_fusion.4.passed_ref), channel_id=1, source_target_pairs={{0,8},{4,12},{8,0},{12,4},{1,9},{5,13},{9,1},{13,5},{2,10},{6,14},... | collective-permute-start | bytes 294920 | tf_op jit(solution)/shard_map/ppermute | solution.py:13
  50.9 1.1 %collective-permute-start.17 = (bf16[16,3072]{1,0:T(8,128)(2,1)S(1)}, bf16[16,3072]{1,0:T(8,128)(2,1)S(1)}, u32[]{:S(2)}, u32[]{:S(2)}) collective-permute-start(bf16[16,3072]{1,0:T(8,128)(2,1)S(1)} %constant_dynamic-update-slice_fusion.4.passed_ref), channel_id=1, source_target_pairs={{0,12},{4,8},{8,4},{12,0},{1,13},{5,9},{9,5},{13,1},{2,14},{6,10},... | collective-permute-start | bytes 294920 | tf_op jit(solution)/shard_map/ppermute | solution.py:13
  52.0 7.2 %fetch.3 = (bf16[3072,3456]{1,0:T(8,128)(2,1)S(1)}, bf16[16,3072]{1,0:T(8,128)(2,1)S(1)}) custom-call(bf16[3072,4608]{1,0:T(8,128)(2,1)} %w_ref.5, bf16[16,3072]{1,0:T(8,128)(2,1)S(1)} %constant_dynamic-update-slice_fusion.4.passed_ref), custom_call_target="tpu_custom_call" | custom-call | bytes 21233664 | tf_op jit(solution)/shard_map/fetch/pallas_call | solution.py:116
  59.6 3.8 %multiply_held.1 = (f32[16,3456]{1,0:T(8,128)S(1)}, bf16[16,3456]{1,0:T(8,128)(2,1)S(1)}, bf16[16,3456]{1,0:T(8,128)(2,1)S(1)}, bf16[16,3456]{1,0:T(8,128)(2,1)S(1)}) custom-call(bf16[64,3072]{1,0:T(8,128)(2,1)S(1)} %constant_dynamic-update-slice_fusion.x_ref, bf16[3072,3456]{1,0:T(8,128)(2,1)S(1)} %get-tuple-element.37.w_ref), custom_call_target="tpu_custom_call" | custom-call | flops 1358954496 | bytes 21233664 | tf_op jit(solution)/shard_map/multiply_held/pallas_call | solution.py:217
  64.3 1.3 %collective-permute-start.21 = (bf16[16,3456]{1,0:T(8,128)(2,1)S(1)}, bf16[16,3456]{1,0:T(8,128)(2,1)S(1)}, u32[]{:S(2)}, u32[]{:S(2)}) collective-permute-start(bf16[16,3456]{1,0:T(8,128)(2,1)S(1)} %get-tuple-element.46), channel_id=1, source_target_pairs={{0,3},{1,2},{2,1},{3,0},{4,7},{5,6},{6,5},{7,4},{8,11},{9,10},{10,... | collective-permute-start | bytes 331784 | tf_op jit(solution)/shard_map/ppermute | solution.py:13
  65.6 3.9 %multiply_streamed.1 = (f32[16,1152]{1,0:T(8,128)S(1)}, bf16[16,1152]{1,0:T(8,128)(2,1)S(1)}, bf16[16,1152]{1,0:T(8,128)(2,1)S(1)}, bf16[16,1152]{1,0:T(8,128)(2,1)S(1)}) custom-call(bf16[64,3072]{1,0:T(8,128)(2,1)S(1)} %constant_dynamic-update-slice_fusion.x_ref, bf16[3072,4608]{1,0:T(8,128)(2,1)} %w_ref.5), custom_call_target="tpu_custom_call" | custom-call | flops 452984832 | bytes 7077888 | tf_op jit(solution)/shard_map/multiply_streamed/pallas_call | solution.py:251
  70.5 1.0 %collective-permute-start.24 = (bf16[16,1152]{1,0:T(8,128)(2,1)S(1)}, bf16[16,1152]{1,0:T(8,128)(2,1)S(1)}, u32[]{:S(2)}, u32[]{:S(2)}) collective-permute-start(bf16[16,1152]{1,0:T(8,128)(2,1)S(1)} %get-tuple-element.50), channel_id=1, source_target_pairs={{0,3},{1,2},{2,1},{3,0},{4,7},{5,6},{6,5},{7,4},{8,11},{9,10},{10,... | collective-permute-start | bytes 110600 | tf_op jit(solution)/shard_map/ppermute | solution.py:13
  71.6 2.2 %collective-permute-done.23 = bf16[16,1152]{1,0:T(8,128)(2,1)S(1)} collective-permute-done((bf16[16,1152]{1,0:T(8,128)(2,1)S(1)}, bf16[16,1152]{1,0:T(8,128)(2,1)S(1)}, u32[]{:S(2)}, u32[]{:S(2)}) %collective-permute-start.23) | collective-permute-done | bytes 36896 | tf_op jit(solution)/shard_map/ppermute | solution.py:13
  (99 shorter events, 11.3 us)
Async XLA Ops:
  1.3 4.5 %collective-permute-start.2 = (f32[1,16,2]{1,2,0:T(2,128)S(1)}, f32[1,16,2]{1,2,0:T(2,128)S(1)}, u32[]{:S(2)}, u32[]{:S(2)}) collective-permute-start(f32[1,16,2]{1,2,0:T(2,128)S(1)} %bitcast.98), channel_id=1, source_target_pairs={{0,2},{1,3},{2,0},{3,1},{4,6},{5,7},{6,4},{7,5},{8,10},{9,11},{10,... | collective-permute-start | bytes 392 | tf_op jit(solution)/shard_map/ppermute | solution.py:13
  4.2 7.6 %collective-permute-start = (bf16[1,16,4608]{2,1,0:T(8,128)(2,1)S(1)}, bf16[1,16,4608]{2,1,0:T(8,128)(2,1)S(1)}, u32[]{:S(2)}, u32[]{:S(2)}) collective-permute-start(bf16[1,16,4608]{2,1,0:T(8,128)(2,1)S(1)} %bitcast.86), channel_id=1, source_target_pairs={{0,2},{1,3},{2,0},{3,1},{4,6},{5,7},{6,4},{7,5},{8,10},{9,11},{10,... | collective-permute-start | bytes 442376 | tf_op jit(solution)/shard_map/ppermute | solution.py:13
  7.1 8.9 %collective-permute-start.4 = (f32[64,2]{1,0:T(8,128)S(1)}, f32[64,2]{1,0:T(8,128)S(1)}, u32[]{:S(2)}, u32[]{:S(2)}) collective-permute-start(f32[64,2]{1,0:T(8,128)S(1)} %bitcast.87), channel_id=1, source_target_pairs={{0,4},{4,0},{8,12},{12,8},{1,5},{5,1},{9,13},{13,9},{2,6},{6,2},{1... | collective-permute-start | bytes 1544 | tf_op jit(solution)/shard_map/ppermute | solution.py:13
  9.2 6.8 %collective-permute-start.5 = (f32[64,2]{1,0:T(8,128)S(1)}, f32[64,2]{1,0:T(8,128)S(1)}, u32[]{:S(2)}, u32[]{:S(2)}) collective-permute-start(f32[64,2]{1,0:T(8,128)S(1)} %bitcast.88), channel_id=1, source_target_pairs={{0,8},{4,12},{8,0},{12,4},{1,9},{5,13},{9,1},{13,5},{2,10},{6,14},... | collective-permute-start | bytes 1544 | tf_op jit(solution)/shard_map/ppermute | solution.py:13
  11.8 5.7 %collective-permute-start.6 = (f32[64,2]{1,0:T(8,128)S(1)}, f32[64,2]{1,0:T(8,128)S(1)}, u32[]{:S(2)}, u32[]{:S(2)}) collective-permute-start(f32[64,2]{1,0:T(8,128)S(1)} %bitcast.89), channel_id=1, source_target_pairs={{0,12},{4,8},{8,4},{12,0},{1,13},{5,9},{9,5},{13,1},{2,14},{6,10},... | collective-permute-start | bytes 1544 | tf_op jit(solution)/shard_map/ppermute | solution.py:13
  11.9 5.8 %collective-permute-start.1 = (bf16[2,16,4608]{2,1,0:T(8,128)(2,1)S(1)}, bf16[2,16,4608]{2,1,0:T(8,128)(2,1)S(1)}, u32[]{:S(2)}, u32[]{:S(2)}) collective-permute-start(bf16[2,16,4608]{2,1,0:T(8,128)(2,1)S(1)} %maximum_bitcast_fusion.refs_0_), channel_id=1, source_target_pairs={{0,1},{1,0},{2,3},{3,2},{4,5},{5,4},{6,7},{7,6},{8,9},{9,8},{10,11... | collective-permute-start | bytes 884744 | tf_op jit(solution)/shard_map/ppermute | solution.py:13
  25.7 10.3 %collective-permute-start.7 = (f16[16,3200]{1,0:T(8,128)(2,1)S(1)}, f16[16,3200]{1,0:T(8,128)(2,1)S(1)}, u32[]{:S(2)}, u32[]{:S(2)}) collective-permute-start(f16[16,3200]{1,0:T(8,128)(2,1)S(1)} %get-tuple-element.53), channel_id=1, source_target_pairs={{0,8},{4,12},{8,0},{12,4},{1,9},{5,13},{9,1},{13,5},{2,10},{6,14},... | collective-permute-start | bytes 307208 | tf_op jit(solution)/shard_map/ppermute | solution.py:13
  26.2 9.8 %collective-permute-start.8 = (f16[16,3200]{1,0:T(8,128)(2,1)S(1)}, f16[16,3200]{1,0:T(8,128)(2,1)S(1)}, u32[]{:S(2)}, u32[]{:S(2)}) collective-permute-start(f16[16,3200]{1,0:T(8,128)(2,1)S(1)} %get-tuple-element.55), channel_id=1, source_target_pairs={{0,12},{4,8},{8,4},{12,0},{1,13},{5,9},{9,5},{13,1},{2,14},{6,10},... | collective-permute-start | bytes 307208 | tf_op jit(solution)/shard_map/ppermute | solution.py:13
  28.1 8.2 %collective-permute-start.9 = (f16[16,3200]{1,0:T(8,128)(2,1)S(1)}, f16[16,3200]{1,0:T(8,128)(2,1)S(1)}, u32[]{:S(2)}, u32[]{:S(2)}) collective-permute-start(f16[16,3200]{1,0:T(8,128)(2,1)S(1)} %get-tuple-element.54), channel_id=1, source_target_pairs={{0,4},{4,0},{8,12},{12,8},{1,5},{5,1},{9,13},{13,9},{2,6},{6,2},{1... | collective-permute-start | bytes 307208 | tf_op jit(solution)/shard_map/ppermute | solution.py:13
  36.5 3.9 %collective-permute-start.11 = (bf16[4,3200]{1,0:T(4,128)(2,1)S(1)}, bf16[4,3200]{1,0:T(4,128)(2,1)S(1)}, u32[]{:S(2)}, u32[]{:S(2)}) collective-permute-start(bf16[4,3200]{1,0:T(4,128)(2,1)S(1)} %get-tuple-element.62), channel_id=1, source_target_pairs={{0,2},{1,3},{2,0},{3,1},{4,6},{5,7},{6,4},{7,5},{8,10},{9,11},{10,... | collective-permute-start | bytes 76808 | tf_op jit(solution)/shard_map/ppermute | solution.py:13
  38.2 3.3 %collective-permute-start.12 = (bf16[4,3200]{1,0:T(4,128)(2,1)S(1)}, bf16[4,3200]{1,0:T(4,128)(2,1)S(1)}, u32[]{:S(2)}, u32[]{:S(2)}) collective-permute-start(bf16[4,3200]{1,0:T(4,128)(2,1)S(1)} %get-tuple-element.61), channel_id=1, source_target_pairs={{0,3},{1,2},{2,1},{3,0},{4,7},{5,6},{6,5},{7,4},{8,11},{9,10},{10,... | collective-permute-start | bytes 76808 | tf_op jit(solution)/shard_map/ppermute | solution.py:13
  38.2 3.3 %collective-permute-start.10 = (bf16[4,3200]{1,0:T(4,128)(2,1)S(1)}, bf16[4,3200]{1,0:T(4,128)(2,1)S(1)}, u32[]{:S(2)}, u32[]{:S(2)}) collective-permute-start(bf16[4,3200]{1,0:T(4,128)(2,1)S(1)} %get-tuple-element.60), channel_id=1, source_target_pairs={{0,1},{1,0},{2,3},{3,2},{4,5},{5,4},{6,7},{7,6},{8,9},{9,8},{10,11... | collective-permute-start | bytes 76808 | tf_op jit(solution)/shard_map/ppermute | solution.py:13
  43.8 3.9 %collective-permute-start.13 = (bf16[4,3072]{1,0:T(4,128)(2,1)S(1)}, bf16[4,3072]{1,0:T(4,128)(2,1)S(1)}, u32[]{:S(2)}, u32[]{:S(2)}) collective-permute-start(bf16[4,3072]{1,0:T(4,128)(2,1)S(1)} %bitcast.94), channel_id=1, source_target_pairs={{0,2},{1,3},{2,0},{3,1},{4,6},{5,7},{6,4},{7,5},{8,10},{9,11},{10,... | collective-permute-start | bytes 73736 | tf_op jit(solution)/shard_map/ppermute | solution.py:13
  44.6 3.6 %collective-permute-start.14 = (bf16[4,3072]{1,0:T(4,128)(2,1)S(1)}, bf16[4,3072]{1,0:T(4,128)(2,1)S(1)}, u32[]{:S(2)}, u32[]{:S(2)}) collective-permute-start(bf16[4,3072]{1,0:T(4,128)(2,1)S(1)} %bitcast.93), channel_id=1, source_target_pairs={{0,3},{1,2},{2,1},{3,0},{4,7},{5,6},{6,5},{7,4},{8,11},{9,10},{10,... | collective-permute-start | bytes 73736 | tf_op jit(solution)/shard_map/ppermute | solution.py:13
  44.7 3.5 %collective-permute-start.15 = (bf16[4,3072]{1,0:T(4,128)(2,1)S(1)}, bf16[4,3072]{1,0:T(4,128)(2,1)S(1)}, u32[]{:S(2)}, u32[]{:S(2)}) collective-permute-start(bf16[4,3072]{1,0:T(4,128)(2,1)S(1)} %bitcast.92), channel_id=1, source_target_pairs={{0,1},{1,0},{2,3},{3,2},{4,5},{5,4},{6,7},{7,6},{8,9},{9,8},{10,11... | collective-permute-start | bytes 73736 | tf_op jit(solution)/shard_map/ppermute | solution.py:13
  48.2 11.0 %collective-permute-start.16 = (bf16[16,3072]{1,0:T(8,128)(2,1)S(1)}, bf16[16,3072]{1,0:T(8,128)(2,1)S(1)}, u32[]{:S(2)}, u32[]{:S(2)}) collective-permute-start(bf16[16,3072]{1,0:T(8,128)(2,1)S(1)} %constant_dynamic-update-slice_fusion.4.passed_ref), channel_id=1, source_target_pairs={{0,8},{4,12},{8,0},{12,4},{1,9},{5,13},{9,1},{13,5},{2,10},{6,14},... | collective-permute-start | bytes 294920 | tf_op jit(solution)/shard_map/ppermute | solution.py:13
  50.9 8.4 %collective-permute-start.17 = (bf16[16,3072]{1,0:T(8,128)(2,1)S(1)}, bf16[16,3072]{1,0:T(8,128)(2,1)S(1)}, u32[]{:S(2)}, u32[]{:S(2)}) collective-permute-start(bf16[16,3072]{1,0:T(8,128)(2,1)S(1)} %constant_dynamic-update-slice_fusion.4.passed_ref), channel_id=1, source_target_pairs={{0,12},{4,8},{8,4},{12,0},{1,13},{5,9},{9,5},{13,1},{2,14},{6,10},... | collective-permute-start | bytes 294920 | tf_op jit(solution)/shard_map/ppermute | solution.py:13
  52.0 7.6 %collective-permute-start.18 = (bf16[16,3072]{1,0:T(8,128)(2,1)S(1)}, bf16[16,3072]{1,0:T(8,128)(2,1)S(1)}, u32[]{:S(2)}, u32[]{:S(2)}) collective-permute-start(bf16[16,3072]{1,0:T(8,128)(2,1)S(1)} %constant_dynamic-update-slice_fusion.4.passed_ref), channel_id=1, source_target_pairs={{0,4},{4,0},{8,12},{12,8},{1,5},{5,1},{9,13},{13,9},{2,6},{6,2},{1... | collective-permute-start | bytes 294920 | tf_op jit(solution)/shard_map/ppermute | solution.py:13
  63.4 6.1 %collective-permute-start.20 = (bf16[16,3456]{1,0:T(8,128)(2,1)S(1)}, bf16[16,3456]{1,0:T(8,128)(2,1)S(1)}, u32[]{:S(2)}, u32[]{:S(2)}) collective-permute-start(bf16[16,3456]{1,0:T(8,128)(2,1)S(1)} %get-tuple-element.44), channel_id=1, source_target_pairs={{0,2},{1,3},{2,0},{3,1},{4,6},{5,7},{6,4},{7,5},{8,10},{9,11},{10,... | collective-permute-start | bytes 331784 | tf_op jit(solution)/shard_map/ppermute | solution.py:13
  64.3 7.2 %collective-permute-start.19 = (bf16[16,3456]{1,0:T(8,128)(2,1)S(1)}, bf16[16,3456]{1,0:T(8,128)(2,1)S(1)}, u32[]{:S(2)}, u32[]{:S(2)}) collective-permute-start(bf16[16,3456]{1,0:T(8,128)(2,1)S(1)} %get-tuple-element.39), channel_id=1, source_target_pairs={{0,1},{1,0},{2,3},{3,2},{4,5},{5,4},{6,7},{7,6},{8,9},{9,8},{10,11... | collective-permute-start | bytes 331784 | tf_op jit(solution)/shard_map/ppermute | solution.py:13
  64.3 7.2 %collective-permute-start.21 = (bf16[16,3456]{1,0:T(8,128)(2,1)S(1)}, bf16[16,3456]{1,0:T(8,128)(2,1)S(1)}, u32[]{:S(2)}, u32[]{:S(2)}) collective-permute-start(bf16[16,3456]{1,0:T(8,128)(2,1)S(1)} %get-tuple-element.46), channel_id=1, source_target_pairs={{0,3},{1,2},{2,1},{3,0},{4,7},{5,6},{6,5},{7,4},{8,11},{9,10},{10,... | collective-permute-start | bytes 331784 | tf_op jit(solution)/shard_map/ppermute | solution.py:13
  69.5 2.0 %collective-permute-start.22 = (bf16[16,1152]{1,0:T(8,128)(2,1)S(1)}, bf16[16,1152]{1,0:T(8,128)(2,1)S(1)}, u32[]{:S(2)}, u32[]{:S(2)}) collective-permute-start(bf16[16,1152]{1,0:T(8,128)(2,1)S(1)} %get-tuple-element.48), channel_id=1, source_target_pairs={{0,1},{1,0},{2,3},{3,2},{4,5},{5,4},{6,7},{7,6},{8,9},{9,8},{10,11... | collective-permute-start | bytes 110600 | tf_op jit(solution)/shard_map/ppermute | solution.py:13
  69.6 4.2 %collective-permute-start.23 = (bf16[16,1152]{1,0:T(8,128)(2,1)S(1)}, bf16[16,1152]{1,0:T(8,128)(2,1)S(1)}, u32[]{:S(2)}, u32[]{:S(2)}) collective-permute-start(bf16[16,1152]{1,0:T(8,128)(2,1)S(1)} %get-tuple-element.49), channel_id=1, source_target_pairs={{0,2},{1,3},{2,0},{3,1},{4,6},{5,7},{6,4},{7,5},{8,10},{9,11},{10,... | collective-permute-start | bytes 110600 | tf_op jit(solution)/shard_map/ppermute | solution.py:13
  70.5 3.8 %collective-permute-start.24 = (bf16[16,1152]{1,0:T(8,128)(2,1)S(1)}, bf16[16,1152]{1,0:T(8,128)(2,1)S(1)}, u32[]{:S(2)}, u32[]{:S(2)}) collective-permute-start(bf16[16,1152]{1,0:T(8,128)(2,1)S(1)} %get-tuple-element.50), channel_id=1, source_target_pairs={{0,3},{1,2},{2,1},{3,0},{4,7},{5,6},{6,5},{7,4},{8,11},{9,10},{10,... | collective-permute-start | bytes 110600 | tf_op jit(solution)/shard_map/ppermute | solution.py:13
  (6 other events, 66.0 us)

commit v4 on v3

--- a/solution.py
+++ b/solution.py
@@ -22,18 +22,13 @@
     return list(range(n // 2, n)) + list(range(1, n // 2))
 
 
+def order_of(n):
+    return far_first(n)[::-1]
+
+
 def exchange(parts, axis, n):
     back = {m: swap(parts[m], axis, n, m) for m in far_first(n)}
     return [parts[0]] + [back[m] for m in range(1, n)]
-
-
-def reduce_rows(partial, axis, n, encode, decode):
-    me = lax.axis_index(axis)
-    got = [swap(encode(rows_of(partial, me ^ m, n)), axis, n, m) for m in far_first(n)]
-    total = rows_of(partial, me, n)
-    for part in got:
-        total = total + decode(part)
-    return total
 
 
 def to_bfloat16(x):
@@ -129,6 +124,32 @@
         ),
         name="fetch",
     )(pltpu.with_memory_space_constraint(w, pltpu.HBM), passed, *after)
+
+
+def set_aside(w, start, passed):
+    rows, cols = w.shape[0], w.shape[1] - start
+
+    def body(w_ref, passed_ref, out_ref, passed_out, sem):
+        copy = pltpu.make_async_copy(w_ref.at[:, pl.ds(start, cols)], out_ref, sem)
+        copy.start()
+        passed_out[...] = passed_ref[...]
+        copy.wait()
+
+    return pl.pallas_call(
+        body,
+        out_shape=[
+            jax.ShapeDtypeStruct((rows, cols), w.dtype),
+            pltpu.VMEM(passed.shape, passed.dtype),
+        ],
+        in_specs=[pl.BlockSpec(memory_space=pltpu.HBM), in_vmem()],
+        out_specs=[pl.BlockSpec(memory_space=pl.ANY), in_vmem()],
+        scratch_shapes=[pltpu.SemaphoreType.DMA],
+        compiler_params=pltpu.CompilerParams(vmem_limit_bytes=4 << 20),
+        cost_estimate=pl.CostEstimate(
+            flops=0, bytes_accessed=4 * rows * cols, transcendentals=0
+        ),
+        name="set_aside",
+    )(pltpu.with_memory_space_constraint(w, pltpu.HBM), passed)
 
 
 def tiles(cols, size=512):
@@ -228,44 +249,6 @@
     )(x, pltpu.with_memory_space_constraint(w, pltpu.VMEM))
 
 
-def multiply_streamed(x, w, start, axis, n):
-    rows, depth = x.shape
-    cols = w.shape[1] - start
-    parts = tiles(cols, 384)
-
-    def body(x_ref, w_ref, *refs):
-        total, scratch, sems = refs[-3:]
-        copies = [
-            pltpu.make_async_copy(
-                w_ref.at[:, pl.ds(start + c, size)], scratch.at[:, pl.ds(c, size)], sems.at[i]
-            )
-            for i, (c, size) in enumerate(parts)
-        ]
-        for copy in copies:
-            copy.start()
-        for copy, (c, size) in zip(copies, parts):
-            copy.wait()
-            total[:, c : c + size] = dot_f32(x_ref[...], scratch[:, c : c + size])
-        shares(total, refs[:-3], axis, n)
-
-    return pl.pallas_call(
-        body,
-        out_shape=share_shapes(rows, cols, n),
-        in_specs=[in_vmem(), pl.BlockSpec(memory_space=pltpu.HBM)],
-        out_specs=[in_vmem()] * n,
-        scratch_shapes=[
-            pltpu.VMEM((rows, cols), jnp.float32),
-            pltpu.VMEM((depth, cols), w.dtype),
-            pltpu.SemaphoreType.DMA((len(parts),)),
-        ],
-        compiler_params=pltpu.CompilerParams(vmem_limit_bytes=16 << 20),
-        cost_estimate=pl.CostEstimate(
-            flops=2 * rows * depth * cols, bytes_accessed=2 * depth * cols, transcendentals=0
-        ),
-        name="multiply_streamed",
-    )(x, pltpu.with_memory_space_constraint(w, pltpu.HBM))
-
-
 def attend_local(query_heads, new_key, new_value, k_cache, v_cache, cache_lengths):
     scores = (
         jnp.einsum("shd,std->sht", query_heads, k_cache, preferred_element_type=jnp.float32)
@@ -327,8 +310,18 @@
         ).astype(jnp.bfloat16)
         kv_cols = w_keyval.shape[1] // ny
         projected = project(normed, w_head, w_query, w_keyval, kv_cols, "gy")
-        part = reduce_rows(projected, "gx", nx, to_wire, from_wire).astype(jnp.bfloat16)
+        cut = whole_tiles(w_out.shape[1] * 11 // 16)
+        me = lax.axis_index("gx")
+        parts = [to_wire(rows_of(projected, me ^ m, nx)) for m in range(nx)]
+        parts = exchange(parts, "gx", nx)[1:]
+        w_right, part = set_aside(w_out, cut, rows_of(projected, me, nx))
+        parts = [parts[m - 1] for m in order_of(nx)]
+        parts, part = lax.optimization_barrier((parts, part))
+        part = sum((from_wire(x) for x in parts), part).astype(jnp.bfloat16)
         mixed = exchange([rows_of(part, gy ^ m, ny) for m in range(ny)], "gy", ny)
+        order = order_of(ny)
+        arrived = lax.optimization_barrier([mixed[m] for m in order])
+        mixed = mixed[:1] + [arrived[order.index(m)] for m in range(1, ny)]
         queries = jnp.concatenate(
             [x[:, :q_cols].reshape(seqs, -1, head_dim) for x in mixed], axis=1
         )
@@ -346,12 +339,15 @@
             ),
             "gy",
         )
-        cut = whole_tiles(w_out.shape[1] * 3 // 4)
         w_left, own = fetch(w_out, 0, cut, returned)
-        everyone = in_order([own] + exchange([returned] * nx, "gx", nx)[1:], "gx")
+        others = exchange([returned] * nx, "gx", nx)
+        order = order_of(nx)
+        arrived, own = lax.optimization_barrier(([others[m] for m in order], own))
+        arrived = dict(zip(order, arrived))
+        everyone = in_order([own] + [arrived[m] for m in range(1, nx)], "gx")
         left = exchange(multiply_held(everyone, w_left, "gy", ny), "gy", ny)
-        right = multiply_streamed(everyone, w_out, cut, "gy", ny)
-        right, left[ny // 2] = lax.optimization_barrier((right, left[ny // 2]))
+        right = multiply_held(everyone, w_right, "gy", ny)
+        right, left[1] = lax.optimization_barrier((right, left[1]))
         right = exchange(right, "gy", ny)
         outs = [sum((to_float32(x) for x in parts[1:]), parts[0]) for parts in (left, right)]
         return jnp.concatenate([to_bfloat16(x) for x in outs], axis=1)

time: 75.2 us -> 73.7 us (0.980)
  waiting for transfers between devices: 18 us -> 11.7 us
  local copies, waits for them, and re-layouts: 2.17 us -> 5.83 us
    ppermute x25, waiting for transfers between devices: 18 us -> 11.7 us  [swap(): return lax.ppermute(x, axis, [(k, k ^ m) for k in range(n)])]
    unnamed x15 -> x21, local copies, waits for them, and re-layouts: 1.43 us -> 5.07 us
    pallas_call x1 -> x2, Pallas kernels: 3.79 us -> 5.18 us  [multiply_held(): pl.pallas_call(body, out_shape=share_shapes(rows, cols, n), in_specs=[in_...]
  transfers between devices with their start and end apart: 25 -> 25, of which waited for: 12 -> 13; matrix products, arithmetic and copies ran while one was open for 2% -> 2% of each run, Pallas kernels for 20% -> 22%
where the time goes in v4:
time: 73.7 us; the launch traced here: 73.4 us
  Pallas kernels  26.8 us (36%)
  starting transfers between devices  24.4 us (33%)
  waiting for transfers between devices  11.7 us (16%)
  local copies, waits for them, and re-layouts  5.83 us (8%)
  other arithmetic  2.63 us (4%)
  matrix products  1.48 us (2%)
    ppermute x25, starting transfers between devices, swap(): return lax.ppermute(x, axis, [(k, k ^ m) for k in range(n)])  24.4 us
    ppermute x25, waiting for transfers between devices, swap(): return lax.ppermute(x, axis, [(k, k ^ m) for k in range(n)])  11.7 us
    pallas_call x2, Pallas kernels, fetch(): pl.pallas_call(body, out_shape=[pltpu.VMEM((rows, cols), w.dtype), pltpu....  10.5 us
    pallas_call x1, Pallas kernels, project(): pl.pallas_call(body, out_shape=jax.ShapeDtypeStruct((rows, cols + last_co...  7.37 us
    pallas_call x2, Pallas kernels, multiply_held(): pl.pallas_call(body, out_shape=share_shapes(rows, cols, n), in_specs=[in_...  5.18 us
    unnamed x21, local copies, waits for them, and re-layouts  5.07 us
    pallas_call x1, Pallas kernels, set_aside(): pl.pallas_call(body, out_shape=[jax.ShapeDtypeStruct((rows, cols), w.dtyp...  3.69 us
  transfers between devices with their start and end apart: 25, of which 13 were waited for; matrix products, arithmetic and copies ran while one was open for 2% of the time, Pallas kernels for 22%

profile of v4, /device:TPU:0, one launch (start us, length us, event | category | flops | bytes accessed | tf_op | source)
XLA Modules:
  0.0 73.4 jit_solution(1331359421049570376)
XLA Ops:
  0.0 1.1 %copy-done.2 = bf16[16,4608]{1,0:T(8,128)(2,1)S(1)} copy-done((bf16[16,4608]{1,0:T(8,128)(2,1)S(1)}, bf16[16,4608]{1,0:T(8,128)(2,1)}, u32[]{:S(2)}) %copy-start.2) | copy-done | bytes 147480
  1.3 2.9 %collective-permute-start.2 = (f32[1,16,2]{1,2,0:T(2,128)S(1)}, f32[1,16,2]{1,2,0:T(2,128)S(1)}, u32[]{:S(2)}, u32[]{:S(2)}) collective-permute-start(f32[1,16,2]{1,2,0:T(2,128)S(1)} %bitcast.94), channel_id=1, source_target_pairs={{0,2},{1,3},{2,0},{3,1},{4,6},{5,7},{6,4},{7,5},{8,10},{9,11},{10,... | collective-permute-start | bytes 392 | tf_op jit(solution)/shard_map/ppermute | solution.py:13
  4.3 1.5 %collective-permute-done.2 = f32[1,16,2]{1,2,0:T(2,128)S(1)} collective-permute-done((f32[1,16,2]{1,2,0:T(2,128)S(1)}, f32[1,16,2]{1,2,0:T(2,128)S(1)}, u32[]{:S(2)}, u32[]{:S(2)}) %collective-permute-start.2) | collective-permute-done | bytes 160 | tf_op jit(solution)/shard_map/ppermute | solution.py:13
  7.1 4.2 %collective-permute-start.6 = (f32[64,2]{1,0:T(8,128)S(1)}, f32[64,2]{1,0:T(8,128)S(1)}, u32[]{:S(2)}, u32[]{:S(2)}) collective-permute-start(f32[64,2]{1,0:T(8,128)S(1)} %bitcast.83), channel_id=1, source_target_pairs={{0,12},{4,8},{8,4},{12,0},{1,13},{5,9},{9,5},{13,1},{2,14},{6,10},... | collective-permute-start | bytes 1544 | tf_op jit(solution)/shard_map/ppermute | solution.py:13
  12.1 4.0 %fetch.2 = (bf16[4608,1152]{1,0:T(8,128)(2,1)S(1)}, f32[64,2]{1,0:T(8,128)S(1)}) custom-call(bf16[4608,3072]{1,0:T(8,128)(2,1)} %all_ref.1, f32[64,2]{1,0:T(8,128)S(1)} %bitcast.86, bf16[2,16,4608]{2,1,0:T(8,128)(2,1)S(1)} %maximum_bitcast_fusion.refs_0_), custom_call_target="tpu_custom_call" | custom-call | bytes 10616832 | tf_op jit(solution)/shard_map/fetch/pallas_call | solution.py:111
  16.8 7.4 %project.1 = f32[64,3200]{1,0:T(8,128)S(1)} custom-call(bf16[64,4608]{1,0:T(8,128)(2,1)S(1)} %fusion.3.x_ref, bf16[4608,1152]{1,0:T(8,128)(2,1)S(1)} %get-tuple-element.48.head_ref, bf16[4608,3072]{1,0:T(8,128)(2,1)} %all_ref.1, bf16[4608,512]{1,0:T(8,128)(2,1)} %last_ref.1), custom_call_target="tpu_custom_call" | custom-call | flops 1811939328 | bytes 28311552 | tf_op jit(solution)/shard_map/project/pallas_call | solution.py:193
  24.3 2.3 %collective-permute-start.9 = (f16[16,3200]{1,0:T(8,128)(2,1)S(1)}, f16[16,3200]{1,0:T(8,128)(2,1)S(1)}, u32[]{:S(2)}, u32[]{:S(2)}) collective-permute-start(f16[16,3200]{1,0:T(8,128)(2,1)S(1)} %get-tuple-element.80), channel_id=1, source_target_pairs={{0,8},{4,12},{8,0},{12,4},{1,9},{5,13},{9,1},{13,5},{2,10},{6,14},... | collective-permute-start | bytes 307208 | tf_op jit(solution)/shard_map/ppermute | solution.py:13
  26.6 1.5 %collective-permute-start.8 = (f16[16,3200]{1,0:T(8,128)(2,1)S(1)}, f16[16,3200]{1,0:T(8,128)(2,1)S(1)}, u32[]{:S(2)}, u32[]{:S(2)}) collective-permute-start(f16[16,3200]{1,0:T(8,128)(2,1)S(1)} %get-tuple-element.81), channel_id=1, source_target_pairs={{0,12},{4,8},{8,4},{12,0},{1,13},{5,9},{9,5},{13,1},{2,14},{6,10},... | collective-permute-start | bytes 307208 | tf_op jit(solution)/shard_map/ppermute | solution.py:13
  28.7 3.7 %set_aside.1 = (bf16[3072,1536]{1,0:T(8,128)(2,1)S(1)}, f32[16,3200]{1,0:T(8,128)S(1)}) custom-call(bf16[3072,4608]{1,0:T(8,128)(2,1)} %w_ref.5, f32[16,3200]{1,0:T(8,128)S(1)} %get-tuple-element.79.passed_ref), custom_call_target="tpu_custom_call" | custom-call | bytes 18874368 | tf_op jit(solution)/shard_map/set_aside/pallas_call | solution.py:138
  32.4 3.6 %copy-done.1 = bf16[3072,1536]{1,0:T(8,128)(2,1)} copy-done((bf16[3072,1536]{1,0:T(8,128)(2,1)}, bf16[3072,1536]{1,0:T(8,128)(2,1)S(1)}, u32[]{:S(2)}) %copy-start.1) | copy-done | bytes 9437208
  36.5 1.7 %collective-permute-start.12 = (bf16[4,3200]{1,0:T(4,128)(2,1)S(1)}, bf16[4,3200]{1,0:T(4,128)(2,1)S(1)}, u32[]{:S(2)}, u32[]{:S(2)}) collective-permute-start(bf16[4,3200]{1,0:T(4,128)(2,1)S(1)} %get-tuple-element.87), channel_id=1, source_target_pairs={{0,2},{1,3},{2,0},{3,1},{4,6},{5,7},{6,4},{7,5},{8,10},{9,11},{10,... | collective-permute-start | bytes 76808 | tf_op jit(solution)/shard_map/ppermute | solution.py:13
  38.8 1.6 %collective-permute-done.12 = bf16[4,3200]{1,0:T(4,128)(2,1)S(1)} collective-permute-done((bf16[4,3200]{1,0:T(4,128)(2,1)S(1)}, bf16[4,3200]{1,0:T(4,128)(2,1)S(1)}, u32[]{:S(2)}, u32[]{:S(2)}) %collective-permute-start.12) | collective-permute-done | bytes 25632 | tf_op jit(solution)/shard_map/ppermute | solution.py:13
  40.4 1.1 %collective-permute-done.11 = bf16[4,3200]{1,0:T(4,128)(2,1)S(1)} collective-permute-done((bf16[4,3200]{1,0:T(4,128)(2,1)S(1)}, bf16[4,3200]{1,0:T(4,128)(2,1)S(1)}, u32[]{:S(2)}, u32[]{:S(2)}) %collective-permute-start.11) | collective-permute-done | bytes 25632 | tf_op jit(solution)/shard_map/ppermute | solution.py:13
  44.6 1.5 %collective-permute-start.15 = (bf16[4,3072]{1,0:T(4,128)(2,1)S(1)}, bf16[4,3072]{1,0:T(4,128)(2,1)S(1)}, u32[]{:S(2)}, u32[]{:S(2)}) collective-permute-start(bf16[4,3072]{1,0:T(4,128)(2,1)S(1)} %bitcast.88), channel_id=1, source_target_pairs={{0,1},{1,0},{2,3},{3,2},{4,5},{5,4},{6,7},{7,6},{8,9},{9,8},{10,11... | collective-permute-start | bytes 73736 | tf_op jit(solution)/shard_map/ppermute | solution.py:13
  46.2 1.8 %collective-permute-done.13 = bf16[4,3072]{1,0:T(4,128)(2,1)S(1)} collective-permute-done((bf16[4,3072]{1,0:T(4,128)(2,1)S(1)}, bf16[4,3072]{1,0:T(4,128)(2,1)S(1)}, u32[]{:S(2)}, u32[]{:S(2)}) %collective-permute-start.13) | collective-permute-done | bytes 24608 | tf_op jit(solution)/shard_map/ppermute | solution.py:13
  48.2 3.2 %collective-permute-start.18 = (bf16[16,3072]{1,0:T(8,128)(2,1)S(1)}, bf16[16,3072]{1,0:T(8,128)(2,1)S(1)}, u32[]{:S(2)}, u32[]{:S(2)}) collective-permute-start(bf16[16,3072]{1,0:T(8,128)(2,1)S(1)} %constant_dynamic-update-slice_fusion.4.passed_ref), channel_id=1, source_target_pairs={{0,8},{4,12},{8,0},{12,4},{1,9},{5,13},{9,1},{13,5},{2,10},{6,14},... | collective-permute-start | bytes 294920 | tf_op jit(solution)/shard_map/ppermute | solution.py:13
  52.1 6.4 %fetch.3 = (bf16[3072,3072]{1,0:T(8,128)(2,1)S(1)}, bf16[16,3072]{1,0:T(8,128)(2,1)S(1)}) custom-call(bf16[3072,4608]{1,0:T(8,128)(2,1)} %w_ref.5, bf16[16,3072]{1,0:T(8,128)(2,1)S(1)} %constant_dynamic-update-slice_fusion.4.passed_ref), custom_call_target="tpu_custom_call" | custom-call | bytes 18874368 | tf_op jit(solution)/shard_map/fetch/pallas_call | solution.py:111
  59.1 0.9 %collective-permute-done.16 = bf16[16,3072]{1,0:T(8,128)(2,1)S(1)} collective-permute-done((bf16[16,3072]{1,0:T(8,128)(2,1)S(1)}, bf16[16,3072]{1,0:T(8,128)(2,1)S(1)}, u32[]{:S(2)}, u32[]{:S(2)}) %collective-permute-start.16) | collective-permute-done | bytes 98336 | tf_op jit(solution)/shard_map/ppermute | solution.py:13
  60.2 3.4 %multiply_held.2 = (f32[16,3072]{1,0:T(8,128)S(1)}, bf16[16,3072]{1,0:T(8,128)(2,1)S(1)}, bf16[16,3072]{1,0:T(8,128)(2,1)S(1)}, bf16[16,3072]{1,0:T(8,128)(2,1)S(1)}) custom-call(bf16[64,3072]{1,0:T(8,128)(2,1)S(1)} %constant_dynamic-update-slice_fusion.x_ref, bf16[3072,3072]{1,0:T(8,128)(2,1)S(1)} %get-tuple-element.62.w_ref), custom_call_target="tpu_custom_call" | custom-call | flops 1207959552 | bytes 18874368 | tf_op jit(solution)/shard_map/multiply_held/pallas_call | solution.py:238
  63.7 0.9 %collective-permute-start.20 = (bf16[16,3072]{1,0:T(8,128)(2,1)S(1)}, bf16[16,3072]{1,0:T(8,128)(2,1)S(1)}, u32[]{:S(2)}, u32[]{:S(2)}) collective-permute-start(bf16[16,3072]{1,0:T(8,128)(2,1)S(1)} %get-tuple-element.71), channel_id=1, source_target_pairs={{0,2},{1,3},{2,0},{3,1},{4,6},{5,7},{6,4},{7,5},{8,10},{9,11},{10,... | collective-permute-start | bytes 294920 | tf_op jit(solution)/shard_map/ppermute | solution.py:13
  64.6 1.0 %collective-permute-start.21 = (bf16[16,3072]{1,0:T(8,128)(2,1)S(1)}, bf16[16,3072]{1,0:T(8,128)(2,1)S(1)}, u32[]{:S(2)}, u32[]{:S(2)}) collective-permute-start(bf16[16,3072]{1,0:T(8,128)(2,1)S(1)} %get-tuple-element.72), channel_id=1, source_target_pairs={{0,3},{1,2},{2,1},{3,0},{4,7},{5,6},{6,5},{7,4},{8,11},{9,10},{10,... | collective-permute-start | bytes 294920 | tf_op jit(solution)/shard_map/ppermute | solution.py:13
  65.6 1.7 %multiply_held.3 = (f32[16,1536]{1,0:T(8,128)S(1)}, bf16[16,1536]{1,0:T(8,128)(2,1)S(1)}, bf16[16,1536]{1,0:T(8,128)(2,1)S(1)}, bf16[16,1536]{1,0:T(8,128)(2,1)S(1)}) custom-call(bf16[64,3072]{1,0:T(8,128)(2,1)S(1)} %constant_dynamic-update-slice_fusion.x_ref, bf16[3072,1536]{1,0:T(8,128)(2,1)S(1)} %bitcast.81), custom_call_target="tpu_custom_call" | custom-call | flops 603979776 | bytes 9437184 | tf_op jit(solution)/shard_map/multiply_held/pallas_call | solution.py:238
  69.4 1.2 %collective-permute-done.21 = bf16[16,3072]{1,0:T(8,128)(2,1)S(1)} collective-permute-done((bf16[16,3072]{1,0:T(8,128)(2,1)S(1)}, bf16[16,3072]{1,0:T(8,128)(2,1)S(1)}, u32[]{:S(2)}, u32[]{:S(2)}) %collective-permute-start.21) | collective-permute-done | bytes 98336 | tf_op jit(solution)/shard_map/ppermute | solution.py:13
  70.6 1.9 %collective-permute-done.23 = bf16[16,1536]{1,0:T(8,128)(2,1)S(1)} collective-permute-done((bf16[16,1536]{1,0:T(8,128)(2,1)S(1)}, bf16[16,1536]{1,0:T(8,128)(2,1)S(1)}, u32[]{:S(2)}, u32[]{:S(2)}) %collective-permute-start.23) | collective-permute-done | bytes 49184 | tf_op jit(solution)/shard_map/ppermute | solution.py:13
  (107 shorter events, 12.3 us)
Async XLA Ops:
  1.3 4.5 %collective-permute-start.2 = (f32[1,16,2]{1,2,0:T(2,128)S(1)}, f32[1,16,2]{1,2,0:T(2,128)S(1)}, u32[]{:S(2)}, u32[]{:S(2)}) collective-permute-start(f32[1,16,2]{1,2,0:T(2,128)S(1)} %bitcast.94), channel_id=1, source_target_pairs={{0,2},{1,3},{2,0},{3,1},{4,6},{5,7},{6,4},{7,5},{8,10},{9,11},{10,... | collective-permute-start | bytes 392 | tf_op jit(solution)/shard_map/ppermute | solution.py:13
  4.2 7.7 %collective-permute-start = (bf16[1,16,4608]{2,1,0:T(8,128)(2,1)S(1)}, bf16[1,16,4608]{2,1,0:T(8,128)(2,1)S(1)}, u32[]{:S(2)}, u32[]{:S(2)}) collective-permute-start(bf16[1,16,4608]{2,1,0:T(8,128)(2,1)S(1)} %bitcast.82), channel_id=1, source_target_pairs={{0,2},{1,3},{2,0},{3,1},{4,6},{5,7},{6,4},{7,5},{8,10},{9,11},{10,... | collective-permute-start | bytes 442376 | tf_op jit(solution)/shard_map/ppermute | solution.py:13
  7.1 9.0 %collective-permute-start.6 = (f32[64,2]{1,0:T(8,128)S(1)}, f32[64,2]{1,0:T(8,128)S(1)}, u32[]{:S(2)}, u32[]{:S(2)}) collective-permute-start(f32[64,2]{1,0:T(8,128)S(1)} %bitcast.83), channel_id=1, source_target_pairs={{0,12},{4,8},{8,4},{12,0},{1,13},{5,9},{9,5},{13,1},{2,14},{6,10},... | collective-permute-start | bytes 1544 | tf_op jit(solution)/shard_map/ppermute | solution.py:13
  11.3 4.8 %collective-permute-start.5 = (f32[64,2]{1,0:T(8,128)S(1)}, f32[64,2]{1,0:T(8,128)S(1)}, u32[]{:S(2)}, u32[]{:S(2)}) collective-permute-start(f32[64,2]{1,0:T(8,128)S(1)} %bitcast.84), channel_id=1, source_target_pairs={{0,8},{4,12},{8,0},{12,4},{1,9},{5,13},{9,1},{13,5},{2,10},{6,14},... | collective-permute-start | bytes 1544 | tf_op jit(solution)/shard_map/ppermute | solution.py:13
  11.3 4.8 %collective-permute-start.4 = (f32[64,2]{1,0:T(8,128)S(1)}, f32[64,2]{1,0:T(8,128)S(1)}, u32[]{:S(2)}, u32[]{:S(2)}) collective-permute-start(f32[64,2]{1,0:T(8,128)S(1)} %bitcast.85), channel_id=1, source_target_pairs={{0,4},{4,0},{8,12},{12,8},{1,5},{5,1},{9,13},{13,9},{2,6},{6,2},{1... | collective-permute-start | bytes 1544 | tf_op jit(solution)/shard_map/ppermute | solution.py:13
  12.0 4.4 %collective-permute-start.1 = (bf16[2,16,4608]{2,1,0:T(8,128)(2,1)S(1)}, bf16[2,16,4608]{2,1,0:T(8,128)(2,1)S(1)}, u32[]{:S(2)}, u32[]{:S(2)}) collective-permute-start(bf16[2,16,4608]{2,1,0:T(8,128)(2,1)S(1)} %maximum_bitcast_fusion.refs_0_), channel_id=1, source_target_pairs={{0,1},{1,0},{2,3},{3,2},{4,5},{5,4},{6,7},{7,6},{8,9},{9,8},{10,11... | collective-permute-start | bytes 884744 | tf_op jit(solution)/shard_map/ppermute | solution.py:13
  24.3 11.8 %collective-permute-start.9 = (f16[16,3200]{1,0:T(8,128)(2,1)S(1)}, f16[16,3200]{1,0:T(8,128)(2,1)S(1)}, u32[]{:S(2)}, u32[]{:S(2)}) collective-permute-start(f16[16,3200]{1,0:T(8,128)(2,1)S(1)} %get-tuple-element.80), channel_id=1, source_target_pairs={{0,8},{4,12},{8,0},{12,4},{1,9},{5,13},{9,1},{13,5},{2,10},{6,14},... | collective-permute-start | bytes 307208 | tf_op jit(solution)/shard_map/ppermute | solution.py:13
  26.6 9.4 %collective-permute-start.8 = (f16[16,3200]{1,0:T(8,128)(2,1)S(1)}, f16[16,3200]{1,0:T(8,128)(2,1)S(1)}, u32[]{:S(2)}, u32[]{:S(2)}) collective-permute-start(f16[16,3200]{1,0:T(8,128)(2,1)S(1)} %get-tuple-element.81), channel_id=1, source_target_pairs={{0,12},{4,8},{8,4},{12,0},{1,13},{5,9},{9,5},{13,1},{2,14},{6,10},... | collective-permute-start | bytes 307208 | tf_op jit(solution)/shard_map/ppermute | solution.py:13
  28.2 8.2 %collective-permute-start.7 = (f16[16,3200]{1,0:T(8,128)(2,1)S(1)}, f16[16,3200]{1,0:T(8,128)(2,1)S(1)}, u32[]{:S(2)}, u32[]{:S(2)}) collective-permute-start(f16[16,3200]{1,0:T(8,128)(2,1)S(1)} %get-tuple-element.82), channel_id=1, source_target_pairs={{0,4},{4,0},{8,12},{12,8},{1,5},{5,1},{9,13},{13,9},{2,6},{6,2},{1... | collective-permute-start | bytes 307208 | tf_op jit(solution)/shard_map/ppermute | solution.py:13
  36.5 3.9 %collective-permute-start.12 = (bf16[4,3200]{1,0:T(4,128)(2,1)S(1)}, bf16[4,3200]{1,0:T(4,128)(2,1)S(1)}, u32[]{:S(2)}, u32[]{:S(2)}) collective-permute-start(bf16[4,3200]{1,0:T(4,128)(2,1)S(1)} %get-tuple-element.87), channel_id=1, source_target_pairs={{0,2},{1,3},{2,0},{3,1},{4,6},{5,7},{6,4},{7,5},{8,10},{9,11},{10,... | collective-permute-start | bytes 76808 | tf_op jit(solution)/shard_map/ppermute | solution.py:13
  38.2 3.3 %collective-permute-start.11 = (bf16[4,3200]{1,0:T(4,128)(2,1)S(1)}, bf16[4,3200]{1,0:T(4,128)(2,1)S(1)}, u32[]{:S(2)}, u32[]{:S(2)}) collective-permute-start(bf16[4,3200]{1,0:T(4,128)(2,1)S(1)} %get-tuple-element.88), channel_id=1, source_target_pairs={{0,3},{1,2},{2,1},{3,0},{4,7},{5,6},{6,5},{7,4},{8,11},{9,10},{10,... | collective-permute-start | bytes 76808 | tf_op jit(solution)/shard_map/ppermute | solution.py:13
  38.2 3.3 %collective-permute-start.10 = (bf16[4,3200]{1,0:T(4,128)(2,1)S(1)}, bf16[4,3200]{1,0:T(4,128)(2,1)S(1)}, u32[]{:S(2)}, u32[]{:S(2)}) collective-permute-start(bf16[4,3200]{1,0:T(4,128)(2,1)S(1)} %get-tuple-element.89), channel_id=1, source_target_pairs={{0,1},{1,0},{2,3},{3,2},{4,5},{5,4},{6,7},{7,6},{8,9},{9,8},{10,11... | collective-permute-start | bytes 76808 | tf_op jit(solution)/shard_map/ppermute | solution.py:13
  43.9 4.1 %collective-permute-start.13 = (bf16[4,3072]{1,0:T(4,128)(2,1)S(1)}, bf16[4,3072]{1,0:T(4,128)(2,1)S(1)}, u32[]{:S(2)}, u32[]{:S(2)}) collective-permute-start(bf16[4,3072]{1,0:T(4,128)(2,1)S(1)} %bitcast.90), channel_id=1, source_target_pairs={{0,2},{1,3},{2,0},{3,1},{4,6},{5,7},{6,4},{7,5},{8,10},{9,11},{10,... | collective-permute-start | bytes 73736 | tf_op jit(solution)/shard_map/ppermute | solution.py:13
  44.6 3.5 %collective-permute-start.14 = (bf16[4,3072]{1,0:T(4,128)(2,1)S(1)}, bf16[4,3072]{1,0:T(4,128)(2,1)S(1)}, u32[]{:S(2)}, u32[]{:S(2)}) collective-permute-start(bf16[4,3072]{1,0:T(4,128)(2,1)S(1)} %bitcast.89), channel_id=1, source_target_pairs={{0,3},{1,2},{2,1},{3,0},{4,7},{5,6},{6,5},{7,4},{8,11},{9,10},{10,... | collective-permute-start | bytes 73736 | tf_op jit(solution)/shard_map/ppermute | solution.py:13
  44.6 3.5 %collective-permute-start.15 = (bf16[4,3072]{1,0:T(4,128)(2,1)S(1)}, bf16[4,3072]{1,0:T(4,128)(2,1)S(1)}, u32[]{:S(2)}, u32[]{:S(2)}) collective-permute-start(bf16[4,3072]{1,0:T(4,128)(2,1)S(1)} %bitcast.88), channel_id=1, source_target_pairs={{0,1},{1,0},{2,3},{3,2},{4,5},{5,4},{6,7},{7,6},{8,9},{9,8},{10,11... | collective-permute-start | bytes 73736 | tf_op jit(solution)/shard_map/ppermute | solution.py:13
  48.2 10.9 %collective-permute-start.18 = (bf16[16,3072]{1,0:T(8,128)(2,1)S(1)}, bf16[16,3072]{1,0:T(8,128)(2,1)S(1)}, u32[]{:S(2)}, u32[]{:S(2)}) collective-permute-start(bf16[16,3072]{1,0:T(8,128)(2,1)S(1)} %constant_dynamic-update-slice_fusion.4.passed_ref), channel_id=1, source_target_pairs={{0,8},{4,12},{8,0},{12,4},{1,9},{5,13},{9,1},{13,5},{2,10},{6,14},... | collective-permute-start | bytes 294920 | tf_op jit(solution)/shard_map/ppermute | solution.py:13
  51.4 7.7 %collective-permute-start.17 = (bf16[16,3072]{1,0:T(8,128)(2,1)S(1)}, bf16[16,3072]{1,0:T(8,128)(2,1)S(1)}, u32[]{:S(2)}, u32[]{:S(2)}) collective-permute-start(bf16[16,3072]{1,0:T(8,128)(2,1)S(1)} %constant_dynamic-update-slice_fusion.4.passed_ref), channel_id=1, source_target_pairs={{0,12},{4,8},{8,4},{12,0},{1,13},{5,9},{9,5},{13,1},{2,14},{6,10},... | collective-permute-start | bytes 294920 | tf_op jit(solution)/shard_map/ppermute | solution.py:13
  52.0 8.0 %collective-permute-start.16 = (bf16[16,3072]{1,0:T(8,128)(2,1)S(1)}, bf16[16,3072]{1,0:T(8,128)(2,1)S(1)}, u32[]{:S(2)}, u32[]{:S(2)}) collective-permute-start(bf16[16,3072]{1,0:T(8,128)(2,1)S(1)} %constant_dynamic-update-slice_fusion.4.passed_ref), channel_id=1, source_target_pairs={{0,4},{4,0},{8,12},{12,8},{1,5},{5,1},{9,13},{13,9},{2,6},{6,2},{1... | collective-permute-start | bytes 294920 | tf_op jit(solution)/shard_map/ppermute | solution.py:13
  63.6 3.7 %collective-permute-start.19 = (bf16[16,3072]{1,0:T(8,128)(2,1)S(1)}, bf16[16,3072]{1,0:T(8,128)(2,1)S(1)}, u32[]{:S(2)}, u32[]{:S(2)}) collective-permute-start(bf16[16,3072]{1,0:T(8,128)(2,1)S(1)} %get-tuple-element.69), channel_id=1, source_target_pairs={{0,1},{1,0},{2,3},{3,2},{4,5},{5,4},{6,7},{7,6},{8,9},{9,8},{10,11... | collective-permute-start | bytes 294920 | tf_op jit(solution)/shard_map/ppermute | solution.py:13
  63.7 5.7 %collective-permute-start.20 = (bf16[16,3072]{1,0:T(8,128)(2,1)S(1)}, bf16[16,3072]{1,0:T(8,128)(2,1)S(1)}, u32[]{:S(2)}, u32[]{:S(2)}) collective-permute-start(bf16[16,3072]{1,0:T(8,128)(2,1)S(1)} %get-tuple-element.71), channel_id=1, source_target_pairs={{0,2},{1,3},{2,0},{3,1},{4,6},{5,7},{6,4},{7,5},{8,10},{9,11},{10,... | collective-permute-start | bytes 294920 | tf_op jit(solution)/shard_map/ppermute | solution.py:13
  64.6 6.0 %collective-permute-start.21 = (bf16[16,3072]{1,0:T(8,128)(2,1)S(1)}, bf16[16,3072]{1,0:T(8,128)(2,1)S(1)}, u32[]{:S(2)}, u32[]{:S(2)}) collective-permute-start(bf16[16,3072]{1,0:T(8,128)(2,1)S(1)} %get-tuple-element.72), channel_id=1, source_target_pairs={{0,3},{1,2},{2,1},{3,0},{4,7},{5,6},{6,5},{7,4},{8,11},{9,10},{10,... | collective-permute-start | bytes 294920 | tf_op jit(solution)/shard_map/ppermute | solution.py:13
  67.3 3.3 %collective-permute-start.22 = (bf16[16,1536]{1,0:T(8,128)(2,1)S(1)}, bf16[16,1536]{1,0:T(8,128)(2,1)S(1)}, u32[]{:S(2)}, u32[]{:S(2)}) collective-permute-start(bf16[16,1536]{1,0:T(8,128)(2,1)S(1)} %get-tuple-element.74), channel_id=1, source_target_pairs={{0,1},{1,0},{2,3},{3,2},{4,5},{5,4},{6,7},{7,6},{8,9},{9,8},{10,11... | collective-permute-start | bytes 147464 | tf_op jit(solution)/shard_map/ppermute | solution.py:13
  67.8 4.8 %collective-permute-start.23 = (bf16[16,1536]{1,0:T(8,128)(2,1)S(1)}, bf16[16,1536]{1,0:T(8,128)(2,1)S(1)}, u32[]{:S(2)}, u32[]{:S(2)}) collective-permute-start(bf16[16,1536]{1,0:T(8,128)(2,1)S(1)} %get-tuple-element.75), channel_id=1, source_target_pairs={{0,2},{1,3},{2,0},{3,1},{4,6},{5,7},{6,4},{7,5},{8,10},{9,11},{10,... | collective-permute-start | bytes 147464 | tf_op jit(solution)/shard_map/ppermute | solution.py:13
  68.5 4.1 %collective-permute-start.24 = (bf16[16,1536]{1,0:T(8,128)(2,1)S(1)}, bf16[16,1536]{1,0:T(8,128)(2,1)S(1)}, u32[]{:S(2)}, u32[]{:S(2)}) collective-permute-start(bf16[16,1536]{1,0:T(8,128)(2,1)S(1)} %get-tuple-element.76), channel_id=1, source_target_pairs={{0,3},{1,2},{2,1},{3,0},{4,7},{5,6},{6,5},{7,4},{8,11},{9,10},{10,... | collective-permute-start | bytes 147464 | tf_op jit(solution)/shard_map/ppermute | solution.py:13
  (9 other events, 77.4 us)

commit v5 on v4

--- a/solution.py
+++ b/solution.py
@@ -6,7 +6,6 @@
 import jax.experimental.pallas.tpu as pltpu
 
 D = 18432
-WIRE_SCALE = 16.0
 
 
 def swap(x, axis, n, m):
@@ -23,20 +22,12 @@
 
 
 def order_of(n):
-    return far_first(n)[::-1]
+    return far_first(n)
 
 
 def exchange(parts, axis, n):
     back = {m: swap(parts[m], axis, n, m) for m in far_first(n)}
     return [parts[0]] + [back[m] for m in range(1, n)]
-
-
-def to_bfloat16(x):
-    return x.astype(jnp.bfloat16)
-
-
-def to_float32(x):
-    return x.astype(jnp.float32)
 
 
 def in_order(parts, axis):
@@ -156,7 +147,74 @@
     return [(c, min(size, cols - c)) for c in range(0, cols, size)]
 
 
-def project(x, w_head, w_all, w_last, last_cols, axis):
+def padded(cols):
+    return (cols + 127) // 128 * 128
+
+
+def code(block):
+    rows, cols = block.shape
+    lane = lax.broadcasted_iota(jnp.int32, (rows, 128), 1)
+    scales = jnp.zeros((rows, 128), jnp.int32)
+    coded = []
+    for g, (c, size) in enumerate(tiles(cols, 128)):
+        part = block[:, c : c + size]
+        top = jnp.maximum(jnp.max(jnp.abs(part), axis=1, keepdims=True), 1e-30)
+        level = jnp.floor(16.0 * jnp.log2(32000.0 / top))
+        coded.append(jnp.round(part * jnp.exp2(level * 0.0625)).astype(jnp.int32))
+        scales = jnp.where(lane == g, level.astype(jnp.int32), scales)
+        if size < 128:
+            coded.append(jnp.zeros((rows, 128 - size), jnp.int32))
+    return jnp.concatenate(coded + [scales], axis=1).astype(jnp.int16)
+
+
+def combine(sums):
+    rows = sums[0][0].shape[0]
+    widths = [own.shape[1] for own, _ in sums]
+
+    def body(*refs):
+        refs, out_ref = list(refs[:-1]), refs[-1]
+        at = 0
+        for own, others in sums:
+            own_ref = refs.pop(0)
+            other_refs = [refs.pop(0) for _ in others]
+            cols = own.shape[1]
+            scales = [
+                jnp.exp2(ref[:, padded(cols) :].astype(jnp.int32).astype(jnp.float32) * -0.0625)
+                for ref in other_refs
+            ]
+            for g, (c, size) in enumerate(tiles(cols, 128)):
+                total = own_ref[:, c : c + size]
+                for ref, scale in zip(other_refs, scales):
+                    value = ref[:, c : c + size].astype(jnp.int32).astype(jnp.float32)
+                    total = total + value * scale[:, g : g + 1]
+                out_ref[:, at + c : at + c + size] = total.astype(jnp.bfloat16)
+            at += cols
+
+    flat = [x for own, others in sums for x in [own, *others]]
+    return pl.pallas_call(
+        body,
+        out_shape=jax.ShapeDtypeStruct((rows, sum(widths)), jnp.bfloat16),
+        in_specs=[in_vmem()] * len(flat),
+        out_specs=in_vmem(),
+        compiler_params=pltpu.CompilerParams(vmem_limit_bytes=8 << 20),
+        name="combine",
+    )(*flat)
+
+
+def shares(total_ref, out_refs, axis, n):
+    me = lax.axis_index(axis)
+    rows = total_ref.shape[0] // n
+    for m, out_ref in enumerate(out_refs):
+        block = total_ref[pl.ds(pl.multiple_of((me ^ m) * rows, rows), rows), :]
+        out_ref[...] = code(block) if m else block
+
+
+def share_shapes(rows, cols, n):
+    kept = jax.ShapeDtypeStruct((rows // n, cols), jnp.float32)
+    return [kept] + [pltpu.VMEM((rows // n, padded(cols) + 128), jnp.int16)] * (n - 1)
+
+
+def project(x, w_head, w_all, w_last, last_cols, axis, share_axis, n):
     depth, cols = w_all.shape
     held = w_head.shape[1]
     rest = tiles(cols - held)
@@ -165,7 +223,8 @@
         start = lax.axis_index(axis) * last_cols
         w_last = lax.dynamic_slice_in_dim(w_last, start, last_cols, 1)
 
-    def body(x_ref, head_ref, all_ref, last_ref, out_ref, scratch, last_scratch, sems):
+    def body(x_ref, head_ref, all_ref, last_ref, *refs):
+        out_ref, scratch, last_scratch, sems = refs[-4:]
         start = 0
         if whole_tiles:
             start = pl.multiple_of(lax.axis_index(axis) * last_cols, 128)
@@ -187,15 +246,17 @@
         for copy, (c, size) in zip(copies, rest):
             copy.wait()
             out_ref[:, held + c : held + c + size] = dot_f32(x_ref[...], scratch[:, c : c + size])
+        shares(out_ref, refs[:-4], share_axis, n)
 
     rows = x.shape[0]
     in_hbm = pl.BlockSpec(memory_space=pltpu.HBM)
     return pl.pallas_call(
         body,
-        out_shape=jax.ShapeDtypeStruct((rows, cols + last_cols), jnp.float32),
+        out_shape=share_shapes(rows, cols + last_cols, n),
         in_specs=[in_vmem(), in_vmem(), in_hbm, in_hbm],
-        out_specs=in_vmem(),
+        out_specs=[in_vmem()] * n,
         scratch_shapes=[
+            pltpu.VMEM((rows, cols + last_cols), jnp.float32),
             pltpu.VMEM((depth, cols - held), w_all.dtype),
             pltpu.VMEM((depth, last_cols), w_last.dtype),
             pltpu.SemaphoreType.DMA((len(rest) + 1,)),
@@ -213,19 +274,6 @@
     )
 
 
-def shares(total_ref, out_refs, axis, n):
-    me = lax.axis_index(axis)
-    rows = total_ref.shape[0] // n
-    for m, out_ref in enumerate(out_refs):
-        block = total_ref[pl.ds(pl.multiple_of((me ^ m) * rows, rows), rows), :]
-        out_ref[...] = block.astype(out_ref.dtype)
-
-
-def share_shapes(rows, cols, n):
-    kept = jax.ShapeDtypeStruct((rows // n, cols), jnp.float32)
-    return [kept] + [pltpu.VMEM((rows // n, cols), jnp.bfloat16)] * (n - 1)
-
-
 def multiply_held(x, w, axis, n):
     rows, depth, cols = x.shape[0], x.shape[1], w.shape[1]
 
@@ -279,12 +327,6 @@
 
 
 def make(nx, ny):
-    def to_wire(x):
-        return (x * WIRE_SCALE).astype(jnp.float16)
-
-    def from_wire(x):
-        return x.astype(jnp.float32) * (1.0 / WIRE_SCALE)
-
     def shards(activations, ln_gain, w_query, w_keyval, w_out, k_cache, v_cache, cache_lengths):
         gy = lax.axis_index("gy")
         head_dim = k_cache.shape[2]
@@ -309,15 +351,13 @@
             * ln_gain.astype(jnp.float32)
         ).astype(jnp.bfloat16)
         kv_cols = w_keyval.shape[1] // ny
-        projected = project(normed, w_head, w_query, w_keyval, kv_cols, "gy")
+        projected = project(normed, w_head, w_query, w_keyval, kv_cols, "gy", "gx", nx)
         cut = whole_tiles(w_out.shape[1] * 11 // 16)
-        me = lax.axis_index("gx")
-        parts = [to_wire(rows_of(projected, me ^ m, nx)) for m in range(nx)]
-        parts = exchange(parts, "gx", nx)[1:]
-        w_right, part = set_aside(w_out, cut, rows_of(projected, me, nx))
+        parts = exchange(projected, "gx", nx)[1:]
+        w_right, part = set_aside(w_out, cut, projected[0])
         parts = [parts[m - 1] for m in order_of(nx)]
         parts, part = lax.optimization_barrier((parts, part))
-        part = sum((from_wire(x) for x in parts), part).astype(jnp.bfloat16)
+        part = combine([(part, parts)])
         mixed = exchange([rows_of(part, gy ^ m, ny) for m in range(ny)], "gy", ny)
         order = order_of(ny)
         arrived = lax.optimization_barrier([mixed[m] for m in order])
@@ -349,8 +389,7 @@
         right = multiply_held(everyone, w_right, "gy", ny)
         right, left[1] = lax.optimization_barrier((right, left[1]))
         right = exchange(right, "gy", ny)
-        outs = [sum((to_float32(x) for x in parts[1:]), parts[0]) for parts in (left, right)]
-        return jnp.concatenate([to_bfloat16(x) for x in outs], axis=1)
+        return combine([(parts[0], parts[1:]) for parts in (left, right)])
 
     return shards
 

time: 73.7 us -> 75.2 us (1.020)
  Pallas kernels: 26.8 us -> 29.2 us
  waiting for transfers between devices: 11.7 us -> 12.6 us
  other arithmetic: 2.63 us -> 1.73 us
  starting transfers between devices: 24.4 us -> 23.6 us
    pallas_call x1 -> x3, Pallas kernels: 7.37 us -> 9.08 us  [the longest x1 7.76 us: project(): pl.pallas_call(body, out_shape=share_shapes(rows, cols + last_cols, n), i...]
    ppermute x25, waiting for transfers between devices: 11.7 us -> 12.6 us  [swap(): return lax.ppermute(x, axis, [(k, k ^ m) for k in range(n)])]
    ppermute x25, starting transfers between devices: 24.4 us -> 23.6 us  [swap(): return lax.ppermute(x, axis, [(k, k ^ m) for k in range(n)])]
  transfers between devices with their start and end apart: 25 -> 25, of which waited for: 13 -> 12; matrix products, arithmetic and copies ran while one was open for 2% -> 2% of each run, Pallas kernels for 22% -> 22%
where the time goes in v5:
time: 75.2 us; the launch traced here: 74.9 us
  Pallas kernels  29.2 us (39%)
  starting transfers between devices  23.6 us (31%)
  waiting for transfers between devices  12.6 us (17%)
  local copies, waits for them, and re-layouts  5.83 us (8%)
  other arithmetic  1.73 us (2%)
  matrix products  1.48 us (2%)
    ppermute x25, starting transfers between devices, swap(): return lax.ppermute(x, axis, [(k, k ^ m) for k in range(n)])  23.6 us
    ppermute x25, waiting for transfers between devices, swap(): return lax.ppermute(x, axis, [(k, k ^ m) for k in range(n)])  12.6 us
    pallas_call x2, Pallas kernels, fetch(): pl.pallas_call(body, out_shape=[pltpu.VMEM((rows, cols), w.dtype), pltpu....  10.5 us
    pallas_call x1, Pallas kernels, project(): pl.pallas_call(body, out_shape=share_shapes(rows, cols + last_cols, n), i...  7.76 us
    pallas_call x2, Pallas kernels, multiply_held(): pl.pallas_call(body, out_shape=share_shapes(rows, cols, n), in_specs=[in_...  5.8 us
    unnamed x21, local copies, waits for them, and re-layouts  5.07 us
    pallas_call x1, Pallas kernels, set_aside(): pl.pallas_call(body, out_shape=[jax.ShapeDtypeStruct((rows, cols), w.dtyp...  3.69 us
  transfers between devices with their start and end apart: 25, of which 12 were waited for; matrix products, arithmetic and copies ran while one was open for 2% of the time, Pallas kernels for 22%

profile of v5, /device:TPU:0, one launch (start us, length us, event | category | flops | bytes accessed | tf_op | source)
XLA Modules:
  0.0 74.9 jit_solution(7950735647459806381)
XLA Ops:
  0.0 1.1 %copy-done.2 = bf16[16,4608]{1,0:T(8,128)(2,1)S(1)} copy-done((bf16[16,4608]{1,0:T(8,128)(2,1)S(1)}, bf16[16,4608]{1,0:T(8,128)(2,1)}, u32[]{:S(2)}) %copy-start.2) | copy-done | bytes 147480
  1.3 2.9 %collective-permute-start.2 = (f32[1,16,2]{1,2,0:T(2,128)S(1)}, f32[1,16,2]{1,2,0:T(2,128)S(1)}, u32[]{:S(2)}, u32[]{:S(2)}) collective-permute-start(f32[1,16,2]{1,2,0:T(2,128)S(1)} %bitcast.94), channel_id=1, source_target_pairs={{0,2},{1,3},{2,0},{3,1},{4,6},{5,7},{6,4},{7,5},{8,10},{9,11},{10,... | collective-permute-start | bytes 392 | tf_op jit(solution)/shard_map/ppermute | solution.py:12
  4.3 1.5 %collective-permute-done.2 = f32[1,16,2]{1,2,0:T(2,128)S(1)} collective-permute-done((f32[1,16,2]{1,2,0:T(2,128)S(1)}, f32[1,16,2]{1,2,0:T(2,128)S(1)}, u32[]{:S(2)}, u32[]{:S(2)}) %collective-permute-start.2) | collective-permute-done | bytes 160 | tf_op jit(solution)/shard_map/ppermute | solution.py:12
  7.1 2.1 %collective-permute-start.4 = (f32[64,2]{1,0:T(8,128)S(1)}, f32[64,2]{1,0:T(8,128)S(1)}, u32[]{:S(2)}, u32[]{:S(2)}) collective-permute-start(f32[64,2]{1,0:T(8,128)S(1)} %bitcast.83), channel_id=1, source_target_pairs={{0,4},{4,0},{8,12},{12,8},{1,5},{5,1},{9,13},{13,9},{2,6},{6,2},{1... | collective-permute-start | bytes 1544 | tf_op jit(solution)/shard_map/ppermute | solution.py:12
  9.2 2.6 %collective-permute-start.5 = (f32[64,2]{1,0:T(8,128)S(1)}, f32[64,2]{1,0:T(8,128)S(1)}, u32[]{:S(2)}, u32[]{:S(2)}) collective-permute-start(f32[64,2]{1,0:T(8,128)S(1)} %bitcast.84), channel_id=1, source_target_pairs={{0,8},{4,12},{8,0},{12,4},{1,9},{5,13},{9,1},{13,5},{2,10},{6,14},... | collective-permute-start | bytes 1544 | tf_op jit(solution)/shard_map/ppermute | solution.py:12
  12.0 4.0 %fetch.2 = (bf16[4608,1152]{1,0:T(8,128)(2,1)S(1)}, f32[64,2]{1,0:T(8,128)S(1)}) custom-call(bf16[4608,3072]{1,0:T(8,128)(2,1)} %all_ref.1, f32[64,2]{1,0:T(8,128)S(1)} %bitcast.86, bf16[2,16,4608]{2,1,0:T(8,128)(2,1)S(1)} %maximum_bitcast_fusion.refs_0_), custom_call_target="tpu_custom_call" | custom-call | bytes 10616832 | tf_op jit(solution)/shard_map/fetch/pallas_call | solution.py:102
  16.0 1.5 %collective-permute-done.6 = f32[64,2]{1,0:T(8,128)S(1)} collective-permute-done((f32[64,2]{1,0:T(8,128)S(1)}, f32[64,2]{1,0:T(8,128)S(1)}, u32[]{:S(2)}, u32[]{:S(2)}) %collective-permute-start.6) | collective-permute-done | bytes 544 | tf_op jit(solution)/shard_map/ppermute | solution.py:12
  18.2 7.8 %project.1 = (f32[16,3200]{1,0:T(8,128)S(1)}, s16[16,3328]{1,0:T(8,128)(2,1)S(1)}, s16[16,3328]{1,0:T(8,128)(2,1)S(1)}, s16[16,3328]{1,0:T(8,128)(2,1)S(1)}) custom-call(bf16[64,4608]{1,0:T(8,128)(2,1)S(1)} %fusion.3.x_ref, bf16[4608,1152]{1,0:T(8,128)(2,1)S(1)} %get-tuple-element.52.head_ref, bf16[4608,3072]{1,0:T(8,128)(2,1)} %all_ref.1, ...), custom_call_target="tpu_custom_call" | custom-call | flops 1811939328 | bytes 28311552 | tf_op jit(solution)/shard_map/project/pallas_call | solution.py:253
  26.5 2.0 %collective-permute-start.8 = (s16[16,3328]{1,0:T(8,128)(2,1)S(1)}, s16[16,3328]{1,0:T(8,128)(2,1)S(1)}, u32[]{:S(2)}, u32[]{:S(2)}) collective-permute-start(s16[16,3328]{1,0:T(8,128)(2,1)S(1)} %get-tuple-element.54), channel_id=1, source_target_pairs={{0,12},{4,8},{8,4},{12,0},{1,13},{5,9},{9,5},{13,1},{2,14},{6,10},... | collective-permute-start | bytes 319496 | tf_op jit(solution)/shard_map/ppermute | solution.py:12
  28.5 1.1 %collective-permute-start.9 = (s16[16,3328]{1,0:T(8,128)(2,1)S(1)}, s16[16,3328]{1,0:T(8,128)(2,1)S(1)}, u32[]{:S(2)}, u32[]{:S(2)}) collective-permute-start(s16[16,3328]{1,0:T(8,128)(2,1)S(1)} %get-tuple-element.55), channel_id=1, source_target_pairs={{0,4},{4,0},{8,12},{12,8},{1,5},{5,1},{9,13},{13,9},{2,6},{6,2},{1... | collective-permute-start | bytes 319496 | tf_op jit(solution)/shard_map/ppermute | solution.py:12
  29.6 3.7 %set_aside.1 = (bf16[3072,1536]{1,0:T(8,128)(2,1)S(1)}, f32[16,3200]{1,0:T(8,128)S(1)}) custom-call(bf16[3072,4608]{1,0:T(8,128)(2,1)} %w_ref.5, f32[16,3200]{1,0:T(8,128)S(1)} %get-tuple-element.56.passed_ref), custom_call_target="tpu_custom_call" | custom-call | bytes 18874368 | tf_op jit(solution)/shard_map/set_aside/pallas_call | solution.py:129
  33.3 3.6 %copy-done.1 = bf16[3072,1536]{1,0:T(8,128)(2,1)} copy-done((bf16[3072,1536]{1,0:T(8,128)(2,1)}, bf16[3072,1536]{1,0:T(8,128)(2,1)S(1)}, u32[]{:S(2)}) %copy-start.1) | copy-done | bytes 9437208
  37.3 1.7 %collective-permute-start.10 = (bf16[4,3200]{1,0:T(4,128)(2,1)S(1)}, bf16[4,3200]{1,0:T(4,128)(2,1)S(1)}, u32[]{:S(2)}, u32[]{:S(2)}) collective-permute-start(bf16[4,3200]{1,0:T(4,128)(2,1)S(1)} %get-tuple-element.93), channel_id=1, source_target_pairs={{0,2},{1,3},{2,0},{3,1},{4,6},{5,7},{6,4},{7,5},{8,10},{9,11},{10,... | collective-permute-start | bytes 76808 | tf_op jit(solution)/shard_map/ppermute | solution.py:12
  39.7 1.6 %collective-permute-done.10 = bf16[4,3200]{1,0:T(4,128)(2,1)S(1)} collective-permute-done((bf16[4,3200]{1,0:T(4,128)(2,1)S(1)}, bf16[4,3200]{1,0:T(4,128)(2,1)S(1)}, u32[]{:S(2)}, u32[]{:S(2)}) %collective-permute-start.10) | collective-permute-done | bytes 25632 | tf_op jit(solution)/shard_map/ppermute | solution.py:12
  45.5 1.5 %collective-permute-start.15 = (bf16[4,3072]{1,0:T(4,128)(2,1)S(1)}, bf16[4,3072]{1,0:T(4,128)(2,1)S(1)}, u32[]{:S(2)}, u32[]{:S(2)}) collective-permute-start(bf16[4,3072]{1,0:T(4,128)(2,1)S(1)} %bitcast.88), channel_id=1, source_target_pairs={{0,1},{1,0},{2,3},{3,2},{4,5},{5,4},{6,7},{7,6},{8,9},{9,8},{10,11... | collective-permute-start | bytes 73736 | tf_op jit(solution)/shard_map/ppermute | solution.py:12
  47.0 1.5 %collective-permute-done.13 = bf16[4,3072]{1,0:T(4,128)(2,1)S(1)} collective-permute-done((bf16[4,3072]{1,0:T(4,128)(2,1)S(1)}, bf16[4,3072]{1,0:T(4,128)(2,1)S(1)}, u32[]{:S(2)}, u32[]{:S(2)}) %collective-permute-start.13) | collective-permute-done | bytes 24608 | tf_op jit(solution)/shard_map/ppermute | solution.py:12
  49.0 2.7 %collective-permute-start.16 = (bf16[16,3072]{1,0:T(8,128)(2,1)S(1)}, bf16[16,3072]{1,0:T(8,128)(2,1)S(1)}, u32[]{:S(2)}, u32[]{:S(2)}) collective-permute-start(bf16[16,3072]{1,0:T(8,128)(2,1)S(1)} %constant_dynamic-update-slice_fusion.4.passed_ref), channel_id=1, source_target_pairs={{0,8},{4,12},{8,0},{12,4},{1,9},{5,13},{9,1},{13,5},{2,10},{6,14},... | collective-permute-start | bytes 294920 | tf_op jit(solution)/shard_map/ppermute | solution.py:12
  51.8 1.1 %collective-permute-start.17 = (bf16[16,3072]{1,0:T(8,128)(2,1)S(1)}, bf16[16,3072]{1,0:T(8,128)(2,1)S(1)}, u32[]{:S(2)}, u32[]{:S(2)}) collective-permute-start(bf16[16,3072]{1,0:T(8,128)(2,1)S(1)} %constant_dynamic-update-slice_fusion.4.passed_ref), channel_id=1, source_target_pairs={{0,12},{4,8},{8,4},{12,0},{1,13},{5,9},{9,5},{13,1},{2,14},{6,10},... | collective-permute-start | bytes 294920 | tf_op jit(solution)/shard_map/ppermute | solution.py:12
  52.8 6.4 %fetch.3 = (bf16[3072,3072]{1,0:T(8,128)(2,1)S(1)}, bf16[16,3072]{1,0:T(8,128)(2,1)S(1)}) custom-call(bf16[3072,4608]{1,0:T(8,128)(2,1)} %w_ref.5, bf16[16,3072]{1,0:T(8,128)(2,1)S(1)} %constant_dynamic-update-slice_fusion.4.passed_ref), custom_call_target="tpu_custom_call" | custom-call | bytes 18874368 | tf_op jit(solution)/shard_map/fetch/pallas_call | solution.py:102
  60.6 3.8 %multiply_held.2 = (f32[16,3072]{1,0:T(8,128)S(1)}, s16[16,3200]{1,0:T(8,128)(2,1)S(1)}, s16[16,3200]{1,0:T(8,128)(2,1)S(1)}, s16[16,3200]{1,0:T(8,128)(2,1)S(1)}) custom-call(bf16[64,3072]{1,0:T(8,128)(2,1)S(1)} %constant_dynamic-update-slice_fusion.x_ref, bf16[3072,3072]{1,0:T(8,128)(2,1)S(1)} %get-tuple-element.70.w_ref), custom_call_target="tpu_custom_call" | custom-call | flops 1207959552 | bytes 18874368 | tf_op jit(solution)/shard_map/multiply_held/pallas_call | solution.py:286
  65.2 1.1 %collective-permute-start.21 = (s16[16,3200]{1,0:T(8,128)(2,1)S(1)}, s16[16,3200]{1,0:T(8,128)(2,1)S(1)}, u32[]{:S(2)}, u32[]{:S(2)}) collective-permute-start(s16[16,3200]{1,0:T(8,128)(2,1)S(1)} %get-tuple-element.80), channel_id=1, source_target_pairs={{0,3},{1,2},{2,1},{3,0},{4,7},{5,6},{6,5},{7,4},{8,11},{9,10},{10,... | collective-permute-start | bytes 307208 | tf_op jit(solution)/shard_map/ppermute | solution.py:12
  66.3 2.0 %multiply_held.3 = (f32[16,1536]{1,0:T(8,128)S(1)}, s16[16,1664]{1,0:T(8,128)(2,1)S(1)}, s16[16,1664]{1,0:T(8,128)(2,1)S(1)}, s16[16,1664]{1,0:T(8,128)(2,1)S(1)}) custom-call(bf16[64,3072]{1,0:T(8,128)(2,1)S(1)} %constant_dynamic-update-slice_fusion.x_ref, bf16[3072,1536]{1,0:T(8,128)(2,1)S(1)} %bitcast.81), custom_call_target="tpu_custom_call" | custom-call | flops 603979776 | bytes 9437184 | tf_op jit(solution)/shard_map/multiply_held/pallas_call | solution.py:286
  70.3 1.2 %collective-permute-done.21.refs_3_ = s16[16,3200]{1,0:T(8,128)(2,1)S(1)} collective-permute-done((s16[16,3200]{1,0:T(8,128)(2,1)S(1)}, s16[16,3200]{1,0:T(8,128)(2,1)S(1)}, u32[]{:S(2)}, u32[]{:S(2)}) %collective-permute-start.21) | collective-permute-done | bytes 102432 | tf_op jit(solution)/shard_map/ppermute | solution.py:12
  71.5 2.0 %collective-permute-done.23.refs_6_ = s16[16,1664]{1,0:T(8,128)(2,1)S(1)} collective-permute-done((s16[16,1664]{1,0:T(8,128)(2,1)S(1)}, s16[16,1664]{1,0:T(8,128)(2,1)S(1)}, u32[]{:S(2)}, u32[]{:S(2)}) %collective-permute-start.23) | collective-permute-done | bytes 53280 | tf_op jit(solution)/shard_map/ppermute | solution.py:12
  (104 shorter events, 14.1 us)
Async XLA Ops:
  1.3 4.5 %collective-permute-start.2 = (f32[1,16,2]{1,2,0:T(2,128)S(1)}, f32[1,16,2]{1,2,0:T(2,128)S(1)}, u32[]{:S(2)}, u32[]{:S(2)}) collective-permute-start(f32[1,16,2]{1,2,0:T(2,128)S(1)} %bitcast.94), channel_id=1, source_target_pairs={{0,2},{1,3},{2,0},{3,1},{4,6},{5,7},{6,4},{7,5},{8,10},{9,11},{10,... | collective-permute-start | bytes 392 | tf_op jit(solution)/shard_map/ppermute | solution.py:12
  4.2 7.6 %collective-permute-start = (bf16[1,16,4608]{2,1,0:T(8,128)(2,1)S(1)}, bf16[1,16,4608]{2,1,0:T(8,128)(2,1)S(1)}, u32[]{:S(2)}, u32[]{:S(2)}) collective-permute-start(bf16[1,16,4608]{2,1,0:T(8,128)(2,1)S(1)} %bitcast.82), channel_id=1, source_target_pairs={{0,2},{1,3},{2,0},{3,1},{4,6},{5,7},{6,4},{7,5},{8,10},{9,11},{10,... | collective-permute-start | bytes 442376 | tf_op jit(solution)/shard_map/ppermute | solution.py:12
  7.1 8.9 %collective-permute-start.4 = (f32[64,2]{1,0:T(8,128)S(1)}, f32[64,2]{1,0:T(8,128)S(1)}, u32[]{:S(2)}, u32[]{:S(2)}) collective-permute-start(f32[64,2]{1,0:T(8,128)S(1)} %bitcast.83), channel_id=1, source_target_pairs={{0,4},{4,0},{8,12},{12,8},{1,5},{5,1},{9,13},{13,9},{2,6},{6,2},{1... | collective-permute-start | bytes 1544 | tf_op jit(solution)/shard_map/ppermute | solution.py:12
  9.2 6.8 %collective-permute-start.5 = (f32[64,2]{1,0:T(8,128)S(1)}, f32[64,2]{1,0:T(8,128)S(1)}, u32[]{:S(2)}, u32[]{:S(2)}) collective-permute-start(f32[64,2]{1,0:T(8,128)S(1)} %bitcast.84), channel_id=1, source_target_pairs={{0,8},{4,12},{8,0},{12,4},{1,9},{5,13},{9,1},{13,5},{2,10},{6,14},... | collective-permute-start | bytes 1544 | tf_op jit(solution)/shard_map/ppermute | solution.py:12
  11.8 5.7 %collective-permute-start.6 = (f32[64,2]{1,0:T(8,128)S(1)}, f32[64,2]{1,0:T(8,128)S(1)}, u32[]{:S(2)}, u32[]{:S(2)}) collective-permute-start(f32[64,2]{1,0:T(8,128)S(1)} %bitcast.85), channel_id=1, source_target_pairs={{0,12},{4,8},{8,4},{12,0},{1,13},{5,9},{9,5},{13,1},{2,14},{6,10},... | collective-permute-start | bytes 1544 | tf_op jit(solution)/shard_map/ppermute | solution.py:12
  11.9 5.8 %collective-permute-start.1 = (bf16[2,16,4608]{2,1,0:T(8,128)(2,1)S(1)}, bf16[2,16,4608]{2,1,0:T(8,128)(2,1)S(1)}, u32[]{:S(2)}, u32[]{:S(2)}) collective-permute-start(bf16[2,16,4608]{2,1,0:T(8,128)(2,1)S(1)} %maximum_bitcast_fusion.refs_0_), channel_id=1, source_target_pairs={{0,1},{1,0},{2,3},{3,2},{4,5},{5,4},{6,7},{7,6},{8,9},{9,8},{10,11... | collective-permute-start | bytes 884744 | tf_op jit(solution)/shard_map/ppermute | solution.py:12
  26.0 11.0 %collective-permute-start.7 = (s16[16,3328]{1,0:T(8,128)(2,1)S(1)}, s16[16,3328]{1,0:T(8,128)(2,1)S(1)}, u32[]{:S(2)}, u32[]{:S(2)}) collective-permute-start(s16[16,3328]{1,0:T(8,128)(2,1)S(1)} %get-tuple-element.53), channel_id=1, source_target_pairs={{0,8},{4,12},{8,0},{12,4},{1,9},{5,13},{9,1},{13,5},{2,10},{6,14},... | collective-permute-start | bytes 319496 | tf_op jit(solution)/shard_map/ppermute | solution.py:12
  26.5 10.5 %collective-permute-start.8 = (s16[16,3328]{1,0:T(8,128)(2,1)S(1)}, s16[16,3328]{1,0:T(8,128)(2,1)S(1)}, u32[]{:S(2)}, u32[]{:S(2)}) collective-permute-start(s16[16,3328]{1,0:T(8,128)(2,1)S(1)} %get-tuple-element.54), channel_id=1, source_target_pairs={{0,12},{4,8},{8,4},{12,0},{1,13},{5,9},{9,5},{13,1},{2,14},{6,10},... | collective-permute-start | bytes 319496 | tf_op jit(solution)/shard_map/ppermute | solution.py:12
  28.5 8.5 %collective-permute-start.9 = (s16[16,3328]{1,0:T(8,128)(2,1)S(1)}, s16[16,3328]{1,0:T(8,128)(2,1)S(1)}, u32[]{:S(2)}, u32[]{:S(2)}) collective-permute-start(s16[16,3328]{1,0:T(8,128)(2,1)S(1)} %get-tuple-element.55), channel_id=1, source_target_pairs={{0,4},{4,0},{8,12},{12,8},{1,5},{5,1},{9,13},{13,9},{2,6},{6,2},{1... | collective-permute-start | bytes 319496 | tf_op jit(solution)/shard_map/ppermute | solution.py:12
  37.3 3.9 %collective-permute-start.10 = (bf16[4,3200]{1,0:T(4,128)(2,1)S(1)}, bf16[4,3200]{1,0:T(4,128)(2,1)S(1)}, u32[]{:S(2)}, u32[]{:S(2)}) collective-permute-start(bf16[4,3200]{1,0:T(4,128)(2,1)S(1)} %get-tuple-element.93), channel_id=1, source_target_pairs={{0,2},{1,3},{2,0},{3,1},{4,6},{5,7},{6,4},{7,5},{8,10},{9,11},{10,... | collective-permute-start | bytes 76808 | tf_op jit(solution)/shard_map/ppermute | solution.py:12
  39.0 3.3 %collective-permute-start.11 = (bf16[4,3200]{1,0:T(4,128)(2,1)S(1)}, bf16[4,3200]{1,0:T(4,128)(2,1)S(1)}, u32[]{:S(2)}, u32[]{:S(2)}) collective-permute-start(bf16[4,3200]{1,0:T(4,128)(2,1)S(1)} %get-tuple-element.92), channel_id=1, source_target_pairs={{0,3},{1,2},{2,1},{3,0},{4,7},{5,6},{6,5},{7,4},{8,11},{9,10},{10,... | collective-permute-start | bytes 76808 | tf_op jit(solution)/shard_map/ppermute | solution.py:12
  39.0 3.3 %collective-permute-start.12 = (bf16[4,3200]{1,0:T(4,128)(2,1)S(1)}, bf16[4,3200]{1,0:T(4,128)(2,1)S(1)}, u32[]{:S(2)}, u32[]{:S(2)}) collective-permute-start(bf16[4,3200]{1,0:T(4,128)(2,1)S(1)} %get-tuple-element.91), channel_id=1, source_target_pairs={{0,1},{1,0},{2,3},{3,2},{4,5},{5,4},{6,7},{7,6},{8,9},{9,8},{10,11... | collective-permute-start | bytes 76808 | tf_op jit(solution)/shard_map/ppermute | solution.py:12
  44.6 3.9 %collective-permute-start.13 = (bf16[4,3072]{1,0:T(4,128)(2,1)S(1)}, bf16[4,3072]{1,0:T(4,128)(2,1)S(1)}, u32[]{:S(2)}, u32[]{:S(2)}) collective-permute-start(bf16[4,3072]{1,0:T(4,128)(2,1)S(1)} %bitcast.90), channel_id=1, source_target_pairs={{0,2},{1,3},{2,0},{3,1},{4,6},{5,7},{6,4},{7,5},{8,10},{9,11},{10,... | collective-permute-start | bytes 73736 | tf_op jit(solution)/shard_map/ppermute | solution.py:12
  45.4 3.6 %collective-permute-start.14 = (bf16[4,3072]{1,0:T(4,128)(2,1)S(1)}, bf16[4,3072]{1,0:T(4,128)(2,1)S(1)}, u32[]{:S(2)}, u32[]{:S(2)}) collective-permute-start(bf16[4,3072]{1,0:T(4,128)(2,1)S(1)} %bitcast.89), channel_id=1, source_target_pairs={{0,3},{1,2},{2,1},{3,0},{4,7},{5,6},{6,5},{7,4},{8,11},{9,10},{10,... | collective-permute-start | bytes 73736 | tf_op jit(solution)/shard_map/ppermute | solution.py:12
  45.5 3.5 %collective-permute-start.15 = (bf16[4,3072]{1,0:T(4,128)(2,1)S(1)}, bf16[4,3072]{1,0:T(4,128)(2,1)S(1)}, u32[]{:S(2)}, u32[]{:S(2)}) collective-permute-start(bf16[4,3072]{1,0:T(4,128)(2,1)S(1)} %bitcast.88), channel_id=1, source_target_pairs={{0,1},{1,0},{2,3},{3,2},{4,5},{5,4},{6,7},{7,6},{8,9},{9,8},{10,11... | collective-permute-start | bytes 73736 | tf_op jit(solution)/shard_map/ppermute | solution.py:12
  49.0 10.9 %collective-permute-start.16 = (bf16[16,3072]{1,0:T(8,128)(2,1)S(1)}, bf16[16,3072]{1,0:T(8,128)(2,1)S(1)}, u32[]{:S(2)}, u32[]{:S(2)}) collective-permute-start(bf16[16,3072]{1,0:T(8,128)(2,1)S(1)} %constant_dynamic-update-slice_fusion.4.passed_ref), channel_id=1, source_target_pairs={{0,8},{4,12},{8,0},{12,4},{1,9},{5,13},{9,1},{13,5},{2,10},{6,14},... | collective-permute-start | bytes 294920 | tf_op jit(solution)/shard_map/ppermute | solution.py:12
  51.8 8.1 %collective-permute-start.17 = (bf16[16,3072]{1,0:T(8,128)(2,1)S(1)}, bf16[16,3072]{1,0:T(8,128)(2,1)S(1)}, u32[]{:S(2)}, u32[]{:S(2)}) collective-permute-start(bf16[16,3072]{1,0:T(8,128)(2,1)S(1)} %constant_dynamic-update-slice_fusion.4.passed_ref), channel_id=1, source_target_pairs={{0,12},{4,8},{8,4},{12,0},{1,13},{5,9},{9,5},{13,1},{2,14},{6,10},... | collective-permute-start | bytes 294920 | tf_op jit(solution)/shard_map/ppermute | solution.py:12
  52.8 7.6 %collective-permute-start.18 = (bf16[16,3072]{1,0:T(8,128)(2,1)S(1)}, bf16[16,3072]{1,0:T(8,128)(2,1)S(1)}, u32[]{:S(2)}, u32[]{:S(2)}) collective-permute-start(bf16[16,3072]{1,0:T(8,128)(2,1)S(1)} %constant_dynamic-update-slice_fusion.4.passed_ref), channel_id=1, source_target_pairs={{0,4},{4,0},{8,12},{12,8},{1,5},{5,1},{9,13},{13,9},{2,6},{6,2},{1... | collective-permute-start | bytes 294920 | tf_op jit(solution)/shard_map/ppermute | solution.py:12
  64.4 4.0 %collective-permute-start.19 = (s16[16,3200]{1,0:T(8,128)(2,1)S(1)}, s16[16,3200]{1,0:T(8,128)(2,1)S(1)}, u32[]{:S(2)}, u32[]{:S(2)}) collective-permute-start(s16[16,3200]{1,0:T(8,128)(2,1)S(1)} %get-tuple-element.77), channel_id=1, source_target_pairs={{0,1},{1,0},{2,3},{3,2},{4,5},{5,4},{6,7},{7,6},{8,9},{9,8},{10,11... | collective-permute-start | bytes 307208 | tf_op jit(solution)/shard_map/ppermute | solution.py:12
  64.5 5.8 %collective-permute-start.20 = (s16[16,3200]{1,0:T(8,128)(2,1)S(1)}, s16[16,3200]{1,0:T(8,128)(2,1)S(1)}, u32[]{:S(2)}, u32[]{:S(2)}) collective-permute-start(s16[16,3200]{1,0:T(8,128)(2,1)S(1)} %get-tuple-element.79), channel_id=1, source_target_pairs={{0,2},{1,3},{2,0},{3,1},{4,6},{5,7},{6,4},{7,5},{8,10},{9,11},{10,... | collective-permute-start | bytes 307208 | tf_op jit(solution)/shard_map/ppermute | solution.py:12
  65.2 6.3 %collective-permute-start.21 = (s16[16,3200]{1,0:T(8,128)(2,1)S(1)}, s16[16,3200]{1,0:T(8,128)(2,1)S(1)}, u32[]{:S(2)}, u32[]{:S(2)}) collective-permute-start(s16[16,3200]{1,0:T(8,128)(2,1)S(1)} %get-tuple-element.80), channel_id=1, source_target_pairs={{0,3},{1,2},{2,1},{3,0},{4,7},{5,6},{6,5},{7,4},{8,11},{9,10},{10,... | collective-permute-start | bytes 307208 | tf_op jit(solution)/shard_map/ppermute | solution.py:12
  68.4 3.1 %collective-permute-start.22 = (s16[16,1664]{1,0:T(8,128)(2,1)S(1)}, s16[16,1664]{1,0:T(8,128)(2,1)S(1)}, u32[]{:S(2)}, u32[]{:S(2)}) collective-permute-start(s16[16,1664]{1,0:T(8,128)(2,1)S(1)} %get-tuple-element.82), channel_id=1, source_target_pairs={{0,1},{1,0},{2,3},{3,2},{4,5},{5,4},{6,7},{7,6},{8,9},{9,8},{10,11... | collective-permute-start | bytes 159752 | tf_op jit(solution)/shard_map/ppermute | solution.py:12
  68.8 4.7 %collective-permute-start.23 = (s16[16,1664]{1,0:T(8,128)(2,1)S(1)}, s16[16,1664]{1,0:T(8,128)(2,1)S(1)}, u32[]{:S(2)}, u32[]{:S(2)}) collective-permute-start(s16[16,1664]{1,0:T(8,128)(2,1)S(1)} %get-tuple-element.83), channel_id=1, source_target_pairs={{0,2},{1,3},{2,0},{3,1},{4,6},{5,7},{6,4},{7,5},{8,10},{9,11},{10,... | collective-permute-start | bytes 159752 | tf_op jit(solution)/shard_map/ppermute | solution.py:12
  69.5 4.4 %collective-permute-start.24 = (s16[16,1664]{1,0:T(8,128)(2,1)S(1)}, s16[16,1664]{1,0:T(8,128)(2,1)S(1)}, u32[]{:S(2)}, u32[]{:S(2)}) collective-permute-start(s16[16,1664]{1,0:T(8,128)(2,1)S(1)} %get-tuple-element.84), channel_id=1, source_target_pairs={{0,3},{1,2},{2,1},{3,0},{4,7},{5,6},{6,5},{7,4},{8,11},{9,10},{10,... | collective-permute-start | bytes 159752 | tf_op jit(solution)/shard_map/ppermute | solution.py:12
  (9 other events, 78.7 us)

commit v6 on v5

--- a/solution.py
+++ b/solution.py
@@ -178,6 +178,13 @@
             own_ref = refs.pop(0)
             other_refs = [refs.pop(0) for _ in others]
             cols = own.shape[1]
+            if others[0].dtype == jnp.bfloat16:
+                total = own_ref[...]
+                for ref in other_refs:
+                    total = total + ref[...].astype(jnp.float32)
+                out_ref[:, at : at + cols] = total.astype(jnp.bfloat16)
+                at += cols
+                continue
             scales = [
                 jnp.exp2(ref[:, padded(cols) :].astype(jnp.int32).astype(jnp.float32) * -0.0625)
                 for ref in other_refs
@@ -206,12 +213,17 @@
     rows = total_ref.shape[0] // n
     for m, out_ref in enumerate(out_refs):
         block = total_ref[pl.ds(pl.multiple_of((me ^ m) * rows, rows), rows), :]
-        out_ref[...] = code(block) if m else block
-
-
-def share_shapes(rows, cols, n):
+        if m:
+            block = code(block) if out_ref.dtype == jnp.int16 else block.astype(out_ref.dtype)
+        out_ref[...] = block
+
+
+def share_shapes(rows, cols, n, coded):
     kept = jax.ShapeDtypeStruct((rows // n, cols), jnp.float32)
-    return [kept] + [pltpu.VMEM((rows // n, padded(cols) + 128), jnp.int16)] * (n - 1)
+    sent = pltpu.VMEM((rows // n, cols), jnp.bfloat16)
+    if coded:
+        sent = pltpu.VMEM((rows // n, padded(cols) + 128), jnp.int16)
+    return [kept] + [sent] * (n - 1)
 
 
 def project(x, w_head, w_all, w_last, last_cols, axis, share_axis, n):
@@ -252,7 +264,7 @@
     in_hbm = pl.BlockSpec(memory_space=pltpu.HBM)
     return pl.pallas_call(
         body,
-        out_shape=share_shapes(rows, cols + last_cols, n),
+        out_shape=share_shapes(rows, cols + last_cols, n, True),
         in_specs=[in_vmem(), in_vmem(), in_hbm, in_hbm],
         out_specs=[in_vmem()] * n,
         scratch_shapes=[
@@ -285,7 +297,7 @@
 
     return pl.pallas_call(
         body,
-        out_shape=share_shapes(rows, cols, n),
+        out_shape=share_shapes(rows, cols, n, False),
         in_specs=[in_vmem(), in_vmem()],
         out_specs=[in_vmem()] * n,
         scratch_shapes=[pltpu.VMEM((rows, cols), jnp.float32)],

time: 75.2 us -> 74.1 us (0.985)
  Pallas kernels: 29.2 us -> 28.2 us
  transfers between devices with their start and end apart: 25 -> 25, of which waited for: 12 -> 13; matrix products, arithmetic and copies ran while one was open for 2% -> 2% of each run, Pallas kernels for 22% -> 22%
where the time goes in v6:
time: 74.1 us; the launch traced here: 73.8 us
  Pallas kernels  28.2 us (38%)
  starting transfers between devices  23.6 us (32%)
  waiting for transfers between devices  12.5 us (17%)
  local copies, waits for them, and re-layouts  5.83 us (8%)
  other arithmetic  1.73 us (2%)
  matrix products  1.48 us (2%)
    ppermute x25, starting transfers between devices, swap(): return lax.ppermute(x, axis, [(k, k ^ m) for k in range(n)])  23.6 us
    ppermute x25, waiting for transfers between devices, swap(): return lax.ppermute(x, axis, [(k, k ^ m) for k in range(n)])  12.5 us
    pallas_call x2, Pallas kernels, fetch(): pl.pallas_call(body, out_shape=[pltpu.VMEM((rows, cols), w.dtype), pltpu....  10.5 us
    pallas_call x1, Pallas kernels, project(): pl.pallas_call(body, out_shape=share_shapes(rows, cols + last_cols, n, Tr...  7.76 us
    pallas_call x2, Pallas kernels, multiply_held(): pl.pallas_call(body, out_shape=share_shapes(rows, cols, n, False), in_spe...  5.18 us
    unnamed x21, local copies, waits for them, and re-layouts  5.07 us
    pallas_call x1, Pallas kernels, set_aside(): pl.pallas_call(body, out_shape=[jax.ShapeDtypeStruct((rows, cols), w.dtyp...  3.69 us
  transfers between devices with their start and end apart: 25, of which 13 were waited for; matrix products, arithmetic and copies ran while one was open for 2% of the time, Pallas kernels for 22%

profile of v6, /device:TPU:0, one launch (start us, length us, event | category | flops | bytes accessed | tf_op | source)
XLA Modules:
  0.0 73.8 jit_solution(7939902103696205187)
XLA Ops:
  0.0 1.1 %copy-done.2 = bf16[16,4608]{1,0:T(8,128)(2,1)S(1)} copy-done((bf16[16,4608]{1,0:T(8,128)(2,1)S(1)}, bf16[16,4608]{1,0:T(8,128)(2,1)}, u32[]{:S(2)}) %copy-start.2) | copy-done | bytes 147480
  1.3 2.9 %collective-permute-start.2 = (f32[1,16,2]{1,2,0:T(2,128)S(1)}, f32[1,16,2]{1,2,0:T(2,128)S(1)}, u32[]{:S(2)}, u32[]{:S(2)}) collective-permute-start(f32[1,16,2]{1,2,0:T(2,128)S(1)} %bitcast.94), channel_id=1, source_target_pairs={{0,2},{1,3},{2,0},{3,1},{4,6},{5,7},{6,4},{7,5},{8,10},{9,11},{10,... | collective-permute-start | bytes 392 | tf_op jit(solution)/shard_map/ppermute | solution.py:12
  4.3 1.5 %collective-permute-done.2 = f32[1,16,2]{1,2,0:T(2,128)S(1)} collective-permute-done((f32[1,16,2]{1,2,0:T(2,128)S(1)}, f32[1,16,2]{1,2,0:T(2,128)S(1)}, u32[]{:S(2)}, u32[]{:S(2)}) %collective-permute-start.2) | collective-permute-done | bytes 160 | tf_op jit(solution)/shard_map/ppermute | solution.py:12
  7.1 2.1 %collective-permute-start.4 = (f32[64,2]{1,0:T(8,128)S(1)}, f32[64,2]{1,0:T(8,128)S(1)}, u32[]{:S(2)}, u32[]{:S(2)}) collective-permute-start(f32[64,2]{1,0:T(8,128)S(1)} %bitcast.83), channel_id=1, source_target_pairs={{0,4},{4,0},{8,12},{12,8},{1,5},{5,1},{9,13},{13,9},{2,6},{6,2},{1... | collective-permute-start | bytes 1544 | tf_op jit(solution)/shard_map/ppermute | solution.py:12
  9.2 2.6 %collective-permute-start.5 = (f32[64,2]{1,0:T(8,128)S(1)}, f32[64,2]{1,0:T(8,128)S(1)}, u32[]{:S(2)}, u32[]{:S(2)}) collective-permute-start(f32[64,2]{1,0:T(8,128)S(1)} %bitcast.84), channel_id=1, source_target_pairs={{0,8},{4,12},{8,0},{12,4},{1,9},{5,13},{9,1},{13,5},{2,10},{6,14},... | collective-permute-start | bytes 1544 | tf_op jit(solution)/shard_map/ppermute | solution.py:12
  12.0 4.0 %fetch.2 = (bf16[4608,1152]{1,0:T(8,128)(2,1)S(1)}, f32[64,2]{1,0:T(8,128)S(1)}) custom-call(bf16[4608,3072]{1,0:T(8,128)(2,1)} %all_ref.1, f32[64,2]{1,0:T(8,128)S(1)} %bitcast.86, bf16[2,16,4608]{2,1,0:T(8,128)(2,1)S(1)} %maximum_bitcast_fusion.refs_0_), custom_call_target="tpu_custom_call" | custom-call | bytes 10616832 | tf_op jit(solution)/shard_map/fetch/pallas_call | solution.py:102
  16.0 1.5 %collective-permute-done.6 = f32[64,2]{1,0:T(8,128)S(1)} collective-permute-done((f32[64,2]{1,0:T(8,128)S(1)}, f32[64,2]{1,0:T(8,128)S(1)}, u32[]{:S(2)}, u32[]{:S(2)}) %collective-permute-start.6) | collective-permute-done | bytes 544 | tf_op jit(solution)/shard_map/ppermute | solution.py:12
  18.2 7.8 %project.1 = (f32[16,3200]{1,0:T(8,128)S(1)}, s16[16,3328]{1,0:T(8,128)(2,1)S(1)}, s16[16,3328]{1,0:T(8,128)(2,1)S(1)}, s16[16,3328]{1,0:T(8,128)(2,1)S(1)}) custom-call(bf16[64,4608]{1,0:T(8,128)(2,1)S(1)} %fusion.3.x_ref, bf16[4608,1152]{1,0:T(8,128)(2,1)S(1)} %get-tuple-element.52.head_ref, bf16[4608,3072]{1,0:T(8,128)(2,1)} %all_ref.1, ...), custom_call_target="tpu_custom_call" | custom-call | flops 1811939328 | bytes 28311552 | tf_op jit(solution)/shard_map/project/pallas_call | solution.py:265
  26.5 2.0 %collective-permute-start.8 = (s16[16,3328]{1,0:T(8,128)(2,1)S(1)}, s16[16,3328]{1,0:T(8,128)(2,1)S(1)}, u32[]{:S(2)}, u32[]{:S(2)}) collective-permute-start(s16[16,3328]{1,0:T(8,128)(2,1)S(1)} %get-tuple-element.54), channel_id=1, source_target_pairs={{0,12},{4,8},{8,4},{12,0},{1,13},{5,9},{9,5},{13,1},{2,14},{6,10},... | collective-permute-start | bytes 319496 | tf_op jit(solution)/shard_map/ppermute | solution.py:12
  28.5 1.1 %collective-permute-start.9 = (s16[16,3328]{1,0:T(8,128)(2,1)S(1)}, s16[16,3328]{1,0:T(8,128)(2,1)S(1)}, u32[]{:S(2)}, u32[]{:S(2)}) collective-permute-start(s16[16,3328]{1,0:T(8,128)(2,1)S(1)} %get-tuple-element.55), channel_id=1, source_target_pairs={{0,4},{4,0},{8,12},{12,8},{1,5},{5,1},{9,13},{13,9},{2,6},{6,2},{1... | collective-permute-start | bytes 319496 | tf_op jit(solution)/shard_map/ppermute | solution.py:12
  29.6 3.7 %set_aside.1 = (bf16[3072,1536]{1,0:T(8,128)(2,1)S(1)}, f32[16,3200]{1,0:T(8,128)S(1)}) custom-call(bf16[3072,4608]{1,0:T(8,128)(2,1)} %w_ref.5, f32[16,3200]{1,0:T(8,128)S(1)} %get-tuple-element.56.passed_ref), custom_call_target="tpu_custom_call" | custom-call | bytes 18874368 | tf_op jit(solution)/shard_map/set_aside/pallas_call | solution.py:129
  33.3 3.6 %copy-done.1 = bf16[3072,1536]{1,0:T(8,128)(2,1)} copy-done((bf16[3072,1536]{1,0:T(8,128)(2,1)}, bf16[3072,1536]{1,0:T(8,128)(2,1)S(1)}, u32[]{:S(2)}) %copy-start.1) | copy-done | bytes 9437208
  37.3 1.7 %collective-permute-start.10 = (bf16[4,3200]{1,0:T(4,128)(2,1)S(1)}, bf16[4,3200]{1,0:T(4,128)(2,1)S(1)}, u32[]{:S(2)}, u32[]{:S(2)}) collective-permute-start(bf16[4,3200]{1,0:T(4,128)(2,1)S(1)} %get-tuple-element.93), channel_id=1, source_target_pairs={{0,2},{1,3},{2,0},{3,1},{4,6},{5,7},{6,4},{7,5},{8,10},{9,11},{10,... | collective-permute-start | bytes 76808 | tf_op jit(solution)/shard_map/ppermute | solution.py:12
  39.7 1.6 %collective-permute-done.10 = bf16[4,3200]{1,0:T(4,128)(2,1)S(1)} collective-permute-done((bf16[4,3200]{1,0:T(4,128)(2,1)S(1)}, bf16[4,3200]{1,0:T(4,128)(2,1)S(1)}, u32[]{:S(2)}, u32[]{:S(2)}) %collective-permute-start.10) | collective-permute-done | bytes 25632 | tf_op jit(solution)/shard_map/ppermute | solution.py:12
  45.5 1.5 %collective-permute-start.15 = (bf16[4,3072]{1,0:T(4,128)(2,1)S(1)}, bf16[4,3072]{1,0:T(4,128)(2,1)S(1)}, u32[]{:S(2)}, u32[]{:S(2)}) collective-permute-start(bf16[4,3072]{1,0:T(4,128)(2,1)S(1)} %bitcast.88), channel_id=1, source_target_pairs={{0,1},{1,0},{2,3},{3,2},{4,5},{5,4},{6,7},{7,6},{8,9},{9,8},{10,11... | collective-permute-start | bytes 73736 | tf_op jit(solution)/shard_map/ppermute | solution.py:12
  47.0 1.5 %collective-permute-done.13 = bf16[4,3072]{1,0:T(4,128)(2,1)S(1)} collective-permute-done((bf16[4,3072]{1,0:T(4,128)(2,1)S(1)}, bf16[4,3072]{1,0:T(4,128)(2,1)S(1)}, u32[]{:S(2)}, u32[]{:S(2)}) %collective-permute-start.13) | collective-permute-done | bytes 24608 | tf_op jit(solution)/shard_map/ppermute | solution.py:12
  49.0 2.7 %collective-permute-start.16 = (bf16[16,3072]{1,0:T(8,128)(2,1)S(1)}, bf16[16,3072]{1,0:T(8,128)(2,1)S(1)}, u32[]{:S(2)}, u32[]{:S(2)}) collective-permute-start(bf16[16,3072]{1,0:T(8,128)(2,1)S(1)} %constant_dynamic-update-slice_fusion.4.passed_ref), channel_id=1, source_target_pairs={{0,8},{4,12},{8,0},{12,4},{1,9},{5,13},{9,1},{13,5},{2,10},{6,14},... | collective-permute-start | bytes 294920 | tf_op jit(solution)/shard_map/ppermute | solution.py:12
  51.8 1.1 %collective-permute-start.17 = (bf16[16,3072]{1,0:T(8,128)(2,1)S(1)}, bf16[16,3072]{1,0:T(8,128)(2,1)S(1)}, u32[]{:S(2)}, u32[]{:S(2)}) collective-permute-start(bf16[16,3072]{1,0:T(8,128)(2,1)S(1)} %constant_dynamic-update-slice_fusion.4.passed_ref), channel_id=1, source_target_pairs={{0,12},{4,8},{8,4},{12,0},{1,13},{5,9},{9,5},{13,1},{2,14},{6,10},... | collective-permute-start | bytes 294920 | tf_op jit(solution)/shard_map/ppermute | solution.py:12
  52.8 6.4 %fetch.3 = (bf16[3072,3072]{1,0:T(8,128)(2,1)S(1)}, bf16[16,3072]{1,0:T(8,128)(2,1)S(1)}) custom-call(bf16[3072,4608]{1,0:T(8,128)(2,1)} %w_ref.5, bf16[16,3072]{1,0:T(8,128)(2,1)S(1)} %constant_dynamic-update-slice_fusion.4.passed_ref), custom_call_target="tpu_custom_call" | custom-call | bytes 18874368 | tf_op jit(solution)/shard_map/fetch/pallas_call | solution.py:102
  60.6 3.4 %multiply_held.2 = (f32[16,3072]{1,0:T(8,128)S(1)}, bf16[16,3072]{1,0:T(8,128)(2,1)S(1)}, bf16[16,3072]{1,0:T(8,128)(2,1)S(1)}, bf16[16,3072]{1,0:T(8,128)(2,1)S(1)}) custom-call(bf16[64,3072]{1,0:T(8,128)(2,1)S(1)} %constant_dynamic-update-slice_fusion.x_ref, bf16[3072,3072]{1,0:T(8,128)(2,1)S(1)} %get-tuple-element.70.w_ref), custom_call_target="tpu_custom_call" | custom-call | flops 1207959552 | bytes 18874368 | tf_op jit(solution)/shard_map/multiply_held/pallas_call | solution.py:298
  64.9 1.1 %collective-permute-start.21 = (bf16[16,3072]{1,0:T(8,128)(2,1)S(1)}, bf16[16,3072]{1,0:T(8,128)(2,1)S(1)}, u32[]{:S(2)}, u32[]{:S(2)}) collective-permute-start(bf16[16,3072]{1,0:T(8,128)(2,1)S(1)} %get-tuple-element.80), channel_id=1, source_target_pairs={{0,3},{1,2},{2,1},{3,0},{4,7},{5,6},{6,5},{7,4},{8,11},{9,10},{10,... | collective-permute-start | bytes 294920 | tf_op jit(solution)/shard_map/ppermute | solution.py:12
  66.0 1.7 %multiply_held.3 = (f32[16,1536]{1,0:T(8,128)S(1)}, bf16[16,1536]{1,0:T(8,128)(2,1)S(1)}, bf16[16,1536]{1,0:T(8,128)(2,1)S(1)}, bf16[16,1536]{1,0:T(8,128)(2,1)S(1)}) custom-call(bf16[64,3072]{1,0:T(8,128)(2,1)S(1)} %constant_dynamic-update-slice_fusion.x_ref, bf16[3072,1536]{1,0:T(8,128)(2,1)S(1)} %bitcast.81), custom_call_target="tpu_custom_call" | custom-call | flops 603979776 | bytes 9437184 | tf_op jit(solution)/shard_map/multiply_held/pallas_call | solution.py:298
  69.8 1.2 %collective-permute-done.21.refs_3_ = bf16[16,3072]{1,0:T(8,128)(2,1)S(1)} collective-permute-done((bf16[16,3072]{1,0:T(8,128)(2,1)S(1)}, bf16[16,3072]{1,0:T(8,128)(2,1)S(1)}, u32[]{:S(2)}, u32[]{:S(2)}) %collective-permute-start.21) | collective-permute-done | bytes 98336 | tf_op jit(solution)/shard_map/ppermute | solution.py:12
  71.0 2.0 %collective-permute-done.23.refs_6_ = bf16[16,1536]{1,0:T(8,128)(2,1)S(1)} collective-permute-done((bf16[16,1536]{1,0:T(8,128)(2,1)S(1)}, bf16[16,1536]{1,0:T(8,128)(2,1)S(1)}, u32[]{:S(2)}, u32[]{:S(2)}) %collective-permute-start.23) | collective-permute-done | bytes 49184 | tf_op jit(solution)/shard_map/ppermute | solution.py:12
  (104 shorter events, 13.6 us)
Async XLA Ops:
  1.3 4.5 %collective-permute-start.2 = (f32[1,16,2]{1,2,0:T(2,128)S(1)}, f32[1,16,2]{1,2,0:T(2,128)S(1)}, u32[]{:S(2)}, u32[]{:S(2)}) collective-permute-start(f32[1,16,2]{1,2,0:T(2,128)S(1)} %bitcast.94), channel_id=1, source_target_pairs={{0,2},{1,3},{2,0},{3,1},{4,6},{5,7},{6,4},{7,5},{8,10},{9,11},{10,... | collective-permute-start | bytes 392 | tf_op jit(solution)/shard_map/ppermute | solution.py:12
  4.2 7.6 %collective-permute-start = (bf16[1,16,4608]{2,1,0:T(8,128)(2,1)S(1)}, bf16[1,16,4608]{2,1,0:T(8,128)(2,1)S(1)}, u32[]{:S(2)}, u32[]{:S(2)}) collective-permute-start(bf16[1,16,4608]{2,1,0:T(8,128)(2,1)S(1)} %bitcast.82), channel_id=1, source_target_pairs={{0,2},{1,3},{2,0},{3,1},{4,6},{5,7},{6,4},{7,5},{8,10},{9,11},{10,... | collective-permute-start | bytes 442376 | tf_op jit(solution)/shard_map/ppermute | solution.py:12
  7.1 8.9 %collective-permute-start.4 = (f32[64,2]{1,0:T(8,128)S(1)}, f32[64,2]{1,0:T(8,128)S(1)}, u32[]{:S(2)}, u32[]{:S(2)}) collective-permute-start(f32[64,2]{1,0:T(8,128)S(1)} %bitcast.83), channel_id=1, source_target_pairs={{0,4},{4,0},{8,12},{12,8},{1,5},{5,1},{9,13},{13,9},{2,6},{6,2},{1... | collective-permute-start | bytes 1544 | tf_op jit(solution)/shard_map/ppermute | solution.py:12
  9.2 6.8 %collective-permute-start.5 = (f32[64,2]{1,0:T(8,128)S(1)}, f32[64,2]{1,0:T(8,128)S(1)}, u32[]{:S(2)}, u32[]{:S(2)}) collective-permute-start(f32[64,2]{1,0:T(8,128)S(1)} %bitcast.84), channel_id=1, source_target_pairs={{0,8},{4,12},{8,0},{12,4},{1,9},{5,13},{9,1},{13,5},{2,10},{6,14},... | collective-permute-start | bytes 1544 | tf_op jit(solution)/shard_map/ppermute | solution.py:12
  11.8 5.7 %collective-permute-start.6 = (f32[64,2]{1,0:T(8,128)S(1)}, f32[64,2]{1,0:T(8,128)S(1)}, u32[]{:S(2)}, u32[]{:S(2)}) collective-permute-start(f32[64,2]{1,0:T(8,128)S(1)} %bitcast.85), channel_id=1, source_target_pairs={{0,12},{4,8},{8,4},{12,0},{1,13},{5,9},{9,5},{13,1},{2,14},{6,10},... | collective-permute-start | bytes 1544 | tf_op jit(solution)/shard_map/ppermute | solution.py:12
  11.9 5.8 %collective-permute-start.1 = (bf16[2,16,4608]{2,1,0:T(8,128)(2,1)S(1)}, bf16[2,16,4608]{2,1,0:T(8,128)(2,1)S(1)}, u32[]{:S(2)}, u32[]{:S(2)}) collective-permute-start(bf16[2,16,4608]{2,1,0:T(8,128)(2,1)S(1)} %maximum_bitcast_fusion.refs_0_), channel_id=1, source_target_pairs={{0,1},{1,0},{2,3},{3,2},{4,5},{5,4},{6,7},{7,6},{8,9},{9,8},{10,11... | collective-permute-start | bytes 884744 | tf_op jit(solution)/shard_map/ppermute | solution.py:12
  26.0 11.0 %collective-permute-start.7 = (s16[16,3328]{1,0:T(8,128)(2,1)S(1)}, s16[16,3328]{1,0:T(8,128)(2,1)S(1)}, u32[]{:S(2)}, u32[]{:S(2)}) collective-permute-start(s16[16,3328]{1,0:T(8,128)(2,1)S(1)} %get-tuple-element.53), channel_id=1, source_target_pairs={{0,8},{4,12},{8,0},{12,4},{1,9},{5,13},{9,1},{13,5},{2,10},{6,14},... | collective-permute-start | bytes 319496 | tf_op jit(solution)/shard_map/ppermute | solution.py:12
  26.5 10.5 %collective-permute-start.8 = (s16[16,3328]{1,0:T(8,128)(2,1)S(1)}, s16[16,3328]{1,0:T(8,128)(2,1)S(1)}, u32[]{:S(2)}, u32[]{:S(2)}) collective-permute-start(s16[16,3328]{1,0:T(8,128)(2,1)S(1)} %get-tuple-element.54), channel_id=1, source_target_pairs={{0,12},{4,8},{8,4},{12,0},{1,13},{5,9},{9,5},{13,1},{2,14},{6,10},... | collective-permute-start | bytes 319496 | tf_op jit(solution)/shard_map/ppermute | solution.py:12
  28.5 8.5 %collective-permute-start.9 = (s16[16,3328]{1,0:T(8,128)(2,1)S(1)}, s16[16,3328]{1,0:T(8,128)(2,1)S(1)}, u32[]{:S(2)}, u32[]{:S(2)}) collective-permute-start(s16[16,3328]{1,0:T(8,128)(2,1)S(1)} %get-tuple-element.55), channel_id=1, source_target_pairs={{0,4},{4,0},{8,12},{12,8},{1,5},{5,1},{9,13},{13,9},{2,6},{6,2},{1... | collective-permute-start | bytes 319496 | tf_op jit(solution)/shard_map/ppermute | solution.py:12
  37.3 3.9 %collective-permute-start.10 = (bf16[4,3200]{1,0:T(4,128)(2,1)S(1)}, bf16[4,3200]{1,0:T(4,128)(2,1)S(1)}, u32[]{:S(2)}, u32[]{:S(2)}) collective-permute-start(bf16[4,3200]{1,0:T(4,128)(2,1)S(1)} %get-tuple-element.93), channel_id=1, source_target_pairs={{0,2},{1,3},{2,0},{3,1},{4,6},{5,7},{6,4},{7,5},{8,10},{9,11},{10,... | collective-permute-start | bytes 76808 | tf_op jit(solution)/shard_map/ppermute | solution.py:12
  39.0 3.3 %collective-permute-start.11 = (bf16[4,3200]{1,0:T(4,128)(2,1)S(1)}, bf16[4,3200]{1,0:T(4,128)(2,1)S(1)}, u32[]{:S(2)}, u32[]{:S(2)}) collective-permute-start(bf16[4,3200]{1,0:T(4,128)(2,1)S(1)} %get-tuple-element.92), channel_id=1, source_target_pairs={{0,3},{1,2},{2,1},{3,0},{4,7},{5,6},{6,5},{7,4},{8,11},{9,10},{10,... | collective-permute-start | bytes 76808 | tf_op jit(solution)/shard_map/ppermute | solution.py:12
  39.0 3.3 %collective-permute-start.12 = (bf16[4,3200]{1,0:T(4,128)(2,1)S(1)}, bf16[4,3200]{1,0:T(4,128)(2,1)S(1)}, u32[]{:S(2)}, u32[]{:S(2)}) collective-permute-start(bf16[4,3200]{1,0:T(4,128)(2,1)S(1)} %get-tuple-element.91), channel_id=1, source_target_pairs={{0,1},{1,0},{2,3},{3,2},{4,5},{5,4},{6,7},{7,6},{8,9},{9,8},{10,11... | collective-permute-start | bytes 76808 | tf_op jit(solution)/shard_map/ppermute | solution.py:12
  44.6 3.9 %collective-permute-start.13 = (bf16[4,3072]{1,0:T(4,128)(2,1)S(1)}, bf16[4,3072]{1,0:T(4,128)(2,1)S(1)}, u32[]{:S(2)}, u32[]{:S(2)}) collective-permute-start(bf16[4,3072]{1,0:T(4,128)(2,1)S(1)} %bitcast.90), channel_id=1, source_target_pairs={{0,2},{1,3},{2,0},{3,1},{4,6},{5,7},{6,4},{7,5},{8,10},{9,11},{10,... | collective-permute-start | bytes 73736 | tf_op jit(solution)/shard_map/ppermute | solution.py:12
  45.4 3.6 %collective-permute-start.14 = (bf16[4,3072]{1,0:T(4,128)(2,1)S(1)}, bf16[4,3072]{1,0:T(4,128)(2,1)S(1)}, u32[]{:S(2)}, u32[]{:S(2)}) collective-permute-start(bf16[4,3072]{1,0:T(4,128)(2,1)S(1)} %bitcast.89), channel_id=1, source_target_pairs={{0,3},{1,2},{2,1},{3,0},{4,7},{5,6},{6,5},{7,4},{8,11},{9,10},{10,... | collective-permute-start | bytes 73736 | tf_op jit(solution)/shard_map/ppermute | solution.py:12
  45.5 3.5 %collective-permute-start.15 = (bf16[4,3072]{1,0:T(4,128)(2,1)S(1)}, bf16[4,3072]{1,0:T(4,128)(2,1)S(1)}, u32[]{:S(2)}, u32[]{:S(2)}) collective-permute-start(bf16[4,3072]{1,0:T(4,128)(2,1)S(1)} %bitcast.88), channel_id=1, source_target_pairs={{0,1},{1,0},{2,3},{3,2},{4,5},{5,4},{6,7},{7,6},{8,9},{9,8},{10,11... | collective-permute-start | bytes 73736 | tf_op jit(solution)/shard_map/ppermute | solution.py:12
  49.0 10.9 %collective-permute-start.16 = (bf16[16,3072]{1,0:T(8,128)(2,1)S(1)}, bf16[16,3072]{1,0:T(8,128)(2,1)S(1)}, u32[]{:S(2)}, u32[]{:S(2)}) collective-permute-start(bf16[16,3072]{1,0:T(8,128)(2,1)S(1)} %constant_dynamic-update-slice_fusion.4.passed_ref), channel_id=1, source_target_pairs={{0,8},{4,12},{8,0},{12,4},{1,9},{5,13},{9,1},{13,5},{2,10},{6,14},... | collective-permute-start | bytes 294920 | tf_op jit(solution)/shard_map/ppermute | solution.py:12
  51.8 8.1 %collective-permute-start.17 = (bf16[16,3072]{1,0:T(8,128)(2,1)S(1)}, bf16[16,3072]{1,0:T(8,128)(2,1)S(1)}, u32[]{:S(2)}, u32[]{:S(2)}) collective-permute-start(bf16[16,3072]{1,0:T(8,128)(2,1)S(1)} %constant_dynamic-update-slice_fusion.4.passed_ref), channel_id=1, source_target_pairs={{0,12},{4,8},{8,4},{12,0},{1,13},{5,9},{9,5},{13,1},{2,14},{6,10},... | collective-permute-start | bytes 294920 | tf_op jit(solution)/shard_map/ppermute | solution.py:12
  52.8 7.6 %collective-permute-start.18 = (bf16[16,3072]{1,0:T(8,128)(2,1)S(1)}, bf16[16,3072]{1,0:T(8,128)(2,1)S(1)}, u32[]{:S(2)}, u32[]{:S(2)}) collective-permute-start(bf16[16,3072]{1,0:T(8,128)(2,1)S(1)} %constant_dynamic-update-slice_fusion.4.passed_ref), channel_id=1, source_target_pairs={{0,4},{4,0},{8,12},{12,8},{1,5},{5,1},{9,13},{13,9},{2,6},{6,2},{1... | collective-permute-start | bytes 294920 | tf_op jit(solution)/shard_map/ppermute | solution.py:12
  64.0 3.7 %collective-permute-start.19 = (bf16[16,3072]{1,0:T(8,128)(2,1)S(1)}, bf16[16,3072]{1,0:T(8,128)(2,1)S(1)}, u32[]{:S(2)}, u32[]{:S(2)}) collective-permute-start(bf16[16,3072]{1,0:T(8,128)(2,1)S(1)} %get-tuple-element.77), channel_id=1, source_target_pairs={{0,1},{1,0},{2,3},{3,2},{4,5},{5,4},{6,7},{7,6},{8,9},{9,8},{10,11... | collective-permute-start | bytes 294920 | tf_op jit(solution)/shard_map/ppermute | solution.py:12
  64.1 5.7 %collective-permute-start.20 = (bf16[16,3072]{1,0:T(8,128)(2,1)S(1)}, bf16[16,3072]{1,0:T(8,128)(2,1)S(1)}, u32[]{:S(2)}, u32[]{:S(2)}) collective-permute-start(bf16[16,3072]{1,0:T(8,128)(2,1)S(1)} %get-tuple-element.79), channel_id=1, source_target_pairs={{0,2},{1,3},{2,0},{3,1},{4,6},{5,7},{6,4},{7,5},{8,10},{9,11},{10,... | collective-permute-start | bytes 294920 | tf_op jit(solution)/shard_map/ppermute | solution.py:12
  64.9 6.1 %collective-permute-start.21 = (bf16[16,3072]{1,0:T(8,128)(2,1)S(1)}, bf16[16,3072]{1,0:T(8,128)(2,1)S(1)}, u32[]{:S(2)}, u32[]{:S(2)}) collective-permute-start(bf16[16,3072]{1,0:T(8,128)(2,1)S(1)} %get-tuple-element.80), channel_id=1, source_target_pairs={{0,3},{1,2},{2,1},{3,0},{4,7},{5,6},{6,5},{7,4},{8,11},{9,10},{10,... | collective-permute-start | bytes 294920 | tf_op jit(solution)/shard_map/ppermute | solution.py:12
  67.8 3.2 %collective-permute-start.22 = (bf16[16,1536]{1,0:T(8,128)(2,1)S(1)}, bf16[16,1536]{1,0:T(8,128)(2,1)S(1)}, u32[]{:S(2)}, u32[]{:S(2)}) collective-permute-start(bf16[16,1536]{1,0:T(8,128)(2,1)S(1)} %get-tuple-element.82), channel_id=1, source_target_pairs={{0,1},{1,0},{2,3},{3,2},{4,5},{5,4},{6,7},{7,6},{8,9},{9,8},{10,11... | collective-permute-start | bytes 147464 | tf_op jit(solution)/shard_map/ppermute | solution.py:12
  68.2 4.8 %collective-permute-start.23 = (bf16[16,1536]{1,0:T(8,128)(2,1)S(1)}, bf16[16,1536]{1,0:T(8,128)(2,1)S(1)}, u32[]{:S(2)}, u32[]{:S(2)}) collective-permute-start(bf16[16,1536]{1,0:T(8,128)(2,1)S(1)} %get-tuple-element.83), channel_id=1, source_target_pairs={{0,2},{1,3},{2,0},{3,1},{4,6},{5,7},{6,4},{7,5},{8,10},{9,11},{10,... | collective-permute-start | bytes 147464 | tf_op jit(solution)/shard_map/ppermute | solution.py:12
  68.9 4.2 %collective-permute-start.24 = (bf16[16,1536]{1,0:T(8,128)(2,1)S(1)}, bf16[16,1536]{1,0:T(8,128)(2,1)S(1)}, u32[]{:S(2)}, u32[]{:S(2)}) collective-permute-start(bf16[16,1536]{1,0:T(8,128)(2,1)S(1)} %get-tuple-element.84), channel_id=1, source_target_pairs={{0,3},{1,2},{2,1},{3,0},{4,7},{5,6},{6,5},{7,4},{8,11},{9,10},{10,... | collective-permute-start | bytes 147464 | tf_op jit(solution)/shard_map/ppermute | solution.py:12
  (9 other events, 77.7 us)

commit v7 on v6

--- a/solution.py
+++ b/solution.py
@@ -349,7 +349,7 @@
         as_float = double_rows(own, "gy", ny, steps).astype(jnp.float32)
         q_cols = w_query.shape[1]
         w_head, moments = fetch(
-            w_query, 0, whole_tiles(q_cols * 3 // 8), partial_moments, steps[0]
+            w_query, 0, whole_tiles(q_cols * 8 // 16), partial_moments, steps[0]
         )
         others, moments = lax.optimization_barrier(
             (exchange([partial_moments] * nx, "gx", nx)[1:], moments)
@@ -364,7 +364,7 @@
         ).astype(jnp.bfloat16)
         kv_cols = w_keyval.shape[1] // ny
         projected = project(normed, w_head, w_query, w_keyval, kv_cols, "gy", "gx", nx)
-        cut = whole_tiles(w_out.shape[1] * 11 // 16)
+        cut = whole_tiles(w_out.shape[1] * 7 // 10)
         parts = exchange(projected, "gx", nx)[1:]
         w_right, part = set_aside(w_out, cut, projected[0])
         parts = [parts[m - 1] for m in order_of(nx)]

time: 74.1 us -> 74.4 us (level)
    pallas_call x2, Pallas kernels: 10.5 us -> 11.7 us  [fetch(): pl.pallas_call(body, out_shape=[pltpu.VMEM((rows, cols), w.dtype), pltpu....]
    pallas_call x1, Pallas kernels: 7.76 us -> 6.85 us  [project(): pl.pallas_call(body, out_shape=share_shapes(rows, cols + last_cols, n, Tr...]
  transfers between devices with their start and end apart: 25 -> 25, of which waited for: 13 -> 15; matrix products, arithmetic and copies ran while one was open for 2% -> 2% of each run, Pallas kernels for 22% -> 23%
where the time goes in v7:
time: 74.4 us; the launch traced here: 74.1 us
  Pallas kernels  28.3 us (38%)
  starting transfers between devices  24.1 us (32%)
  waiting for transfers between devices  12.4 us (17%)
  local copies, waits for them, and re-layouts  5.58 us (7%)
  other arithmetic  1.73 us (2%)
  matrix products  1.48 us (2%)
    ppermute x25, starting transfers between devices, swap(): return lax.ppermute(x, axis, [(k, k ^ m) for k in range(n)])  24.1 us
    ppermute x25, waiting for transfers between devices, swap(): return lax.ppermute(x, axis, [(k, k ^ m) for k in range(n)])  12.4 us
    pallas_call x2, Pallas kernels, fetch(): pl.pallas_call(body, out_shape=[pltpu.VMEM((rows, cols), w.dtype), pltpu....  11.7 us
    pallas_call x1, Pallas kernels, project(): pl.pallas_call(body, out_shape=share_shapes(rows, cols + last_cols, n, Tr...  6.85 us
    pallas_call x2, Pallas kernels, multiply_held(): pl.pallas_call(body, out_shape=share_shapes(rows, cols, n, False), in_spe...  5.21 us
    unnamed x21, local copies, waits for them, and re-layouts  4.82 us
    pallas_call x1, Pallas kernels, set_aside(): pl.pallas_call(body, out_shape=[jax.ShapeDtypeStruct((rows, cols), w.dtyp...  3.47 us
  transfers between devices with their start and end apart: 25, of which 15 were waited for; matrix products, arithmetic and copies ran while one was open for 2% of the time, Pallas kernels for 23%

profile of v7, /device:TPU:0, one launch (start us, length us, event | category | flops | bytes accessed | tf_op | source)
XLA Modules:
  0.0 74.1 jit_solution(2506364716638521251)
XLA Ops:
  0.0 1.1 %copy-done.2 = bf16[16,4608]{1,0:T(8,128)(2,1)S(1)} copy-done((bf16[16,4608]{1,0:T(8,128)(2,1)S(1)}, bf16[16,4608]{1,0:T(8,128)(2,1)}, u32[]{:S(2)}) %copy-start.2) | copy-done | bytes 147480
  1.3 2.9 %collective-permute-start.2 = (f32[1,16,2]{1,2,0:T(2,128)S(1)}, f32[1,16,2]{1,2,0:T(2,128)S(1)}, u32[]{:S(2)}, u32[]{:S(2)}) collective-permute-start(f32[1,16,2]{1,2,0:T(2,128)S(1)} %bitcast.94), channel_id=1, source_target_pairs={{0,2},{1,3},{2,0},{3,1},{4,6},{5,7},{6,4},{7,5},{8,10},{9,11},{10,... | collective-permute-start | bytes 392 | tf_op jit(solution)/shard_map/ppermute | solution.py:12
  4.3 1.5 %collective-permute-done.2 = f32[1,16,2]{1,2,0:T(2,128)S(1)} collective-permute-done((f32[1,16,2]{1,2,0:T(2,128)S(1)}, f32[1,16,2]{1,2,0:T(2,128)S(1)}, u32[]{:S(2)}, u32[]{:S(2)}) %collective-permute-start.2) | collective-permute-done | bytes 160 | tf_op jit(solution)/shard_map/ppermute | solution.py:12
  7.1 2.1 %collective-permute-start.4 = (f32[64,2]{1,0:T(8,128)S(1)}, f32[64,2]{1,0:T(8,128)S(1)}, u32[]{:S(2)}, u32[]{:S(2)}) collective-permute-start(f32[64,2]{1,0:T(8,128)S(1)} %bitcast.83), channel_id=1, source_target_pairs={{0,4},{4,0},{8,12},{12,8},{1,5},{5,1},{9,13},{13,9},{2,6},{6,2},{1... | collective-permute-start | bytes 1544 | tf_op jit(solution)/shard_map/ppermute | solution.py:12
  9.2 2.6 %collective-permute-start.5 = (f32[64,2]{1,0:T(8,128)S(1)}, f32[64,2]{1,0:T(8,128)S(1)}, u32[]{:S(2)}, u32[]{:S(2)}) collective-permute-start(f32[64,2]{1,0:T(8,128)S(1)} %bitcast.84), channel_id=1, source_target_pairs={{0,8},{4,12},{8,0},{12,4},{1,9},{5,13},{9,1},{13,5},{2,10},{6,14},... | collective-permute-start | bytes 1544 | tf_op jit(solution)/shard_map/ppermute | solution.py:12
  12.0 5.0 %fetch.2 = (bf16[4608,1536]{1,0:T(8,128)(2,1)S(1)}, f32[64,2]{1,0:T(8,128)S(1)}) custom-call(bf16[4608,3072]{1,0:T(8,128)(2,1)} %all_ref.1, f32[64,2]{1,0:T(8,128)S(1)} %bitcast.86, bf16[2,16,4608]{2,1,0:T(8,128)(2,1)S(1)} %maximum_bitcast_fusion.refs_0_), custom_call_target="tpu_custom_call" | custom-call | bytes 14155776 | tf_op jit(solution)/shard_map/fetch/pallas_call | solution.py:102
  18.2 6.8 %project.1 = (f32[16,3200]{1,0:T(8,128)S(1)}, s16[16,3328]{1,0:T(8,128)(2,1)S(1)}, s16[16,3328]{1,0:T(8,128)(2,1)S(1)}, s16[16,3328]{1,0:T(8,128)(2,1)S(1)}) custom-call(bf16[64,4608]{1,0:T(8,128)(2,1)S(1)} %fusion.3.x_ref, bf16[4608,1536]{1,0:T(8,128)(2,1)S(1)} %get-tuple-element.52.head_ref, bf16[4608,3072]{1,0:T(8,128)(2,1)} %all_ref.1, ...), custom_call_target="tpu_custom_call" | custom-call | flops 1811939328 | bytes 28311552 | tf_op jit(solution)/shard_map/project/pallas_call | solution.py:265
  25.1 1.5 %collective-permute-start.7 = (s16[16,3328]{1,0:T(8,128)(2,1)S(1)}, s16[16,3328]{1,0:T(8,128)(2,1)S(1)}, u32[]{:S(2)}, u32[]{:S(2)}) collective-permute-start(s16[16,3328]{1,0:T(8,128)(2,1)S(1)} %get-tuple-element.53), channel_id=1, source_target_pairs={{0,8},{4,12},{8,0},{12,4},{1,9},{5,13},{9,1},{13,5},{2,10},{6,14},... | collective-permute-start | bytes 319496 | tf_op jit(solution)/shard_map/ppermute | solution.py:12
  26.6 2.0 %collective-permute-start.8 = (s16[16,3328]{1,0:T(8,128)(2,1)S(1)}, s16[16,3328]{1,0:T(8,128)(2,1)S(1)}, u32[]{:S(2)}, u32[]{:S(2)}) collective-permute-start(s16[16,3328]{1,0:T(8,128)(2,1)S(1)} %get-tuple-element.54), channel_id=1, source_target_pairs={{0,12},{4,8},{8,4},{12,0},{1,13},{5,9},{9,5},{13,1},{2,14},{6,10},... | collective-permute-start | bytes 319496 | tf_op jit(solution)/shard_map/ppermute | solution.py:12
  29.1 3.5 %set_aside.1 = (bf16[3072,1408]{1,0:T(8,128)(2,1)S(1)}, f32[16,3200]{1,0:T(8,128)S(1)}) custom-call(bf16[3072,4608]{1,0:T(8,128)(2,1)} %w_ref.5, f32[16,3200]{1,0:T(8,128)S(1)} %get-tuple-element.56.passed_ref), custom_call_target="tpu_custom_call" | custom-call | bytes 17301504 | tf_op jit(solution)/shard_map/set_aside/pallas_call | solution.py:129
  32.6 3.4 %copy-done.1 = bf16[3072,1408]{1,0:T(8,128)(2,1)} copy-done((bf16[3072,1408]{1,0:T(8,128)(2,1)}, bf16[3072,1408]{1,0:T(8,128)(2,1)S(1)}, u32[]{:S(2)}) %copy-start.1) | copy-done | bytes 8650776
  37.3 1.8 %collective-permute-start.10 = (bf16[4,3200]{1,0:T(4,128)(2,1)S(1)}, bf16[4,3200]{1,0:T(4,128)(2,1)S(1)}, u32[]{:S(2)}, u32[]{:S(2)}) collective-permute-start(bf16[4,3200]{1,0:T(4,128)(2,1)S(1)} %get-tuple-element.93), channel_id=1, source_target_pairs={{0,2},{1,3},{2,0},{3,1},{4,6},{5,7},{6,4},{7,5},{8,10},{9,11},{10,... | collective-permute-start | bytes 76808 | tf_op jit(solution)/shard_map/ppermute | solution.py:12
  39.6 1.6 %collective-permute-done.10 = bf16[4,3200]{1,0:T(4,128)(2,1)S(1)} collective-permute-done((bf16[4,3200]{1,0:T(4,128)(2,1)S(1)}, bf16[4,3200]{1,0:T(4,128)(2,1)S(1)}, u32[]{:S(2)}, u32[]{:S(2)}) %collective-permute-start.10) | collective-permute-done | bytes 25632 | tf_op jit(solution)/shard_map/ppermute | solution.py:12
  41.2 1.2 %collective-permute-done.11 = bf16[4,3200]{1,0:T(4,128)(2,1)S(1)} collective-permute-done((bf16[4,3200]{1,0:T(4,128)(2,1)S(1)}, bf16[4,3200]{1,0:T(4,128)(2,1)S(1)}, u32[]{:S(2)}, u32[]{:S(2)}) %collective-permute-start.11) | collective-permute-done | bytes 25632 | tf_op jit(solution)/shard_map/ppermute | solution.py:12
  45.5 1.6 %collective-permute-start.15 = (bf16[4,3072]{1,0:T(4,128)(2,1)S(1)}, bf16[4,3072]{1,0:T(4,128)(2,1)S(1)}, u32[]{:S(2)}, u32[]{:S(2)}) collective-permute-start(bf16[4,3072]{1,0:T(4,128)(2,1)S(1)} %bitcast.88), channel_id=1, source_target_pairs={{0,1},{1,0},{2,3},{3,2},{4,5},{5,4},{6,7},{7,6},{8,9},{9,8},{10,11... | collective-permute-start | bytes 73736 | tf_op jit(solution)/shard_map/ppermute | solution.py:12
  47.1 1.6 %collective-permute-done.13 = bf16[4,3072]{1,0:T(4,128)(2,1)S(1)} collective-permute-done((bf16[4,3072]{1,0:T(4,128)(2,1)S(1)}, bf16[4,3072]{1,0:T(4,128)(2,1)S(1)}, u32[]{:S(2)}, u32[]{:S(2)}) %collective-permute-start.13) | collective-permute-done | bytes 24608 | tf_op jit(solution)/shard_map/ppermute | solution.py:12
  49.0 2.9 %collective-permute-start.16 = (bf16[16,3072]{1,0:T(8,128)(2,1)S(1)}, bf16[16,3072]{1,0:T(8,128)(2,1)S(1)}, u32[]{:S(2)}, u32[]{:S(2)}) collective-permute-start(bf16[16,3072]{1,0:T(8,128)(2,1)S(1)} %constant_dynamic-update-slice_fusion.4.passed_ref), channel_id=1, source_target_pairs={{0,8},{4,12},{8,0},{12,4},{1,9},{5,13},{9,1},{13,5},{2,10},{6,14},... | collective-permute-start | bytes 294920 | tf_op jit(solution)/shard_map/ppermute | solution.py:12
  51.9 1.0 %collective-permute-start.17 = (bf16[16,3072]{1,0:T(8,128)(2,1)S(1)}, bf16[16,3072]{1,0:T(8,128)(2,1)S(1)}, u32[]{:S(2)}, u32[]{:S(2)}) collective-permute-start(bf16[16,3072]{1,0:T(8,128)(2,1)S(1)} %constant_dynamic-update-slice_fusion.4.passed_ref), channel_id=1, source_target_pairs={{0,12},{4,8},{8,4},{12,0},{1,13},{5,9},{9,5},{13,1},{2,14},{6,10},... | collective-permute-start | bytes 294920 | tf_op jit(solution)/shard_map/ppermute | solution.py:12
  52.9 6.6 %fetch.3 = (bf16[3072,3200]{1,0:T(8,128)(2,1)S(1)}, bf16[16,3072]{1,0:T(8,128)(2,1)S(1)}) custom-call(bf16[3072,4608]{1,0:T(8,128)(2,1)} %w_ref.5, bf16[16,3072]{1,0:T(8,128)(2,1)S(1)} %constant_dynamic-update-slice_fusion.4.passed_ref), custom_call_target="tpu_custom_call" | custom-call | bytes 19660800 | tf_op jit(solution)/shard_map/fetch/pallas_call | solution.py:102
  60.7 3.6 %multiply_held.2 = (f32[16,3200]{1,0:T(8,128)S(1)}, bf16[16,3200]{1,0:T(8,128)(2,1)S(1)}, bf16[16,3200]{1,0:T(8,128)(2,1)S(1)}, bf16[16,3200]{1,0:T(8,128)(2,1)S(1)}) custom-call(bf16[64,3072]{1,0:T(8,128)(2,1)S(1)} %constant_dynamic-update-slice_fusion.x_ref, bf16[3072,3200]{1,0:T(8,128)(2,1)S(1)} %get-tuple-element.70.w_ref), custom_call_target="tpu_custom_call" | custom-call | flops 1258291200 | bytes 19660800 | tf_op jit(solution)/shard_map/multiply_held/pallas_call | solution.py:298
  65.1 1.1 %collective-permute-start.21 = (bf16[16,3200]{1,0:T(8,128)(2,1)S(1)}, bf16[16,3200]{1,0:T(8,128)(2,1)S(1)}, u32[]{:S(2)}, u32[]{:S(2)}) collective-permute-start(bf16[16,3200]{1,0:T(8,128)(2,1)S(1)} %get-tuple-element.80), channel_id=1, source_target_pairs={{0,3},{1,2},{2,1},{3,0},{4,7},{5,6},{6,5},{7,4},{8,11},{9,10},{10,... | collective-permute-start | bytes 307208 | tf_op jit(solution)/shard_map/ppermute | solution.py:12
  66.2 1.6 %multiply_held.3 = (f32[16,1408]{1,0:T(8,128)S(1)}, bf16[16,1408]{1,0:T(8,128)(2,1)S(1)}, bf16[16,1408]{1,0:T(8,128)(2,1)S(1)}, bf16[16,1408]{1,0:T(8,128)(2,1)S(1)}) custom-call(bf16[64,3072]{1,0:T(8,128)(2,1)S(1)} %constant_dynamic-update-slice_fusion.x_ref, bf16[3072,1408]{1,0:T(8,128)(2,1)S(1)} %bitcast.81), custom_call_target="tpu_custom_call" | custom-call | flops 553648128 | bytes 8650752 | tf_op jit(solution)/shard_map/multiply_held/pallas_call | solution.py:298
  70.1 1.3 %collective-permute-done.21.refs_3_ = bf16[16,3200]{1,0:T(8,128)(2,1)S(1)} collective-permute-done((bf16[16,3200]{1,0:T(8,128)(2,1)S(1)}, bf16[16,3200]{1,0:T(8,128)(2,1)S(1)}, u32[]{:S(2)}, u32[]{:S(2)}) %collective-permute-start.21) | collective-permute-done | bytes 102432 | tf_op jit(solution)/shard_map/ppermute | solution.py:12
  71.4 1.9 %collective-permute-done.23.refs_6_ = bf16[16,1408]{1,0:T(8,128)(2,1)S(1)} collective-permute-done((bf16[16,1408]{1,0:T(8,128)(2,1)S(1)}, bf16[16,1408]{1,0:T(8,128)(2,1)S(1)}, u32[]{:S(2)}, u32[]{:S(2)}) %collective-permute-start.23) | collective-permute-done | bytes 45088 | tf_op jit(solution)/shard_map/ppermute | solution.py:12
  (104 shorter events, 13.5 us)
Async XLA Ops:
  1.3 4.5 %collective-permute-start.2 = (f32[1,16,2]{1,2,0:T(2,128)S(1)}, f32[1,16,2]{1,2,0:T(2,128)S(1)}, u32[]{:S(2)}, u32[]{:S(2)}) collective-permute-start(f32[1,16,2]{1,2,0:T(2,128)S(1)} %bitcast.94), channel_id=1, source_target_pairs={{0,2},{1,3},{2,0},{3,1},{4,6},{5,7},{6,4},{7,5},{8,10},{9,11},{10,... | collective-permute-start | bytes 392 | tf_op jit(solution)/shard_map/ppermute | solution.py:12
  4.2 7.6 %collective-permute-start = (bf16[1,16,4608]{2,1,0:T(8,128)(2,1)S(1)}, bf16[1,16,4608]{2,1,0:T(8,128)(2,1)S(1)}, u32[]{:S(2)}, u32[]{:S(2)}) collective-permute-start(bf16[1,16,4608]{2,1,0:T(8,128)(2,1)S(1)} %bitcast.82), channel_id=1, source_target_pairs={{0,2},{1,3},{2,0},{3,1},{4,6},{5,7},{6,4},{7,5},{8,10},{9,11},{10,... | collective-permute-start | bytes 442376 | tf_op jit(solution)/shard_map/ppermute | solution.py:12
  7.1 9.9 %collective-permute-start.4 = (f32[64,2]{1,0:T(8,128)S(1)}, f32[64,2]{1,0:T(8,128)S(1)}, u32[]{:S(2)}, u32[]{:S(2)}) collective-permute-start(f32[64,2]{1,0:T(8,128)S(1)} %bitcast.83), channel_id=1, source_target_pairs={{0,4},{4,0},{8,12},{12,8},{1,5},{5,1},{9,13},{13,9},{2,6},{6,2},{1... | collective-permute-start | bytes 1544 | tf_op jit(solution)/shard_map/ppermute | solution.py:12
  9.2 7.8 %collective-permute-start.5 = (f32[64,2]{1,0:T(8,128)S(1)}, f32[64,2]{1,0:T(8,128)S(1)}, u32[]{:S(2)}, u32[]{:S(2)}) collective-permute-start(f32[64,2]{1,0:T(8,128)S(1)} %bitcast.84), channel_id=1, source_target_pairs={{0,8},{4,12},{8,0},{12,4},{1,9},{5,13},{9,1},{13,5},{2,10},{6,14},... | collective-permute-start | bytes 1544 | tf_op jit(solution)/shard_map/ppermute | solution.py:12
  11.8 5.7 %collective-permute-start.6 = (f32[64,2]{1,0:T(8,128)S(1)}, f32[64,2]{1,0:T(8,128)S(1)}, u32[]{:S(2)}, u32[]{:S(2)}) collective-permute-start(f32[64,2]{1,0:T(8,128)S(1)} %bitcast.85), channel_id=1, source_target_pairs={{0,12},{4,8},{8,4},{12,0},{1,13},{5,9},{9,5},{13,1},{2,14},{6,10},... | collective-permute-start | bytes 1544 | tf_op jit(solution)/shard_map/ppermute | solution.py:12
  11.9 5.8 %collective-permute-start.1 = (bf16[2,16,4608]{2,1,0:T(8,128)(2,1)S(1)}, bf16[2,16,4608]{2,1,0:T(8,128)(2,1)S(1)}, u32[]{:S(2)}, u32[]{:S(2)}) collective-permute-start(bf16[2,16,4608]{2,1,0:T(8,128)(2,1)S(1)} %maximum_bitcast_fusion.refs_0_), channel_id=1, source_target_pairs={{0,1},{1,0},{2,3},{3,2},{4,5},{5,4},{6,7},{7,6},{8,9},{9,8},{10,11... | collective-permute-start | bytes 884744 | tf_op jit(solution)/shard_map/ppermute | solution.py:12
  25.1 11.4 %collective-permute-start.7 = (s16[16,3328]{1,0:T(8,128)(2,1)S(1)}, s16[16,3328]{1,0:T(8,128)(2,1)S(1)}, u32[]{:S(2)}, u32[]{:S(2)}) collective-permute-start(s16[16,3328]{1,0:T(8,128)(2,1)S(1)} %get-tuple-element.53), channel_id=1, source_target_pairs={{0,8},{4,12},{8,0},{12,4},{1,9},{5,13},{9,1},{13,5},{2,10},{6,14},... | collective-permute-start | bytes 319496 | tf_op jit(solution)/shard_map/ppermute | solution.py:12
  26.6 9.9 %collective-permute-start.8 = (s16[16,3328]{1,0:T(8,128)(2,1)S(1)}, s16[16,3328]{1,0:T(8,128)(2,1)S(1)}, u32[]{:S(2)}, u32[]{:S(2)}) collective-permute-start(s16[16,3328]{1,0:T(8,128)(2,1)S(1)} %get-tuple-element.54), channel_id=1, source_target_pairs={{0,12},{4,8},{8,4},{12,0},{1,13},{5,9},{9,5},{13,1},{2,14},{6,10},... | collective-permute-start | bytes 319496 | tf_op jit(solution)/shard_map/ppermute | solution.py:12
  28.6 8.4 %collective-permute-start.9 = (s16[16,3328]{1,0:T(8,128)(2,1)S(1)}, s16[16,3328]{1,0:T(8,128)(2,1)S(1)}, u32[]{:S(2)}, u32[]{:S(2)}) collective-permute-start(s16[16,3328]{1,0:T(8,128)(2,1)S(1)} %get-tuple-element.55), channel_id=1, source_target_pairs={{0,4},{4,0},{8,12},{12,8},{1,5},{5,1},{9,13},{13,9},{2,6},{6,2},{1... | collective-permute-start | bytes 319496 | tf_op jit(solution)/shard_map/ppermute | solution.py:12
  37.3 3.9 %collective-permute-start.10 = (bf16[4,3200]{1,0:T(4,128)(2,1)S(1)}, bf16[4,3200]{1,0:T(4,128)(2,1)S(1)}, u32[]{:S(2)}, u32[]{:S(2)}) collective-permute-start(bf16[4,3200]{1,0:T(4,128)(2,1)S(1)} %get-tuple-element.93), channel_id=1, source_target_pairs={{0,2},{1,3},{2,0},{3,1},{4,6},{5,7},{6,4},{7,5},{8,10},{9,11},{10,... | collective-permute-start | bytes 76808 | tf_op jit(solution)/shard_map/ppermute | solution.py:12
  39.1 3.3 %collective-permute-start.11 = (bf16[4,3200]{1,0:T(4,128)(2,1)S(1)}, bf16[4,3200]{1,0:T(4,128)(2,1)S(1)}, u32[]{:S(2)}, u32[]{:S(2)}) collective-permute-start(bf16[4,3200]{1,0:T(4,128)(2,1)S(1)} %get-tuple-element.92), channel_id=1, source_target_pairs={{0,3},{1,2},{2,1},{3,0},{4,7},{5,6},{6,5},{7,4},{8,11},{9,10},{10,... | collective-permute-start | bytes 76808 | tf_op jit(solution)/shard_map/ppermute | solution.py:12
  39.1 3.3 %collective-permute-start.12 = (bf16[4,3200]{1,0:T(4,128)(2,1)S(1)}, bf16[4,3200]{1,0:T(4,128)(2,1)S(1)}, u32[]{:S(2)}, u32[]{:S(2)}) collective-permute-start(bf16[4,3200]{1,0:T(4,128)(2,1)S(1)} %get-tuple-element.91), channel_id=1, source_target_pairs={{0,1},{1,0},{2,3},{3,2},{4,5},{5,4},{6,7},{7,6},{8,9},{9,8},{10,11... | collective-permute-start | bytes 76808 | tf_op jit(solution)/shard_map/ppermute | solution.py:12
  44.7 4.1 %collective-permute-start.13 = (bf16[4,3072]{1,0:T(4,128)(2,1)S(1)}, bf16[4,3072]{1,0:T(4,128)(2,1)S(1)}, u32[]{:S(2)}, u32[]{:S(2)}) collective-permute-start(bf16[4,3072]{1,0:T(4,128)(2,1)S(1)} %bitcast.90), channel_id=1, source_target_pairs={{0,2},{1,3},{2,0},{3,1},{4,6},{5,7},{6,4},{7,5},{8,10},{9,11},{10,... | collective-permute-start | bytes 73736 | tf_op jit(solution)/shard_map/ppermute | solution.py:12
  45.4 3.6 %collective-permute-start.14 = (bf16[4,3072]{1,0:T(4,128)(2,1)S(1)}, bf16[4,3072]{1,0:T(4,128)(2,1)S(1)}, u32[]{:S(2)}, u32[]{:S(2)}) collective-permute-start(bf16[4,3072]{1,0:T(4,128)(2,1)S(1)} %bitcast.89), channel_id=1, source_target_pairs={{0,3},{1,2},{2,1},{3,0},{4,7},{5,6},{6,5},{7,4},{8,11},{9,10},{10,... | collective-permute-start | bytes 73736 | tf_op jit(solution)/shard_map/ppermute | solution.py:12
  45.5 3.5 %collective-permute-start.15 = (bf16[4,3072]{1,0:T(4,128)(2,1)S(1)}, bf16[4,3072]{1,0:T(4,128)(2,1)S(1)}, u32[]{:S(2)}, u32[]{:S(2)}) collective-permute-start(bf16[4,3072]{1,0:T(4,128)(2,1)S(1)} %bitcast.88), channel_id=1, source_target_pairs={{0,1},{1,0},{2,3},{3,2},{4,5},{5,4},{6,7},{7,6},{8,9},{9,8},{10,11... | collective-permute-start | bytes 73736 | tf_op jit(solution)/shard_map/ppermute | solution.py:12
  49.0 10.8 %collective-permute-start.16 = (bf16[16,3072]{1,0:T(8,128)(2,1)S(1)}, bf16[16,3072]{1,0:T(8,128)(2,1)S(1)}, u32[]{:S(2)}, u32[]{:S(2)}) collective-permute-start(bf16[16,3072]{1,0:T(8,128)(2,1)S(1)} %constant_dynamic-update-slice_fusion.4.passed_ref), channel_id=1, source_target_pairs={{0,8},{4,12},{8,0},{12,4},{1,9},{5,13},{9,1},{13,5},{2,10},{6,14},... | collective-permute-start | bytes 294920 | tf_op jit(solution)/shard_map/ppermute | solution.py:12
  51.9 8.0 %collective-permute-start.17 = (bf16[16,3072]{1,0:T(8,128)(2,1)S(1)}, bf16[16,3072]{1,0:T(8,128)(2,1)S(1)}, u32[]{:S(2)}, u32[]{:S(2)}) collective-permute-start(bf16[16,3072]{1,0:T(8,128)(2,1)S(1)} %constant_dynamic-update-slice_fusion.4.passed_ref), channel_id=1, source_target_pairs={{0,12},{4,8},{8,4},{12,0},{1,13},{5,9},{9,5},{13,1},{2,14},{6,10},... | collective-permute-start | bytes 294920 | tf_op jit(solution)/shard_map/ppermute | solution.py:12
  52.9 7.6 %collective-permute-start.18 = (bf16[16,3072]{1,0:T(8,128)(2,1)S(1)}, bf16[16,3072]{1,0:T(8,128)(2,1)S(1)}, u32[]{:S(2)}, u32[]{:S(2)}) collective-permute-start(bf16[16,3072]{1,0:T(8,128)(2,1)S(1)} %constant_dynamic-update-slice_fusion.4.passed_ref), channel_id=1, source_target_pairs={{0,4},{4,0},{8,12},{12,8},{1,5},{5,1},{9,13},{13,9},{2,6},{6,2},{1... | collective-permute-start | bytes 294920 | tf_op jit(solution)/shard_map/ppermute | solution.py:12
  64.3 3.6 %collective-permute-start.19 = (bf16[16,3200]{1,0:T(8,128)(2,1)S(1)}, bf16[16,3200]{1,0:T(8,128)(2,1)S(1)}, u32[]{:S(2)}, u32[]{:S(2)}) collective-permute-start(bf16[16,3200]{1,0:T(8,128)(2,1)S(1)} %get-tuple-element.77), channel_id=1, source_target_pairs={{0,1},{1,0},{2,3},{3,2},{4,5},{5,4},{6,7},{7,6},{8,9},{9,8},{10,11... | collective-permute-start | bytes 307208 | tf_op jit(solution)/shard_map/ppermute | solution.py:12
  64.4 5.7 %collective-permute-start.20 = (bf16[16,3200]{1,0:T(8,128)(2,1)S(1)}, bf16[16,3200]{1,0:T(8,128)(2,1)S(1)}, u32[]{:S(2)}, u32[]{:S(2)}) collective-permute-start(bf16[16,3200]{1,0:T(8,128)(2,1)S(1)} %get-tuple-element.79), channel_id=1, source_target_pairs={{0,2},{1,3},{2,0},{3,1},{4,6},{5,7},{6,4},{7,5},{8,10},{9,11},{10,... | collective-permute-start | bytes 307208 | tf_op jit(solution)/shard_map/ppermute | solution.py:12
  65.1 6.3 %collective-permute-start.21 = (bf16[16,3200]{1,0:T(8,128)(2,1)S(1)}, bf16[16,3200]{1,0:T(8,128)(2,1)S(1)}, u32[]{:S(2)}, u32[]{:S(2)}) collective-permute-start(bf16[16,3200]{1,0:T(8,128)(2,1)S(1)} %get-tuple-element.80), channel_id=1, source_target_pairs={{0,3},{1,2},{2,1},{3,0},{4,7},{5,6},{6,5},{7,4},{8,11},{9,10},{10,... | collective-permute-start | bytes 307208 | tf_op jit(solution)/shard_map/ppermute | solution.py:12
  67.9 3.5 %collective-permute-start.22 = (bf16[16,1408]{1,0:T(8,128)(2,1)S(1)}, bf16[16,1408]{1,0:T(8,128)(2,1)S(1)}, u32[]{:S(2)}, u32[]{:S(2)}) collective-permute-start(bf16[16,1408]{1,0:T(8,128)(2,1)S(1)} %get-tuple-element.82), channel_id=1, source_target_pairs={{0,1},{1,0},{2,3},{3,2},{4,5},{5,4},{6,7},{7,6},{8,9},{9,8},{10,11... | collective-permute-start | bytes 135176 | tf_op jit(solution)/shard_map/ppermute | solution.py:12
  68.3 5.0 %collective-permute-start.23 = (bf16[16,1408]{1,0:T(8,128)(2,1)S(1)}, bf16[16,1408]{1,0:T(8,128)(2,1)S(1)}, u32[]{:S(2)}, u32[]{:S(2)}) collective-permute-start(bf16[16,1408]{1,0:T(8,128)(2,1)S(1)} %get-tuple-element.83), channel_id=1, source_target_pairs={{0,2},{1,3},{2,0},{3,1},{4,6},{5,7},{6,4},{7,5},{8,10},{9,11},{10,... | collective-permute-start | bytes 135176 | tf_op jit(solution)/shard_map/ppermute | solution.py:12
  69.0 4.4 %collective-permute-start.24 = (bf16[16,1408]{1,0:T(8,128)(2,1)S(1)}, bf16[16,1408]{1,0:T(8,128)(2,1)S(1)}, u32[]{:S(2)}, u32[]{:S(2)}) collective-permute-start(bf16[16,1408]{1,0:T(8,128)(2,1)S(1)} %get-tuple-element.84), channel_id=1, source_target_pairs={{0,3},{1,2},{2,1},{3,0},{4,7},{5,6},{6,5},{7,4},{8,11},{9,10},{10,... | collective-permute-start | bytes 135176 | tf_op jit(solution)/shard_map/ppermute | solution.py:12
  (9 other events, 77.5 us)
